TPU v7x, 128 devices: a whole 4x4x4 slice. The times are simulated.
128 devices in a mesh: row: 8 (over x, core), col: 16 (over z, y).
Axes of the slice: x: 4, y: 4, z: 4, core: 2. Of those that a mesh axis runs over, the one named last changes fastest.
Arguments:
- density: bfloat16 [4096, 3, 256], P(('row', 'col')), may hold values from -6 to 6
- coords: bfloat16 [4096, 3, 256], P(('row', 'col')), may hold values from 0 to 1
- basis: bfloat16 [4096, 32, 768], P(('row', 'col')), may hold values from -0.21875 to 0.21875
- transfer: float32 [4096, 32, 32], P(('row', 'col')), may hold values from -1 to 1
- parent: int32 [4096], replicated, may hold values from 0 to 1023
- near_pairs: int32 [2, 16384], P(None, ('row', 'col')), may hold values from 0 to 4095, as said below
- near_count: int32 [128], P(('row', 'col')), may hold values from 16 to 128, as said below
- far_pairs: int32 [2, 8192], P(None, ('row', 'col')), may hold values from 0 to 1023
- coupling: float32 [8192, 32, 32], P(('row', 'col')), may hold values from -1 to 1
Outputs:
- velocity: float32 [4096, 3, 256], P(('row', 'col'))
Inputs may be any that keep to these rules, and one draw needn't show every extreme that they name: `near_pairs`: let i = j % 128 for slot j of device (r, c), owners in row-major order with 32 clusters each. The first cluster is owned by device (r, i // (128 // 16)) and the second by device (i // (128 // 8), c); the two may be equal. Slots past a device's live count hold valid but unused pairs. `near_count`: the largest live count equals 128 in every draw.
All inputs are finite; a program needn't handle non-finite values.
Results may differ from a plain program's by a relative error of at most 0.0026.
Values may be sent and summed in bfloat16 or wider, within the bound.
No kernel may reach another device: no remote copies, remote signals or barrier semaphores. Data moves between devices by JAX's collectives and lax.ppermute only.
A program may use at most 64 MiB of HBM per device.

v0:
```python
import math

import jax
import jax.numpy as jnp
from jax import lax
from jax.sharding import PartitionSpec as P

REG_EPS = 0.02
STOKES_SCALE = 1.0 / (8.0 * math.pi)


def stokeslet(near_x, far_x):
    offset = near_x[:, :, :, None] - far_x[:, :, None, :]
    dist_sq = jnp.sum(offset * offset, axis=1)
    inv_dist = lax.rsqrt(dist_sq + REG_EPS * REG_EPS)
    inv_cube = inv_dist * inv_dist * inv_dist
    isotropic = (dist_sq + 2.0 * REG_EPS * REG_EPS) * inv_cube
    dyadic = offset[:, :, None] * offset[:, None, :] * inv_cube[:, None, None]
    identity = jnp.eye(3, dtype=jnp.float32)
    return (dyadic + identity[None, :, :, None, None] * isotropic[:, None, None]) * STOKES_SCALE


def shards(density, coords, basis, transfer, parent, near_pairs, near_count, far_pairs, coupling):
    highest = lax.Precision.HIGHEST
    per_device = density.shape[0]
    panels = density.shape[2]
    rank = basis.shape[1]
    col_devices = lax.axis_size("col")
    row_span = per_device * col_devices
    row_base = lax.axis_index("row") * row_span
    own_base = row_base + lax.axis_index("col") * per_device
    row_density, row_coords = (
        lax.all_gather(density, "col", axis=0, tiled=True),
        lax.all_gather(coords, "col", axis=0, tiled=True),
    )
    col_density, col_coords = (
        lax.all_gather(density, "row", axis=0, tiled=True),
        lax.all_gather(coords, "row", axis=0, tiled=True),
    )
    live_pairs = near_count[0]
    block_total = (live_pairs + 3) // 4

    def fetch(slot_block):
        first_slot = slot_block * 4
        glob_a = lax.dynamic_slice_in_dim(near_pairs[0], first_slot, 4)
        glob_b = lax.dynamic_slice_in_dim(near_pairs[1], first_slot, 4)
        local_a = glob_a - row_base
        local_b = glob_b // row_span * per_device + glob_b % per_device
        within = first_slot + jnp.arange(4, dtype=jnp.int32) < live_pairs
        row_keep = within.astype(jnp.float32)
        col_keep = (within & (glob_a != glob_b)).astype(jnp.float32)
        kernel_tile = stokeslet(
            row_coords[local_a].astype(jnp.float32), col_coords[local_b].astype(jnp.float32)
        )
        return (local_a, local_b, kernel_tile.astype(jnp.bfloat16), row_keep, col_keep)

    def to_rows(kernel_tile, local_b, row_keep):
        values = jnp.einsum(
            "pijxy,pjy->pix", kernel_tile, col_density[local_b], preferred_element_type=jnp.float32
        )
        return values * row_keep[:, None, None]

    def to_cols(kernel_tile, local_a, col_keep):
        values = jnp.einsum(
            "pijxy,pix->pjy", kernel_tile, row_density[local_a], preferred_element_type=jnp.float32
        )
        return values * col_keep[:, None, None]

    row_zero = jnp.zeros((row_span, 3, panels), jnp.float32)
    col_zero = jnp.zeros((col_density.shape[0], 3, panels), jnp.float32)

    def both_ways(slot_block, partials):
        row_part, col_part = partials
        local_a, local_b, kernel_tile, row_keep, col_keep = fetch(slot_block)
        row_part = row_part.at[local_a].add(to_rows(kernel_tile, local_b, row_keep))
        col_part = col_part.at[local_b].add(to_cols(kernel_tile, local_a, col_keep))
        return (row_part, col_part)

    row_part, col_part = lax.fori_loop(0, block_total, both_ways, (row_zero, col_zero))
    near_cols = lax.psum_scatter(col_part, "row", scatter_dimension=0, tiled=True)
    near_rows = lax.psum_scatter(row_part, "col", scatter_dimension=0, tiled=True)
    parent_total = parent.shape[0] // 4
    flattened = density.reshape(per_device, 3 * panels)
    moments = jnp.einsum("crk,ck->cr", basis, flattened, preferred_element_type=jnp.float32)
    lifted = jnp.einsum("crs,cs->cr", transfer, moments, precision=highest)
    own_parent = lax.dynamic_slice_in_dim(parent, own_base, per_device)
    all_lifted = lax.all_gather(lifted, ("row", "col"), axis=0, tiled=True)
    parent_moments = jnp.zeros((parent_total, rank), jnp.float32).at[parent].add(all_lifted)
    to_first = jnp.einsum("krs,ks->kr", coupling, parent_moments[far_pairs[1]], precision=highest)
    to_second = jnp.einsum("ksr,ks->kr", coupling, parent_moments[far_pairs[0]], precision=highest)
    own_locals = (
        jnp.zeros((parent_total, rank), jnp.float32)
        .at[far_pairs[0]]
        .add(to_first)
        .at[far_pairs[1]]
        .add(to_second)
    )
    parent_locals = lax.psum(own_locals, ("row", "col"))
    local_coef = jnp.einsum("csr,cs->cr", transfer, parent_locals[own_parent], precision=highest)
    far_part = jnp.einsum("crk,cr->ck", basis.astype(jnp.float32), local_coef, precision=highest)
    return near_rows + near_cols + far_part.reshape(per_device, 3, panels)


def solution(mesh):
    placed = (
        P(("row", "col"), None, None),
        P(("row", "col"), None, None),
        P(("row", "col"), None, None),
        P(("row", "col"), None, None),
        P(),
        P(None, ("row", "col")),
        P(("row", "col")),
        P(None, ("row", "col")),
        P(("row", "col"), None, None),
    )
    return jax.shard_map(
        shards, mesh=mesh, in_specs=placed, out_specs=P(("row", "col"), None, None), check_vma=False
    )
```

profile of v0, /device:TPU:7, one launch (start us, length us, event | category | flops | bytes accessed | tf_op | source)
XLA Modules:
  0.0 1157.9 jit_solution(1265014361668180818)
XLA Ops:
  8.8 2.0 fusion.21
  10.8 74.9 %all_gather.19 = f32[4096,32]{1,0:T(8,128)} all-gather(f32[32,32]{1,0:T(8,128)S(1)} %bitcast.112), channel_id=1, replica_groups=mesh['row'=8,'col'=16] {'row','col'}, dimensions={0}, use_global_device_ids=true | all-gather | bytes 528384 | tf_op jit(solution)/shard_map/all_gather | solution.py:87
  86.7 22.8 %scatter_custom_fusion.2 = f32[1024,32]{1,0:T(8,128)S(1)} fusion(s32[4096]{0:T(1024)S(1)} %compare_select_fusion.2, f32[4096,32]{1,0:T(8,128)} %all_gather.19, f32[]{:T(128)} %constant.132.clone.1), kind=kCustom, calls=%fused_computation.53 | custom fusion | flops 131072 | bytes 131584 | tf_op jit(solution)/shard_map/scatter-add | solution.py:88
  110.1 1.7 fusion.22
  112.8 1.6 gather_fusion.5
  118.1 18.7 %all_gather.18 = bf16[512,3,256]{2,0,1:T(8,128)(2,1)S(1)} all-gather(bf16[32,3,256]{2,0,1:T(8,128)(2,1)S(1)} %copy-done.6), channel_id=1, replica_groups=mesh['row'=8,'col'=16] {'col'}, dimensions={0}, use_global_device_ids=true | all-gather | bytes 835584 | tf_op jit(solution)/shard_map/all_gather | solution.py:33
  136.8 18.1 %all_gather.15 = bf16[512,3,256]{2,0,1:T(8,128)(2,1)S(1)} all-gather(bf16[32,3,256]{2,0,1:T(8,128)(2,1)S(1)} %copy-done.7), channel_id=1, replica_groups=mesh['row'=8,'col'=16] {'col'}, dimensions={0}, use_global_device_ids=true | all-gather | bytes 835584 | tf_op jit(solution)/shard_map/all_gather | solution.py:34
  154.9 20.6 %all_gather.16 = bf16[256,3,256]{2,0,1:T(8,128)(2,1)} all-gather(bf16[32,3,256]{2,0,1:T(8,128)(2,1)S(1)} %copy-done.7), channel_id=1, replica_groups=mesh['row'=8,'col'=16] {'row'}, dimensions={0}, use_global_device_ids=true | all-gather | bytes 442368 | tf_op jit(solution)/shard_map/all_gather | solution.py:38
  175.5 13.6 %all_gather.17 = bf16[256,3,256]{2,0,1:T(8,128)(2,1)S(1)} all-gather(bf16[32,3,256]{2,0,1:T(8,128)(2,1)} %param.11), channel_id=1, replica_groups=mesh['row'=8,'col'=16] {'row'}, dimensions={0}, use_global_device_ids=true | all-gather | bytes 442368 | tf_op jit(solution)/shard_map/all_gather | solution.py:37
  189.1 1.7 copy.28
  190.8 1.7 copy.31
  194.8 1.6 broadcast_in_dim.8
  197.6 125.5 %while.14 = (s32[]{:T(128)}, f32[512,3,256]{2,1,0:T(4,128)}, f32[256,3,256]{2,1,0:T(4,128)}, s32[]{:T(128)}, s32[2,128]{1,0:T(2,128)S(1)}, /*index=5*/s32[]{:T(1...) while((s32[]{:T(128)}, f32[512,3,256]{2,1,0:T(4,128)}, ...), condition=%wide.region_4.5_spmd, body=%wide.region_0.4_spmd.sunk | while | flops 41177264 | bytes 18106972 | solution.py:79
  197.7 1.6 gather_fusion
  199.3 1.8 gather_fusion.1
  201.1 2.2 broadcast_subtract_fusion.2
  203.3 1.3 multiply_multiply_fusion.2
  204.6 1.8 gather_fusion.3
  206.4 5.0 fusion.52
  212.2 1.9 scatter_fusion.1
  214.1 1.6 gather_fusion.2
  215.7 5.0 fusion.50
  220.8 1.9 scatter_fusion
  222.8 1.6 gather_fusion
  224.5 1.8 gather_fusion.1
  226.3 2.2 broadcast_subtract_fusion.2
  228.5 1.3 multiply_multiply_fusion.2
  229.8 1.8 gather_fusion.3
  231.6 5.0 fusion.52
  237.4 1.9 scatter_fusion.1
  239.3 1.6 gather_fusion.2
  240.9 5.0 fusion.50
  245.9 1.9 scatter_fusion
  248.0 1.6 gather_fusion
  249.6 1.8 gather_fusion.1
  251.4 2.2 broadcast_subtract_fusion.2
  253.6 1.3 multiply_multiply_fusion.2
  254.9 1.8 gather_fusion.3
  256.7 5.0 fusion.52
  262.5 1.9 scatter_fusion.1
  264.4 1.6 gather_fusion.2
  266.0 5.0 fusion.50
  271.1 1.9 scatter_fusion
  273.1 1.6 gather_fusion
  274.7 1.8 gather_fusion.1
  276.5 2.2 broadcast_subtract_fusion.2
  280.0 1.8 gather_fusion.3
  281.8 5.0 fusion.52
  287.6 1.9 scatter_fusion.1
  289.5 1.6 gather_fusion.2
  291.1 5.0 fusion.50
  296.2 1.9 scatter_fusion
  298.1 1.6 gather_fusion
  299.8 1.8 gather_fusion.1
  301.6 2.2 broadcast_subtract_fusion.2
  305.1 1.8 gather_fusion.3
  306.9 5.0 fusion.52
  312.7 1.9 scatter_fusion.1
  314.5 1.6 gather_fusion.2
  316.2 5.0 fusion.50
  321.2 1.9 scatter_fusion
  326.4 1.6 gather_fusion.6
  329.4 726.7 %all-reduce.10.cloned.1.call-done = f32[256,3,256]{2,1,0:T(4,128)} async-done(((f32[256,3,256]{2,1,0:T(4,128)}), f32[256,3,256]{2,1,0:T(4,128)}) %all-reduce.10.cloned.1.call-update) | async-done | bytes 786448
  1056.1 93.5 %all-reduce.8.cloned.1.call-done = f32[512,3,256]{2,1,0:T(4,128)} async-done(((f32[512,3,256]{2,1,0:T(4,128)}), f32[512,3,256]{2,1,0:T(4,128)}) %all-reduce.8.cloned.1.call-update) | async-done | bytes 1572880
  (107 shorter events, 23.6 us)
Async XLA Ops:
  6.5 1.8 copy-start
  6.5 79.2 %copy-start.9 = (s32[4096]{0:T(1024)S(1)}, s32[4096]{0:T(1024)}, u32[]{:S(2)}) copy-start(s32[4096]{0:T(1024)} %param.15) | copy-start | bytes 49156
  6.5 79.2 %copy-start.5 = (f32[64,32,32]{0,2,1:T(8,128)S(1)}, f32[64,32,32]{0,2,1:T(8,128)}, u32[]{:S(2)}) copy-start(f32[64,32,32]{0,2,1:T(8,128)} %param.19) | copy-start | bytes 786436
  6.5 319.9 %all-reduce.6.cloned.1.call-start = ((), (), s32[]{:S(2)}) async-start(), calls=%async_computation | async-start | bytes 1048576 | tf_op jit(solution)/shard_map/psum | solution.py:98
  85.8 32.3 %copy-start.6 = (bf16[32,3,256]{2,0,1:T(8,128)(2,1)S(1)}, bf16[32,3,256]{2,0,1:T(8,128)(2,1)}, u32[]{:S(2)}) copy-start(bf16[32,3,256]{2,0,1:T(8,128)(2,1)} %param.11) | copy-start | bytes 147460
  86.7 50.1 %copy-start.7 = (bf16[32,3,256]{2,0,1:T(8,128)(2,1)S(1)}, bf16[32,3,256]{2,0,1:T(8,128)(2,1)}, u32[]{:S(2)}) copy-start(bf16[32,3,256]{2,0,1:T(8,128)(2,1)} %param.12) | copy-start | bytes 147460
  109.5 2.4 copy-start.2
  116.6 0.8 copy-start.1
  117.4 938.8 %all-reduce.10.cloned.1.call-start = ((), (), s32[]{:S(2)}) async-start(), calls=%async_computation.2 | async-start | bytes 2097152
  189.1 3.4 copy-start.4
  190.8 6.7 copy-start.8
  323.1 0.8 copy-start.11
  323.1 1.4 copy-start.10
  323.1 5.0 copy-start.3
  323.1 826.5 %all-reduce.8.cloned.1.call-start = ((), (), s32[]{:S(2)}) async-start(), calls=%async_computation.1 | async-start | bytes 4194304
Sparse Core Ops, SparseCore 0:
  117.5 142.7 all-reduce.5
  323.3 732.8 all-reduce.9
  1059.8 89.7 all-reduce.7
where the time goes:
time: 1170 us; the launch traced here: 1160 us
  waiting for transfers between devices  821 us (70%)
  blocking collectives  146 us (12%)
  other arithmetic  68.2 us (6%)
  matrix products  56.4 us (5%)
  local copies, waits for them, and re-layouts  50.9 us (4%)
  between operations  15.2 us (1%)
    unnamed x5, waiting for transfers between devices  821 us
    all_gather x1, blocking collectives, shards(): all_lifted = lax.all_gather(lifted, ('row', 'col'), axis=0, tiled=True)  74.9 us
    dot_general x5, matrix products, to_cols(): jnp.einsum('pijxy,pix->pjy', kernel_tile, row_density[local_a], preferred...  25 us
    dot_general x5, matrix products, to_rows(): jnp.einsum('pijxy,pjy->pix', kernel_tile, col_density[local_b], preferred...  25 us
  transfers between devices with their start and end apart: 3, of which 2 were waited for; matrix products, arithmetic and copies ran while one was open for 12% of the time, Pallas kernels for 0%

commit v1 on v0

v1 whole, which is shorter than its diff:
```python
import functools
import math

import jax
import jax.numpy as jnp
from jax import lax
from jax.experimental import pallas as pl
from jax.experimental.pallas import tpu as pltpu
from jax.sharding import PartitionSpec as P

REG_EPS = 0.02
EPS_SQ = REG_EPS * REG_EPS
STOKES_SCALE = 1.0 / (8.0 * math.pi)
BOTH = ("row", "col")
GROUP = 16
PANELS = 256
FIELD_ROWS = 40
POINT_ROWS = 16
f32, bf16 = jnp.float32, jnp.bfloat16


def pieces(value, count):
    out = []
    for _ in range(count):
        head = value.astype(bf16).astype(f32)
        out.append(head)
        value = value - head
    return out


def put(ref, row, value):
    for half in range(2):
        ref[half, row * GROUP : (row + 1) * GROUP, :] = value[:, half * 128 : (half + 1) * 128]


def get(ref, row):
    return jnp.concatenate([ref[half, row * GROUP : (row + 1) * GROUP, :] for half in range(2)], 1)


def split_parts(block):
    parts = [block[:, k * PANELS : (k + 1) * PANELS] for k in range(6)]
    return parts[:3], parts[3:]


def prepare(block, field, left, right):
    q, y = split_parts(block)
    one, zero = jnp.ones_like(q[0]), jnp.zeros_like(q[0])
    norm = pieces(y[0] * y[0] + y[1] * y[1] + y[2] * y[2] + EPS_SQ / 2, 3)
    along = y[0] * q[0] + y[1] * q[1] + y[2] * q[2]
    rows = list(q) + pieces(along, 3)
    for i in range(3):
        for j in range(3):
            rows += pieces(y[i] * q[j], 2)
    for i in range(3):
        rows += pieces(y[i] * along, 3)
    rows += [zero] * (FIELD_ROWS - len(rows))
    for k, value in enumerate(rows):
        put(field, k, value)
    for k, value in enumerate([-2 * v for v in y] + norm + [one] * 3 + [zero] * 7):
        put(left, k, value)
    for k, value in enumerate(y + [one] * 3 + norm + [zero] * 7):
        put(right, k, value)


def finish(block, sums, point_sums):
    _, x = split_parts(block)
    mom = [get(sums, i) for i in range(3)]
    dot = x[0] * mom[0] + x[1] * mom[1] + x[2] * mom[2] - (get(sums, 3) + get(sums, 4) + get(sums, 5))
    out = []
    for i in range(3):
        cross = sum(x[j] * (get(sums, 6 + 2 * (3 * i + j)) + get(sums, 7 + 2 * (3 * i + j))) for j in range(3))
        tail = get(sums, 24 + 3 * i) + get(sums, 25 + 3 * i) + get(sums, 26 + 3 * i)
        total = get(point_sums, i) + EPS_SQ * mom[i] + ((x[i] * dot - cross) + tail)
        out.append(total * STOKES_SCALE)
    return out


def near_kernel(a_ref, b_ref, to_a, to_b, fa, la, ra, fb, lb, rb, sum_a, pt_a, sum_b, pt_b):
    def group(g, carry):
        rows = pl.ds(pl.multiple_of(g * GROUP, GROUP), GROUP)
        block_a, block_b = a_ref[rows, :].astype(f32), b_ref[rows, :].astype(f32)
        prepare(block_a, fa, la, ra)
        prepare(block_b, fb, lb, rb)

        def slot(s, carry):
            def load(ref, count):
                return jnp.concatenate(
                    [ref[half, pl.ds(s, count, stride=GROUP), :] for half in range(2)], 1
                ).astype(bf16)

            def store(ref, count, value):
                for half in range(2):
                    ref[half, pl.ds(s, count, stride=GROUP), :] = value[:, half * 128 : (half + 1) * 128]

            def one_way(field, left, right, sums, point_sums):
                shifted = lax.dot_general(
                    load(left, POINT_ROWS),
                    load(right, POINT_ROWS),
                    (((0,), (0,)), ((), ())),
                    preferred_element_type=f32,
                )
                inv = lax.rsqrt(shifted)
                cube = inv * inv * inv
                source = load(field, FIELD_ROWS)
                store(sums, FIELD_ROWS, jnp.dot(source, cube.astype(bf16), preferred_element_type=f32))
                store(point_sums, 8, jnp.dot(source[:8], inv.astype(bf16), preferred_element_type=f32))

            one_way(fa, la, rb, sum_b, pt_b)
            one_way(fb, lb, ra, sum_a, pt_a)
            return carry

        lax.fori_loop(0, GROUP, slot, 0, unroll=4)
        for out, block, sums, point_sums in ((to_a, block_a, sum_a, pt_a), (to_b, block_b, sum_b, pt_b)):
            for i, value in enumerate(finish(block, sums, point_sums)):
                out[rows, i * PANELS : (i + 1) * PANELS] = value
        return carry

    lax.fori_loop(0, a_ref.shape[0] // GROUP, group, 0)


def near_products(first, second):
    slots = first.shape[0]
    vmem = pl.BlockSpec(memory_space=pltpu.VMEM)

    def rows(count):
        return pltpu.VMEM((2, count * GROUP, 128), f32)

    return pl.pallas_call(
        near_kernel,
        out_shape=[jax.ShapeDtypeStruct((slots, 3 * PANELS), f32)] * 2,
        in_specs=[vmem] * 2,
        out_specs=[vmem] * 2,
        scratch_shapes=[rows(FIELD_ROWS), rows(POINT_ROWS), rows(POINT_ROWS)] * 2
        + [rows(FIELD_ROWS), rows(8)] * 2,
        compiler_params=pltpu.CompilerParams(vmem_limit_bytes=32 << 20),
        cost_estimate=pl.CostEstimate(
            flops=slots * 2 * 2 * 64 * PANELS * PANELS, bytes_accessed=slots * 9216, transcendentals=0
        ),
    )(first, second)


def one_hot(ids, count):
    return (ids[:, None] == jnp.arange(count, dtype=ids.dtype)[None, :]).astype(f32)


def shards(density, coords, basis, transfer, parent, near_pairs, near_count, far_pairs, coupling):
    highest = lax.Precision.HIGHEST
    own, _, panels = density.shape
    rank = basis.shape[1]
    rows, cols = lax.axis_size("row"), lax.axis_size("col")
    devices, half = rows * cols, cols // rows
    my_row, my_col = lax.axis_index("row"), lax.axis_index("col")
    slots = near_pairs.shape[1]
    per_pair = slots // cols

    swap = [
        (r * cols + half * p + h, p * cols + half * r + h)
        for r in range(rows)
        for p in range(rows)
        for h in range(half)
    ]
    flat = density.reshape(own, 3 * panels)
    data = jnp.concatenate([flat, coords.reshape(own, 3 * panels)], axis=1)
    first_data = lax.ppermute(data, BOTH, swap)

    moments = jnp.einsum("crk,ck->cr", basis, flat, preferred_element_type=f32)
    lifted = jnp.einsum("crs,cs->cr", transfer, moments, precision=highest)
    ids = (near_pairs % own).astype(f32)
    live = jnp.arange(slots) < near_count[0]
    message = jnp.concatenate(
        [lifted.reshape(-1, 128), jnp.where(live, ids[0], -1.0)[None], ids[1][None]], axis=0
    )
    lift_rows = message.shape[0] - 2
    everyone = lax.all_to_all(
        jnp.broadcast_to(message[None], (devices,) + message.shape), BOTH, 0, 0, tiled=True
    )

    table = everyone[:, lift_rows:, :].reshape(rows, cols, 2, rows, half * per_pair)
    mine = lax.dynamic_index_in_dim(table, my_col, 1, keepdims=False)
    mine = lax.dynamic_index_in_dim(mine, my_row, 2, keepdims=False)
    own_first, own_second = mine[:, 0].reshape(-1), mine[:, 1].reshape(-1)
    same_place = (jnp.arange(rows)[:, None] == my_row) & (
        half * my_row + jnp.arange(half * per_pair)[None, :] // per_pair == my_col
    )
    back_ids = jnp.where(
        (own_first < 0) | (same_place.reshape(-1) & (own_first == own_second)), -1.0, own_second
    )
    picked = jnp.dot(
        one_hot(own_second, own).astype(bf16), data, preferred_element_type=f32
    ).astype(bf16)
    second = lax.all_to_all(picked, "col", 0, 0, tiled=True)

    held = lax.dynamic_index_in_dim(table, my_col // half, 0, keepdims=False)
    held = lax.dynamic_index_in_dim(held, my_row, 2, keepdims=False)[:, 0]
    held = lax.dynamic_slice_in_dim(held, my_col % half * per_pair, per_pair, 1).reshape(-1)
    first_hot = one_hot(held, own)
    first = jnp.dot(first_hot.astype(bf16), first_data, preferred_element_type=f32).astype(bf16)
    to_first, to_second = near_products(first, second)
    near_first = lax.ppermute(
        jnp.einsum("sc,sk->ck", first_hot, to_first, precision=highest), BOTH, swap
    )
    returned = lax.all_to_all(to_second, "col", 0, 0, tiled=True)
    near_second = jnp.einsum("sc,sk->ck", one_hot(back_ids, own), returned, precision=highest)

    per_lane = 128 // rank
    all_lifted = everyone[:, :lift_rows, :].reshape(-1, 128)
    parents = parent.reshape(-1, per_lane)
    ends = far_pairs.reshape(-1)
    hits = (parents.T[:, None, :] == ends[None, :, None]).astype(f32)
    found = jnp.einsum("mkn,nl->mkl", hits, all_lifted, precision=highest)
    at_ends = sum(found[m, :, m * rank : (m + 1) * rank] for m in range(per_lane))
    count = far_pairs.shape[1]
    sent_first = jnp.einsum("krs,ks->kr", coupling, at_ends[count:], precision=highest)
    sent_second = jnp.einsum("ksr,ks->kr", coupling, at_ends[:count], precision=highest)
    sent = jnp.concatenate([sent_first, sent_second], axis=0)
    partial = jnp.concatenate(
        [jnp.einsum("kn,kr->nr", hits[m], sent, precision=highest) for m in range(per_lane)], axis=1
    )
    gathered = lax.all_to_all(partial.reshape(devices, lift_rows, 128), BOTH, 0, 0, tiled=True)
    parent_locals = jnp.sum(gathered, axis=0).reshape(own, rank)
    local_coef = jnp.einsum("csr,cs->cr", transfer, parent_locals, precision=highest)
    far_part = jnp.einsum("crk,cr->ck", basis.astype(f32), local_coef, precision=highest)
    return (near_first + near_second + far_part).reshape(own, 3, panels)


def solution(mesh):
    placed = (
        P(BOTH, None, None),
        P(BOTH, None, None),
        P(BOTH, None, None),
        P(BOTH, None, None),
        P(),
        P(None, BOTH),
        P(BOTH),
        P(None, BOTH),
        P(BOTH, None, None),
    )
    return jax.shard_map(
        shards, mesh=mesh, in_specs=placed, out_specs=P(BOTH, None, None), check_vma=False
    )
```

time: 1170 us -> 122 us (0.10)
  waiting for transfers between devices: 821 us -> 22.4 us
  blocking collectives: 146 us -> 0 us
  other arithmetic: 68.2 us -> 2.79 us
  matrix products: 56.4 us -> 11 us
  local copies, waits for them, and re-layouts: 50.9 us -> 6.63 us
  starting transfers between devices: 0.08 us -> 42.5 us
  Pallas kernels: 0 us -> 33.8 us
  between operations: 15.2 us -> 1.02 us
    unnamed x5 -> x0, waiting for transfers between devices: 821 us -> none
    all_gather x5 -> x0, blocking collectives: 146 us -> none  [the longest x1 74.9 us: shards(): all_lifted = lax.all_gather(lifted, ('row', 'col'), axis=0, tiled=True)]
    dot_general x15 -> x12, matrix products: 54.4 us -> 10.1 us  [the longest x4 3.08 us: shards(): jnp.einsum('kn,kr->nr', hits[m], sent, precision=highest)]
    scatter-add x13 -> x0, other arithmetic: 43.9 us -> none  [the longest x1 22.8 us: shards(): jnp.zeros((parent_total, rank), jnp.float32).at[parent].add(all_lifted)]
    gather x23 -> x0, local copies, waits for them, and re-layouts: 38 us -> none  [the longest x5 9 us: fetch(): row_coords[local_a].astype(jnp.float32)]
    pallas_call x0 -> x1, Pallas kernels: none -> 33.8 us  [near_products(): pl.pallas_call(near_kernel, out_shape=[jax.ShapeDtypeStruct((slots, 3 * P...]
    all_to_all x0 -> x4, starting transfers between devices: none -> 26.8 us  [the longest x1 11.2 us: shards(): lax.all_to_all(jnp.broadcast_to(message[None], (devices,) + message.shape...]
    all_to_all x0 -> x4, waiting for transfers between devices: none -> 21 us  [the longest x1 9.1 us: shards(): lax.all_to_all(jnp.broadcast_to(message[None], (devices,) + message.shape...]
  transfers between devices with their start and end apart: 3 -> 6, of which waited for: 2 -> 4; matrix products, arithmetic and copies ran while one was open for 12% -> 13% of each run, Pallas kernels for 0% -> 28%
where the time goes in v1:
time: 122 us; the launch traced here: 120 us
  starting transfers between devices  42.5 us (35%)
  Pallas kernels  33.8 us (28%)
  waiting for transfers between devices  22.4 us (18%)
  matrix products  11 us (9%)
  local copies, waits for them, and re-layouts  6.63 us (5%)
  other arithmetic  2.79 us (2%)
    pallas_call x1, Pallas kernels, near_products(): pl.pallas_call(near_kernel, out_shape=[jax.ShapeDtypeStruct((slots, 3 * P...  33.8 us
    all_to_all x1, starting transfers between devices, shards(): lax.all_to_all(jnp.broadcast_to(message[None], (devices,) + message.shape...  11.2 us
    all_to_all x1, waiting for transfers between devices, shards(): lax.all_to_all(jnp.broadcast_to(message[None], (devices,) + message.shape...  9.1 us
    all_to_all x1, starting transfers between devices, shards(): lax.all_to_all(partial.reshape(devices, lift_rows, 128), BOTH, 0, 0, tile...  8.49 us
    ppermute x1, starting transfers between devices, shards(): first_data = lax.ppermute(data, BOTH, swap)  7.88 us
    ppermute x1, starting transfers between devices, shards(): lax.ppermute(jnp.einsum('sc,sk->ck', first_hot, to_first, precision=highe...  7.74 us
    all_to_all x1, waiting for transfers between devices, shards(): returned = lax.all_to_all(to_second, 'col', 0, 0, tiled=True)  6.58 us
    all_to_all x1, waiting for transfers between devices, shards(): second = lax.all_to_all(picked, 'col', 0, 0, tiled=True)  5.28 us
  transfers between devices with their start and end apart: 6, of which 4 were waited for; matrix products, arithmetic and copies ran while one was open for 13% of the time, Pallas kernels for 28%

profile of v1, /device:TPU:7, one launch (start us, length us, event | category | flops | bytes accessed | tf_op | source)
XLA Modules:
  0.0 120.2 jit_solution(2258920613173638358)
XLA Ops:
  0.0 0.0 copy-start
  0.0 0.8 fusion.13
  1.5 0.8 copy.23
  2.3 0.1 reshape.155
  2.4 0.0 copy-done
  2.4 0.5 convolution_bitcast_fusion
  2.9 0.0 copy-done.2
  2.9 0.9 fusion.18
  3.9 0.1 reshape.133
  4.0 0.0 copy-start.3
  4.0 0.0 copy-start.4
  4.0 0.0 copy-start.5
  4.0 1.1 broadcast_in_dim.11
  5.1 11.2 %all-to-all-start = ((f32[128,10,128]{2,1,0:T(8,128)}), f32[128,10,128]{2,1,0:T(8,128)}, u32[]{:S(2)}, u32[]{:S(2)}) async-start(f32[128,10,128]{2,1,0:T(8,128)} %broadcast_in_dim.11), calls=%async_computation | async-start | bytes 2097152 | tf_op jit(solution)/shard_map/all_to_all | solution.py:174
  16.3 0.0 copy-done.3
  16.4 0.0 copy-start.1
  16.4 0.0 copy-done.4
  16.4 7.9 %collective-permute-start = (bf16[32,1536]{1,0:T(8,128)(2,1)S(1)}, bf16[32,1536]{1,0:T(8,128)(2,1)}, u32[]{:S(2)}, u32[]{:S(2)}) collective-permute-start(bf16[32,1536]{1,0:T(8,128)(2,1)S(1)} %constant_dynamic-update-slice_fusion), channel_id=1, source_target_pairs={{0,0},{1,1},{2,16},{3,17},{4,32},{5,33},{6,48},{7,49},{8,64},{9,65... | collective-permute-start | bytes 294920 | tf_op jit(solution)/shard_map/ppermute | solution.py:164
  24.4 0.1 broadcast_and_fusion
  24.4 0.1 and.67
  24.5 0.0 copy-done.5
  24.5 0.5 reshape.136
  25.1 0.2 copy.27
  25.3 0.0 copy-done.6
  25.3 0.1 eq.108
  25.3 0.4 broadcast_compare_fusion
  25.7 9.1 %all-to-all-done = f32[128,10,128]{2,1,0:T(8,128)} async-done(((f32[128,10,128]{2,1,0:T(8,128)}), f32[128,10,128]{2,1,0:T(8,128)}, u32[]{:S(2)}, u32[]{:S(2)}) %all-to-all-start) | async-done | bytes 655392 | tf_op jit(solution)/shard_map/all_to_all | solution.py:174
  34.8 2.3 %fusion.2 = f32[4,128,128]{1,2,0:T(8,128)S(1)} fusion(f32[128,10,128]{2,1,0:T(8,128)} %all-to-all-done, s32[4,1024]{1,0:T(4,128)S(1)} %copy.27, s32[128]{0:T(128)S(1)} %eq.108), kind=kOutput, calls=%fused_computation.9 | convolution fusion | flops 805830656 | bytes 803328 | tf_op jit(solution)/shard_map/mkn,nl->mkl/dot_general | solution.py:210
  37.2 0.1 slice_bitcast_fusion.11
  37.2 0.0 copy-done.1
  37.2 0.1 multiply_reduce_fusion
  37.3 0.1 multiply_reduce_fusion.1
  37.4 0.1 pad_maximum_fusion.1
  37.5 0.3 fusion.3
  37.8 0.9 fusion.4
  38.7 0.9 fusion.5
  39.6 0.9 fusion.6
  40.6 1.1 slice.76
  41.7 0.4 reshape.134
  42.1 0.1 eq.95
  42.2 1.1 fusion
  43.3 3.6 %all-to-all-start.1 = ((bf16[16,8,1536]{2,1,0:T(8,128)(2,1)}), bf16[16,8,1536]{2,1,0:T(8,128)(2,1)S(1)}, u32[]{:S(2)}, u32[]{:S(2)}) async-start(bf16[16,8,1536]{2,1,0:T(8,128)(2,1)} %fusion), calls=%async_computation.1 | async-start | bytes 786432 | tf_op jit(solution)/shard_map/all_to_all | solution.py:191
  46.8 0.1 constant_dynamic-slice_fusion.1
  46.9 0.1 eq.91
  47.0 0.1 reshape_squeeze.4
  47.1 1.1 pad_maximum_fusion
  48.2 1.0 copy.29
  49.2 0.0 collective-permute-done
  49.2 1.2 convolution_convert_fusion.1.a_ref
  50.4 5.3 %all-to-all-done.1 = bf16[16,8,1536]{2,1,0:T(8,128)(2,1)S(1)} async-done(((bf16[16,8,1536]{2,1,0:T(8,128)(2,1)}), bf16[16,8,1536]{2,1,0:T(8,128)(2,1)S(1)}, u32[]{:S(2)}, u32[]{:S(2)}) %all-to-all-start.1) | async-done | bytes 393248 | tf_op jit(solution)/shard_map/all_to_all | solution.py:191
  55.7 8.5 %all-to-all-start.3 = ((f32[128,8,128]{2,1,0:T(8,128)}), f32[128,8,128]{2,1,0:T(8,128)S(1)}, u32[]{:S(2)}, u32[]{:S(2)}) async-start(f32[128,8,128]{2,1,0:T(8,128)} %bitcast.23), calls=%async_computation.3 | async-start | bytes 1048576 | tf_op jit(solution)/shard_map/all_to_all | solution.py:219
  64.2 33.8 %shard_map.91 = (f32[128,768]{1,0:T(8,128)S(1)}, f32[128,768]{1,0:T(8,128)}) custom-call(bf16[128,1536]{1,0:T(8,128)(2,1)S(1)} %convolution_convert_fusion.1.a_ref, bf16[128,1536]{1,0:T(8,128)(2,1)S(1)} %bitcast.86), custom_call_target="tpu_custom_call" | custom-call | flops 2147483648 | bytes 1179648 | tf_op jit(solution)/shard_map/pallas_call | solution.py:128
  98.0 0.3 fusion.8
  98.3 7.7 %collective-permute-start.1 = (f32[32,768]{1,0:T(8,128)S(1)}, f32[32,768]{1,0:T(8,128)S(1)}, u32[]{:S(2)}, u32[]{:S(2)}) collective-permute-start(f32[32,768]{1,0:T(8,128)S(1)} %fusion.8), channel_id=1, source_target_pairs={{0,0},{1,1},{2,16},{3,17},{4,32},{5,33},{6,48},{7,49},{8,64},{9,65... | collective-permute-start | bytes 294920 | tf_op jit(solution)/shard_map/ppermute | solution.py:199
  106.1 0.0 all-to-all-done.3
  106.1 3.6 %all-to-all-start.2 = ((f32[16,8,768]{2,1,0:T(8,128)}), f32[16,8,768]{2,1,0:T(8,128)S(1)}, u32[]{:S(2)}, u32[]{:S(2)}) async-start(f32[16,8,768]{2,1,0:T(8,128)} %bitcast.12), calls=%async_computation.2 | async-start | bytes 786432 | tf_op jit(solution)/shard_map/all_to_all | solution.py:202
  109.7 0.1 reduce_sum.9
  109.8 0.1 reshape.150
  109.9 0.5 convolution_bitcast_fusion.1
  110.4 0.7 fusion.19
  111.1 1.5 %collective-permute-done.1 = f32[32,768]{1,0:T(8,128)S(1)} collective-permute-done((f32[32,768]{1,0:T(8,128)S(1)}, f32[32,768]{1,0:T(8,128)S(1)}, u32[]{:S(2)}, u32[]{:S(2)}) %collective-permute-start.1) | collective-permute-done | bytes 98336 | tf_op jit(solution)/shard_map/ppermute | solution.py:199
  112.6 6.6 %all-to-all-done.2 = f32[16,8,768]{2,1,0:T(8,128)S(1)} async-done(((f32[16,8,768]{2,1,0:T(8,128)}), f32[16,8,768]{2,1,0:T(8,128)S(1)}, u32[]{:S(2)}, u32[]{:S(2)}) %all-to-all-start.2) | async-done | bytes 393248 | tf_op jit(solution)/shard_map/all_to_all | solution.py:202
  119.2 0.3 fusion.1
  119.5 0.7 copy.59
  (18 shorter events, 0.1 us)
Async XLA Ops:
  0.0 2.4 %copy-start = (bf16[32,32,768]{2,1,0:T(8,128)(2,1)S(1)}, bf16[32,32,768]{2,1,0:T(8,128)(2,1)}, u32[]{:S(2)}) copy-start(bf16[32,32,768]{2,1,0:T(8,128)(2,1)} %param.11) | copy-start | bytes 4718596
  0.0 2.9 %copy-start.2 = (f32[32,32,32]{2,1,0:T(8,128)S(1)}, f32[32,32,32]{2,1,0:T(8,128)}, u32[]{:S(2)}) copy-start(f32[32,32,32]{2,1,0:T(8,128)} %param.12) | copy-start | bytes 393220
  4.0 12.4 %copy-start.3 = (bf16[32,3,256]{2,0,1:T(8,128)(2,1)S(1)}, bf16[32,3,256]{2,0,1:T(8,128)(2,1)}, u32[]{:S(2)}) copy-start(bf16[32,3,256]{2,0,1:T(8,128)(2,1)} %param.9) | copy-start | bytes 147460
  4.0 12.4 %copy-start.4 = (bf16[32,3,256]{2,0,1:T(8,128)(2,1)S(1)}, bf16[32,3,256]{2,0,1:T(8,128)(2,1)}, u32[]{:S(2)}) copy-start(bf16[32,3,256]{2,0,1:T(8,128)(2,1)} %param.10) | copy-start | bytes 147460
  4.0 20.5 %copy-start.5 = (s32[4096]{0:T(1024)S(1)}, s32[4096]{0:T(1024)}, u32[]{:S(2)}) copy-start(s32[4096]{0:T(1024)} %param.13) | copy-start | bytes 49156
  5.1 20.2 %copy-start.6 = (s32[2,64]{1,0:T(2,128)S(1)}, s32[2,64]{1,0:T(2,128)}, u32[]{:S(2)}) copy-start(s32[2,64]{1,0:T(2,128)} %param.16) | copy-start | bytes 1540
  5.1 29.8 %all-to-all-start = ((f32[128,10,128]{2,1,0:T(8,128)}), f32[128,10,128]{2,1,0:T(8,128)}, u32[]{:S(2)}, u32[]{:S(2)}) async-start(f32[128,10,128]{2,1,0:T(8,128)} %broadcast_in_dim.11), calls=%async_computation | async-start | bytes 2097152 | tf_op jit(solution)/shard_map/all_to_all | solution.py:174
  16.4 20.9 %copy-start.1 = (f32[64,32,32]{0,2,1:T(8,128)S(1)}, f32[64,32,32]{0,2,1:T(8,128)}, u32[]{:S(2)}) copy-start(f32[64,32,32]{0,2,1:T(8,128)} %param.17) | copy-start | bytes 786436
  16.4 32.8 %collective-permute-start = (bf16[32,1536]{1,0:T(8,128)(2,1)S(1)}, bf16[32,1536]{1,0:T(8,128)(2,1)}, u32[]{:S(2)}, u32[]{:S(2)}) collective-permute-start(bf16[32,1536]{1,0:T(8,128)(2,1)S(1)} %constant_dynamic-update-slice_fusion), channel_id=1, source_target_pairs={{0,0},{1,1},{2,16},{3,17},{4,32},{5,33},{6,48},{7,49},{8,64},{9,65... | collective-permute-start | bytes 294920 | tf_op jit(solution)/shard_map/ppermute | solution.py:164
  43.3 12.4 %all-to-all-start.1 = ((bf16[16,8,1536]{2,1,0:T(8,128)(2,1)}), bf16[16,8,1536]{2,1,0:T(8,128)(2,1)S(1)}, u32[]{:S(2)}, u32[]{:S(2)}) async-start(bf16[16,8,1536]{2,1,0:T(8,128)(2,1)} %fusion), calls=%async_computation.1 | async-start | bytes 786432 | tf_op jit(solution)/shard_map/all_to_all | solution.py:191
  55.7 50.4 %all-to-all-start.3 = ((f32[128,8,128]{2,1,0:T(8,128)}), f32[128,8,128]{2,1,0:T(8,128)S(1)}, u32[]{:S(2)}, u32[]{:S(2)}) async-start(f32[128,8,128]{2,1,0:T(8,128)} %bitcast.23), calls=%async_computation.3 | async-start | bytes 1048576 | tf_op jit(solution)/shard_map/all_to_all | solution.py:219
  98.3 14.3 %collective-permute-start.1 = (f32[32,768]{1,0:T(8,128)S(1)}, f32[32,768]{1,0:T(8,128)S(1)}, u32[]{:S(2)}, u32[]{:S(2)}) collective-permute-start(f32[32,768]{1,0:T(8,128)S(1)} %fusion.8), channel_id=1, source_target_pairs={{0,0},{1,1},{2,16},{3,17},{4,32},{5,33},{6,48},{7,49},{8,64},{9,65... | collective-permute-start | bytes 294920 | tf_op jit(solution)/shard_map/ppermute | solution.py:199
  106.1 13.1 %all-to-all-start.2 = ((f32[16,8,768]{2,1,0:T(8,128)}), f32[16,8,768]{2,1,0:T(8,128)S(1)}, u32[]{:S(2)}, u32[]{:S(2)}) async-start(f32[16,8,768]{2,1,0:T(8,128)} %bitcast.12), calls=%async_computation.2 | async-start | bytes 786432 | tf_op jit(solution)/shard_map/all_to_all | solution.py:202

commit v2 on v1

--- a/solution.py
+++ b/solution.py
@@ -75,10 +75,16 @@
     return out
 
 
-def near_kernel(a_ref, b_ref, to_a, to_b, fa, la, ra, fb, lb, rb, sum_a, pt_a, sum_b, pt_b):
+def near_kernel(ids_lane, first_ref, second_ref, near_first, to_second, fa, la, ra, fb, lb, rb, sum_a, pt_a, sum_b, pt_b):
+    own = first_ref.shape[0]
+    near_first[...] = jnp.zeros_like(near_first)
+
     def group(g, carry):
         rows = pl.ds(pl.multiple_of(g * GROUP, GROUP), GROUP)
-        block_a, block_b = a_ref[rows, :].astype(f32), b_ref[rows, :].astype(f32)
+        ids = second_ref[rows, ids_lane : ids_lane + 128].astype(f32)[:, :own]
+        chosen = (ids == lax.broadcasted_iota(jnp.int32, (GROUP, own), 1).astype(f32)).astype(bf16)
+        block_a = jnp.dot(chosen, first_ref[...], preferred_element_type=f32)
+        block_b = second_ref[rows, : 6 * PANELS].astype(f32)
         prepare(block_a, fa, la, ra)
         prepare(block_b, fb, lb, rb)
 
@@ -109,25 +115,32 @@
             one_way(fb, lb, ra, sum_a, pt_a)
             return carry
 
-        lax.fori_loop(0, GROUP, slot, 0, unroll=4)
-        for out, block, sums, point_sums in ((to_a, block_a, sum_a, pt_a), (to_b, block_b, sum_b, pt_b)):
-            for i, value in enumerate(finish(block, sums, point_sums)):
-                out[rows, i * PANELS : (i + 1) * PANELS] = value
+        lax.fori_loop(0, GROUP, slot, 0, unroll=GROUP)
+        for i, value in enumerate(finish(block_b, sum_b, pt_b)):
+            to_second[rows, i * PANELS : (i + 1) * PANELS] = value
+        for i, value in enumerate(finish(block_a, sum_a, pt_a)):
+            for piece in pieces(value, 3):
+                near_first[:, i * PANELS : (i + 1) * PANELS] += lax.dot_general(
+                    chosen, piece.astype(bf16), (((0,), (0,)), ((), ())), preferred_element_type=f32
+                )
         return carry
 
-    lax.fori_loop(0, a_ref.shape[0] // GROUP, group, 0)
-
-
-def near_products(first, second):
-    slots = first.shape[0]
+    lax.fori_loop(0, second_ref.shape[0] // GROUP, group, 0)
+
+
+def near_products(first, second, ids_lane):
+    slots = second.shape[0]
     vmem = pl.BlockSpec(memory_space=pltpu.VMEM)
 
     def rows(count):
         return pltpu.VMEM((2, count * GROUP, 128), f32)
 
     return pl.pallas_call(
-        near_kernel,
-        out_shape=[jax.ShapeDtypeStruct((slots, 3 * PANELS), f32)] * 2,
+        functools.partial(near_kernel, ids_lane),
+        out_shape=[
+            jax.ShapeDtypeStruct((first.shape[0], 3 * PANELS), f32),
+            jax.ShapeDtypeStruct((slots, 3 * PANELS), f32),
+        ],
         in_specs=[vmem] * 2,
         out_specs=[vmem] * 2,
         scratch_shapes=[rows(FIELD_ROWS), rows(POINT_ROWS), rows(POINT_ROWS)] * 2
@@ -139,6 +152,38 @@
     )(first, second)
 
 
+def ends_kernel(start, count, recv, parents, ends, out):
+    parts = parents.shape[1]
+    sums = [jnp.zeros((ends.shape[0], 256), f32) for _ in range(parts)]
+    for r in range(count):
+        lifted = recv[:, start + 256 * r : start + 256 * (r + 1)]
+        for m in range(parts):
+            hit = (parents[r, m : m + 1, :] == ends[...]).astype(f32).astype(bf16)
+            sums[m] += jnp.dot(hit, lifted, preferred_element_type=f32)
+    lane = lax.broadcasted_iota(jnp.int32, (ends.shape[0], 128), 1)
+    width = 128 // parts
+    total = jnp.zeros((ends.shape[0], 128), f32)
+    for m in range(parts):
+        total += jnp.where(lane // width == m, sums[m][:, :128] + sums[m][:, 128:], 0.0)
+    out[...] = total
+
+
+def spread_kernel(parents, ends, sent, out):
+    parts = parents.shape[1]
+    width = 128 // parts
+    lane = lax.broadcasted_iota(jnp.int32, sent.shape, 1)
+    head, rest = pieces(sent[...], 2)
+    for r in range(out.shape[0] // 128):
+        rows = slice(r * 128, (r + 1) * 128)
+        total = jnp.zeros((128, 256), f32)
+        for m in range(parts):
+            hit = (parents[rows, m : m + 1] == ends[...]).astype(f32).astype(bf16)
+            here = lane // width == m
+            both = jnp.concatenate([jnp.where(here, head, 0.0), jnp.where(here, rest, 0.0)], 1)
+            total += jnp.dot(hit, both.astype(bf16), preferred_element_type=f32)
+        out[rows, :] = total[:, :128] + total[:, 128:]
+
+
 def one_hot(ids, count):
     return (ids[:, None] == jnp.arange(count, dtype=ids.dtype)[None, :]).astype(f32)
 
@@ -148,10 +193,12 @@
     own, _, panels = density.shape
     rank = basis.shape[1]
     rows, cols = lax.axis_size("row"), lax.axis_size("col")
-    devices, half = rows * cols, cols // rows
+    half = cols // rows
     my_row, my_col = lax.axis_index("row"), lax.axis_index("col")
     slots = near_pairs.shape[1]
     per_pair = slots // cols
+    block = slots // rows
+    vmem = pl.BlockSpec(memory_space=pltpu.VMEM)
 
     swap = [
         (r * cols + half * p + h, p * cols + half * r + h)
@@ -164,60 +211,70 @@
     first_data = lax.ppermute(data, BOTH, swap)
 
     moments = jnp.einsum("crk,ck->cr", basis, flat, preferred_element_type=f32)
-    lifted = jnp.einsum("crs,cs->cr", transfer, moments, precision=highest)
-    ids = (near_pairs % own).astype(f32)
+    lifted = jnp.einsum("crs,cs->cr", transfer, moments, precision=highest).reshape(-1, 128)
+    lift_rows = lifted.shape[0]
     live = jnp.arange(slots) < near_count[0]
+    ids = jnp.where(live[None], near_pairs % own, -1).astype(f32)
+    ids = ids.reshape(2, rows, block).transpose(1, 0, 2).reshape(rows, 1, 2 * block)
     message = jnp.concatenate(
-        [lifted.reshape(-1, 128), jnp.where(live, ids[0], -1.0)[None], ids[1][None]], axis=0
-    )
-    lift_rows = message.shape[0] - 2
-    everyone = lax.all_to_all(
-        jnp.broadcast_to(message[None], (devices,) + message.shape), BOTH, 0, 0, tiled=True
-    )
-
-    table = everyone[:, lift_rows:, :].reshape(rows, cols, 2, rows, half * per_pair)
-    mine = lax.dynamic_index_in_dim(table, my_col, 1, keepdims=False)
-    mine = lax.dynamic_index_in_dim(mine, my_row, 2, keepdims=False)
-    own_first, own_second = mine[:, 0].reshape(-1), mine[:, 1].reshape(-1)
-    same_place = (jnp.arange(rows)[:, None] == my_row) & (
-        half * my_row + jnp.arange(half * per_pair)[None, :] // per_pair == my_col
-    )
-    back_ids = jnp.where(
-        (own_first < 0) | (same_place.reshape(-1) & (own_first == own_second)), -1.0, own_second
-    )
-    picked = jnp.dot(
-        one_hot(own_second, own).astype(bf16), data, preferred_element_type=f32
-    ).astype(bf16)
-    second = lax.all_to_all(picked, "col", 0, 0, tiled=True)
-
-    held = lax.dynamic_index_in_dim(table, my_col // half, 0, keepdims=False)
-    held = lax.dynamic_index_in_dim(held, my_row, 2, keepdims=False)[:, 0]
-    held = lax.dynamic_slice_in_dim(held, my_col % half * per_pair, per_pair, 1).reshape(-1)
-    first_hot = one_hot(held, own)
-    first = jnp.dot(first_hot.astype(bf16), first_data, preferred_element_type=f32).astype(bf16)
-    to_first, to_second = near_products(first, second)
-    near_first = lax.ppermute(
-        jnp.einsum("sc,sk->ck", first_hot, to_first, precision=highest), BOTH, swap
-    )
-    returned = lax.all_to_all(to_second, "col", 0, 0, tiled=True)
-    near_second = jnp.einsum("sc,sk->ck", one_hot(back_ids, own), returned, precision=highest)
-
-    per_lane = 128 // rank
-    all_lifted = everyone[:, :lift_rows, :].reshape(-1, 128)
-    parents = parent.reshape(-1, per_lane)
+        [
+            jnp.broadcast_to(lifted[None], (rows, lift_rows, 128)),
+            jnp.pad(ids, ((0, 0), (0, 0), (0, 128 - 2 * block))),
+        ],
+        axis=1,
+    )
+    from_row = lax.all_to_all(message, "row", 0, 0, tiled=True)
+
+    own_first = from_row[:, lift_rows, :block].reshape(-1)
+    own_second = from_row[:, lift_rows, block : 2 * block].reshape(-1)
+    place = jnp.arange(slots)
+    same_owner = (place // block == my_row) & (half * my_row + place % block // per_pair == my_col)
+    back_ids = jnp.where(same_owner & (own_first == own_second), -1.0, own_second)
+    picked = jnp.dot(one_hot(own_second, own).astype(bf16), data, preferred_element_type=f32)
+    head, rest = pieces(from_row[:, :lift_rows, :], 2)
+    row_lifted = jnp.stack([head, rest], 2).transpose(1, 0, 2, 3).reshape(lift_rows, -1)
+    message = jnp.concatenate(
+        [
+            picked.astype(bf16),
+            jnp.broadcast_to(own_first[:, None], (slots, 128)).astype(bf16),
+            jnp.tile(row_lifted.astype(bf16), (cols, 1)),
+        ],
+        axis=1,
+    )
+    second = lax.all_to_all(message, "col", 0, 0, tiled=True)
+    ids_lane = 6 * panels
+
+    parts = 128 // rank
+    by_row = parent.reshape(rows, slots, parts)
     ends = far_pairs.reshape(-1)
-    hits = (parents.T[:, None, :] == ends[None, :, None]).astype(f32)
-    found = jnp.einsum("mkn,nl->mkl", hits, all_lifted, precision=highest)
-    at_ends = sum(found[m, :, m * rank : (m + 1) * rank] for m in range(per_lane))
+    at_ends = pl.pallas_call(
+        functools.partial(ends_kernel, ids_lane + 128, rows),
+        out_shape=jax.ShapeDtypeStruct((ends.shape[0], 128), f32),
+        in_specs=[vmem] * 3,
+        out_specs=vmem,
+    )(second, by_row.transpose(0, 2, 1), ends[:, None])
+    at_ends = at_ends.reshape(-1, parts, rank).sum(axis=1)
     count = far_pairs.shape[1]
     sent_first = jnp.einsum("krs,ks->kr", coupling, at_ends[count:], precision=highest)
     sent_second = jnp.einsum("ksr,ks->kr", coupling, at_ends[:count], precision=highest)
-    sent = jnp.concatenate([sent_first, sent_second], axis=0)
-    partial = jnp.concatenate(
-        [jnp.einsum("kn,kr->nr", hits[m], sent, precision=highest) for m in range(per_lane)], axis=1
-    )
-    gathered = lax.all_to_all(partial.reshape(devices, lift_rows, 128), BOTH, 0, 0, tiled=True)
-    parent_locals = jnp.sum(gathered, axis=0).reshape(own, rank)
+    sent = jnp.tile(jnp.concatenate([sent_first, sent_second], axis=0), (1, parts))
+    partial = pl.pallas_call(
+        spread_kernel,
+        out_shape=jax.ShapeDtypeStruct((rows * slots, 128), f32),
+        in_specs=[vmem] * 3,
+        out_specs=vmem,
+    )(parent.reshape(-1, parts), ends[None], sent)
+    row_locals = lax.all_to_all(partial.reshape(rows, slots, 128), "row", 0, 0, tiled=True)
+
+    near_first, to_second = near_products(first_data, second, ids_lane)
+    near_first = lax.ppermute(near_first, BOTH, swap)
+    returned = lax.all_to_all(
+        jnp.concatenate([to_second, row_locals.sum(axis=0)], axis=1), "col", 0, 0, tiled=True
+    )
+    near_second = jnp.einsum(
+        "sc,sk->ck", one_hot(back_ids, own), returned[:, : 3 * panels], precision=highest
+    )
+    parent_locals = returned[:, 3 * panels :].reshape(cols, lift_rows, 128).sum(axis=0).reshape(own, rank)
     local_coef = jnp.einsum("csr,cs->cr", transfer, parent_locals, precision=highest)
     far_part = jnp.einsum("crk,cr->ck", basis.astype(f32), local_coef, precision=highest)
     return (near_first + near_second + far_part).reshape(own, 3, panels)

time: 122 us -> 115 us (0.943)
  matrix products: 11 us -> 3.34 us
  starting transfers between devices: 42.5 us -> 37.7 us
  local copies, waits for them, and re-layouts: 6.63 us -> 11.1 us
  Pallas kernels: 33.8 us -> 31.9 us
  waiting for transfers between devices: 22.4 us -> 24 us
    ppermute x1, waiting for transfers between devices: 0.01 us -> 10.2 us  [shards(): first_data = lax.ppermute(data, BOTH, swap)]
    all_to_all x4, waiting for transfers between devices: 21 us -> 12 us  [the longest x1 8.89 us: shards(): second = lax.all_to_all(message, 'col', 0, 0, tiled=True)]
    dot_general x9 -> x2, matrix products: 8.2 us -> 1.28 us  [the longest x1 0.94 us: shards(): jnp.einsum('crs,cs->cr', transfer, moments, precision=highest)]
    ppermute x1, starting transfers between devices: 7.88 us -> 2.59 us  [shards(): first_data = lax.ppermute(data, BOTH, swap)]
    reshape x4 -> x7, local copies, waits for them, and re-layouts: 1.06 us -> 4.78 us  [the longest x2 3.19 us: shards(): by_row = parent.reshape(rows, slots, parts)]
    ppermute x1, starting transfers between devices: 7.74 us -> 10.9 us  [shards(): near_first = lax.ppermute(near_first, BOTH, swap)]
    all_to_all x4, starting transfers between devices: 26.8 us -> 24.1 us  [the longest x1 7.77 us: shards(): second = lax.all_to_all(message, 'col', 0, 0, tiled=True)]
    another operation x1 -> x7, local copies, waits for them, and re-layouts: 0.08 us -> 2.24 us  [the longest x1 0.77 us: shards(): ends[:, None]]
  transfers between devices with their start and end apart: 6 -> 6, of which waited for: 4 -> 4; matrix products, arithmetic and copies ran while one was open for 13% -> 7% of each run, Pallas kernels for 28% -> 24%
where the time goes in v2:
time: 115 us; the launch traced here: 113 us
  starting transfers between devices  37.7 us (33%)
  Pallas kernels  31.9 us (28%)
  waiting for transfers between devices  24 us (21%)
  local copies, waits for them, and re-layouts  11.1 us (10%)
  other arithmetic  3.49 us (3%)
  matrix products  3.34 us (3%)
    pallas_call x1, Pallas kernels, near_products(): pl.pallas_call(functools.partial(near_kernel, ids_lane), out_shape=[jax.S...  26.6 us
    ppermute x1, starting transfers between devices, shards(): near_first = lax.ppermute(near_first, BOTH, swap)  10.9 us
    ppermute x1, waiting for transfers between devices, shards(): first_data = lax.ppermute(data, BOTH, swap)  10.2 us
    all_to_all x1, waiting for transfers between devices, shards(): second = lax.all_to_all(message, 'col', 0, 0, tiled=True)  8.89 us
    all_to_all x1, starting transfers between devices, shards(): second = lax.all_to_all(message, 'col', 0, 0, tiled=True)  7.77 us
    all_to_all x1, starting transfers between devices, shards(): lax.all_to_all(partial.reshape(rows, slots, 128), 'row', 0, 0, tiled=True)  7.72 us
    all_to_all x1, starting transfers between devices, shards(): from_row = lax.all_to_all(message, 'row', 0, 0, tiled=True)  5.09 us
    all_to_all x1, starting transfers between devices, shards(): lax.all_to_all(jnp.concatenate([to_second, row_locals.sum(axis=0)], axis=...  3.56 us
  transfers between devices with their start and end apart: 6, of which 4 were waited for; matrix products, arithmetic and copies ran while one was open for 7% of the time, Pallas kernels for 24%

profile of v2, /device:TPU:7, one launch (start us, length us, event | category | flops | bytes accessed | tf_op | source)
XLA Modules:
  0.0 112.5 jit_solution(3504975883048231206)
XLA Ops:
  0.0 0.0 copy-start
  0.0 0.0 copy-start.9
  0.8 0.7 fusion.9
  1.5 0.1 reshape.123
  1.6 0.1 reshape.124
  1.7 0.8 copy.24
  2.5 0.1 reshape.145
  2.6 0.0 copy-done
  2.6 0.5 convolution_bitcast_fusion
  3.1 0.0 copy-done.4
  3.1 0.9 fusion.12
  4.1 0.1 broadcast_in_dim.32
  4.1 0.6 select_maximum_fusion
  4.8 5.1 %all-to-all-start = ((f32[8,9,128]{2,1,0:T(8,128)}), f32[8,9,128]{2,1,0:T(8,128)S(1)}, u32[]{:S(2)}, u32[]{:S(2)}) async-start(f32[8,9,128]{2,1,0:T(8,128)} %select_maximum_fusion), calls=%async_computation | async-start | bytes 131072 | tf_op jit(solution)/shard_map/all_to_all | solution.py:226
  9.9 0.0 copy-done.9
  9.9 0.0 copy-done.7
  9.9 0.0 copy-start.6
  9.9 3.1 %all-to-all-done = f32[8,9,128]{2,1,0:T(8,128)S(1)} async-done(((f32[8,9,128]{2,1,0:T(8,128)}), f32[8,9,128]{2,1,0:T(8,128)S(1)}, u32[]{:S(2)}, u32[]{:S(2)}) %all-to-all-start) | async-done | bytes 36896 | tf_op jit(solution)/shard_map/all_to_all | solution.py:226
  13.0 0.1 convert_element_type.50
  13.1 0.1 slice_reduce_fusion.1
  13.2 0.1 eq.59
  13.4 0.3 fusion
  13.7 0.1 broadcast_in_dim.36
  13.8 0.0 copy-start.10
  13.8 0.0 copy-start.8
  13.9 1.0 pad_maximum_fusion
  14.9 0.0 copy-done.6
  14.9 7.8 %all-to-all-start.1 = ((bf16[16,8,3712]{2,1,0:T(8,128)(2,1)}), bf16[16,8,3712]{2,1,0:T(8,128)(2,1)S(1)}, u32[]{:S(2)}, u32[]{:S(2)}) async-start(bf16[16,8,3712]{2,1,0:T(8,128)(2,1)} %pad_maximum_fusion), calls=%async_computation.1 | async-start | bytes 1900544 | tf_op jit(solution)/shard_map/all_to_all | solution.py:244
  22.6 0.0 copy-done.10
  22.7 0.0 copy-start.3
  22.7 0.6 broadcast_in_dim_reshape.7.ends
  23.3 0.8 broadcast_in_dim_reshape.9.ends
  24.0 0.0 copy-done.8
  24.0 1.4 %reshape.126 = s32[8,128,4]{2,1,0:T(8,128)} reshape(s32[4096]{0:T(1024)S(1)} %copy-done.8) | data formatting | bytes 32768 | tf_op jit(solution)/shard_map/reshape | solution.py:248
  25.4 1.3 %reshape.125.parents = s32[1024,4]{1,0:T(8,128)} reshape(s32[4096]{0:T(1024)S(1)} %copy-done.8) | data formatting | bytes 32768 | tf_op jit(solution)/shard_map/reshape | solution.py:266
  26.7 1.8 %copy.28 = s32[8,128,4]{1,2,0:T(4,128)} copy(s32[8,128,4]{2,1,0:T(8,128)} %reshape.126) | data formatting | bytes 32768 | tf_op jit(solution)/shard_map/reshape | solution.py:248
  28.6 8.9 %all-to-all-done.1 = bf16[16,8,3712]{2,1,0:T(8,128)(2,1)S(1)} async-done(((bf16[16,8,3712]{2,1,0:T(8,128)(2,1)}), bf16[16,8,3712]{2,1,0:T(8,128)(2,1)S(1)}, u32[]{:S(2)}, u32[]{:S(2)}) %all-to-all-start.1) | async-done | bytes 950304 | tf_op jit(solution)/shard_map/all_to_all | solution.py:244
  37.5 0.9 copy-done.1
  38.4 2.6 %shard_map.92 = f32[128,128]{1,0:T(8,128)} custom-call(bf16[128,3712]{1,0:T(8,128)(2,1)} %bitcast.61, s32[8,4,128]{2,1,0:T(4,128)} %bitcast.72, s32[128,1]{1,0:T(8,128)} %broadcast_in_dim_reshape.9.ends), custom_call_target="tpu_custom_call" | custom-call | tf_op jit(solution)/shard_map/pallas_call | solution.py:250
  41.0 0.9 copy.30
  41.9 0.1 fusion.11
  42.0 0.1 multiply_reduce_fusion.1
  42.1 0.1 multiply_reduce_fusion
  42.2 0.1 pad_maximum_fusion.1
  42.3 0.7 copy.31.sent
  43.0 2.7 %shard_map.93 = f32[1024,128]{1,0:T(8,128)} custom-call(s32[1024,4]{1,0:T(8,128)} %reshape.125.parents, s32[1,128]{1,0:T(1,128)} %broadcast_in_dim_reshape.7.ends, f32[128,128]{1,0:T(8,128)} %copy.31.sent), custom_call_target="tpu_custom_call" | custom-call | tf_op jit(solution)/shard_map/pallas_call | solution.py:261
  45.7 7.7 %all-to-all-start.2 = ((f32[8,128,128]{2,1,0:T(8,128)}), f32[8,128,128]{2,1,0:T(8,128)S(1)}, u32[]{:S(2)}, u32[]{:S(2)}) async-start(f32[8,128,128]{2,1,0:T(8,128)} %bitcast.63), calls=%async_computation.2 | async-start | bytes 1048576 | tf_op jit(solution)/shard_map/all_to_all | solution.py:267
  53.5 2.6 %collective-permute-start = (bf16[32,1536]{1,0:T(8,128)(2,1)}, bf16[32,1536]{1,0:T(8,128)(2,1)S(1)}, u32[]{:S(2)}, u32[]{:S(2)}) collective-permute-start(bf16[32,1536]{1,0:T(8,128)(2,1)} %copy-done.6), channel_id=1, source_target_pairs={{0,0},{1,1},{2,16},{3,17},{4,32},{5,33},{6,48},{7,49},{8,64},{9,65... | collective-permute-start | bytes 294920 | tf_op jit(solution)/shard_map/ppermute | solution.py:211
  56.1 10.2 %collective-permute-done.first_ref = bf16[32,1536]{1,0:T(8,128)(2,1)S(1)} collective-permute-done((bf16[32,1536]{1,0:T(8,128)(2,1)}, bf16[32,1536]{1,0:T(8,128)(2,1)S(1)}, u32[]{:S(2)}, u32[]{:S(2)}) %collective-permute-start) | collective-permute-done | bytes 98336 | tf_op jit(solution)/shard_map/ppermute | solution.py:211
  66.2 26.6 %shard_map.91 = (f32[32,768]{1,0:T(8,128)S(1)}, f32[128,768]{1,0:T(8,128)S(1)}) custom-call(bf16[32,1536]{1,0:T(8,128)(2,1)S(1)} %collective-permute-done.first_ref, bf16[128,3712]{1,0:T(8,128)(2,1)S(1)} %bitcast.62), custom_call_target="tpu_custom_call" | custom-call | flops 2147483648 | bytes 1179648 | tf_op jit(solution)/shard_map/pallas_call | solution.py:138
  92.9 0.0 copy-start.5
  92.9 0.0 all-to-all-done.2
  92.9 0.8 maximum_bitcast_fusion
  93.7 3.6 %all-to-all-start.3 = ((f32[16,8,896]{2,1,0:T(8,128)}), f32[16,8,896]{2,1,0:T(8,128)S(1)}, u32[]{:S(2)}, u32[]{:S(2)}) async-start(f32[16,8,896]{2,1,0:T(8,128)} %maximum_bitcast_fusion), calls=%async_computation.3 | async-start | bytes 917504 | tf_op jit(solution)/shard_map/all_to_all | solution.py:271
  97.3 0.1 reshape_squeeze.4
  97.4 10.9 %collective-permute-start.1 = (f32[32,768]{1,0:T(8,128)S(1)}, f32[32,768]{1,0:T(8,128)S(1)}, u32[]{:S(2)}, u32[]{:S(2)}) collective-permute-start(f32[32,768]{1,0:T(8,128)S(1)} %get-tuple-element.7), channel_id=1, source_target_pairs={{0,0},{1,1},{2,16},{3,17},{4,32},{5,33},{6,48},{7,49},{8,64},{9,65... | collective-permute-start | bytes 294920 | tf_op jit(solution)/shard_map/ppermute | solution.py:270
  108.3 0.0 all-to-all-done.3
  108.4 0.1 reshape.140
  108.4 0.0 copy-done.5
  108.4 0.5 convolution_bitcast_fusion.1
  109.0 0.7 fusion.13
  109.7 0.3 fusion.1
  110.0 1.8 %collective-permute-done.1 = f32[32,768]{1,0:T(8,128)S(1)} collective-permute-done((f32[32,768]{1,0:T(8,128)S(1)}, f32[32,768]{1,0:T(8,128)S(1)}, u32[]{:S(2)}, u32[]{:S(2)}) %collective-permute-start.1) | collective-permute-done | bytes 98336 | tf_op jit(solution)/shard_map/ppermute | solution.py:270
  111.9 0.6 copy.58
  (26 shorter events, 0.3 us)
Async XLA Ops:
  0.0 2.6 %copy-start = (bf16[32,32,768]{2,1,0:T(8,128)(2,1)S(1)}, bf16[32,32,768]{2,1,0:T(8,128)(2,1)}, u32[]{:S(2)}) copy-start(bf16[32,32,768]{2,1,0:T(8,128)(2,1)} %param.11) | copy-start | bytes 4718596
  0.0 9.9 %copy-start.7 = (bf16[32,3,256]{2,0,1:T(8,128)(2,1)S(1)}, bf16[32,3,256]{2,0,1:T(8,128)(2,1)}, u32[]{:S(2)}) copy-start(bf16[32,3,256]{2,0,1:T(8,128)(2,1)} %param.9) | copy-start | bytes 147460
  0.0 3.1 %copy-start.4 = (f32[32,32,32]{2,1,0:T(8,128)S(1)}, f32[32,32,32]{2,1,0:T(8,128)}, u32[]{:S(2)}) copy-start(f32[32,32,32]{2,1,0:T(8,128)} %param.12) | copy-start | bytes 393220
  0.0 9.9 %copy-start.9 = (bf16[32,3,256]{2,0,1:T(8,128)(2,1)S(1)}, bf16[32,3,256]{2,0,1:T(8,128)(2,1)}, u32[]{:S(2)}) copy-start(bf16[32,3,256]{2,0,1:T(8,128)(2,1)} %param.10) | copy-start | bytes 147460
  4.8 8.2 %all-to-all-start = ((f32[8,9,128]{2,1,0:T(8,128)}), f32[8,9,128]{2,1,0:T(8,128)S(1)}, u32[]{:S(2)}, u32[]{:S(2)}) async-start(f32[8,9,128]{2,1,0:T(8,128)} %select_maximum_fusion), calls=%async_computation | async-start | bytes 131072 | tf_op jit(solution)/shard_map/all_to_all | solution.py:226
  9.9 4.9 %copy-start.6 = (bf16[32,1536]{1,0:T(8,128)(2,1)}, bf16[32,1536]{1,0:T(8,128)(2,1)S(1)}, u32[]{:S(2)}) copy-start(bf16[32,1536]{1,0:T(8,128)(2,1)S(1)} %constant_dynamic-update-slice_fusion) | copy-start | bytes 294916
  13.8 8.8 %copy-start.10 = (s32[2,64]{1,0:T(2,128)S(1)}, s32[2,64]{1,0:T(2,128)}, u32[]{:S(2)}) copy-start(s32[2,64]{1,0:T(2,128)} %param.16) | copy-start | bytes 1540
  13.8 10.2 %copy-start.8 = (s32[4096]{0:T(1024)S(1)}, s32[4096]{0:T(1024)}, u32[]{:S(2)}) copy-start(s32[4096]{0:T(1024)} %param.13) | copy-start | bytes 49156
  14.9 22.6 %all-to-all-start.1 = ((bf16[16,8,3712]{2,1,0:T(8,128)(2,1)}), bf16[16,8,3712]{2,1,0:T(8,128)(2,1)S(1)}, u32[]{:S(2)}, u32[]{:S(2)}) async-start(bf16[16,8,3712]{2,1,0:T(8,128)(2,1)} %pad_maximum_fusion), calls=%async_computation.1 | async-start | bytes 1900544 | tf_op jit(solution)/shard_map/all_to_all | solution.py:244
  22.7 19.4 %copy-start.3 = (f32[64,32,32]{0,2,1:T(8,128)S(1)}, f32[64,32,32]{0,2,1:T(8,128)}, u32[]{:S(2)}) copy-start(f32[64,32,32]{0,2,1:T(8,128)} %param.17) | copy-start | bytes 786436
  37.5 0.9 copy-start.1
  42.1 24.1 %copy-start.2 = (bf16[16,8,3712]{2,1,0:T(8,128)(2,1)S(1)}, bf16[16,8,3712]{2,1,0:T(8,128)(2,1)}, u32[]{:S(2)}) copy-start(bf16[16,8,3712]{2,1,0:T(8,128)(2,1)} %copy-done.1) | copy-start | bytes 2850820
  45.7 47.1 %all-to-all-start.2 = ((f32[8,128,128]{2,1,0:T(8,128)}), f32[8,128,128]{2,1,0:T(8,128)S(1)}, u32[]{:S(2)}, u32[]{:S(2)}) async-start(f32[8,128,128]{2,1,0:T(8,128)} %bitcast.63), calls=%async_computation.2 | async-start | bytes 1048576 | tf_op jit(solution)/shard_map/all_to_all | solution.py:267
  53.5 12.8 %collective-permute-start = (bf16[32,1536]{1,0:T(8,128)(2,1)}, bf16[32,1536]{1,0:T(8,128)(2,1)S(1)}, u32[]{:S(2)}, u32[]{:S(2)}) collective-permute-start(bf16[32,1536]{1,0:T(8,128)(2,1)} %copy-done.6), channel_id=1, source_target_pairs={{0,0},{1,1},{2,16},{3,17},{4,32},{5,33},{6,48},{7,49},{8,64},{9,65... | collective-permute-start | bytes 294920 | tf_op jit(solution)/shard_map/ppermute | solution.py:211
  92.9 15.6 %copy-start.5 = (f32[32,32,32]{2,1,0:T(8,128)S(1)}, f32[32,32,32]{2,1,0:T(8,128)}, u32[]{:S(2)}) copy-start(f32[32,32,32]{2,1,0:T(8,128)} %param.12) | copy-start | bytes 393220
  93.7 14.6 %all-to-all-start.3 = ((f32[16,8,896]{2,1,0:T(8,128)}), f32[16,8,896]{2,1,0:T(8,128)S(1)}, u32[]{:S(2)}, u32[]{:S(2)}) async-start(f32[16,8,896]{2,1,0:T(8,128)} %maximum_bitcast_fusion), calls=%async_computation.3 | async-start | bytes 917504 | tf_op jit(solution)/shard_map/all_to_all | solution.py:271
  97.4 14.5 %collective-permute-start.1 = (f32[32,768]{1,0:T(8,128)S(1)}, f32[32,768]{1,0:T(8,128)S(1)}, u32[]{:S(2)}, u32[]{:S(2)}) collective-permute-start(f32[32,768]{1,0:T(8,128)S(1)} %get-tuple-element.7), channel_id=1, source_target_pairs={{0,0},{1,1},{2,16},{3,17},{4,32},{5,33},{6,48},{7,49},{8,64},{9,65... | collective-permute-start | bytes 294920 | tf_op jit(solution)/shard_map/ppermute | solution.py:270

commit v3 on v2

v3 whole, which is shorter than its diff:
```python
import functools
import math

import jax
import jax.numpy as jnp
from jax import lax
from jax.experimental import pallas as pl
from jax.experimental.pallas import tpu as pltpu
from jax.sharding import PartitionSpec as P

REG_EPS = 0.02
EPS_SQ = REG_EPS * REG_EPS
STOKES_SCALE = 1.0 / (8.0 * math.pi)
BOTH = ("row", "col")
GROUP = 16
PANELS = 256
FIELD_ROWS = 40
POINT_ROWS = 16
f32, bf16 = jnp.float32, jnp.bfloat16


def pieces(value, count):
    out = []
    for _ in range(count):
        head = value.astype(bf16).astype(f32)
        out.append(head)
        value = value - head
    return out


def put(ref, row, value):
    for half in range(2):
        ref[half, row * GROUP : (row + 1) * GROUP, :] = value[:, half * 128 : (half + 1) * 128]


def get(ref, row):
    return jnp.concatenate([ref[half, row * GROUP : (row + 1) * GROUP, :] for half in range(2)], 1)


def split_parts(block):
    parts = [block[:, k * PANELS : (k + 1) * PANELS] for k in range(6)]
    return parts[:3], parts[3:]


def prepare_source(block, field, left):
    q, y = split_parts(block)
    one, zero = jnp.ones_like(q[0]), jnp.zeros_like(q[0])
    norm = pieces(y[0] * y[0] + y[1] * y[1] + y[2] * y[2] + EPS_SQ / 2, 3)
    along = y[0] * q[0] + y[1] * q[1] + y[2] * q[2]
    rows = list(q) + pieces(along, 3)
    for i in range(3):
        for j in range(3):
            rows += pieces(y[i] * q[j], 2)
    for i in range(3):
        rows += pieces(y[i] * along, 3)
    rows += [zero] * (FIELD_ROWS - len(rows))
    for k, value in enumerate(rows):
        put(field, k, value)
    for k, value in enumerate([-2 * v for v in y] + norm + [one] * 3 + [zero] * 7):
        put(left, k, value)


def prepare_target(block, right):
    _, x = split_parts(block)
    one, zero = jnp.ones_like(x[0]), jnp.zeros_like(x[0])
    norm = pieces(x[0] * x[0] + x[1] * x[1] + x[2] * x[2] + EPS_SQ / 2, 3)
    for k, value in enumerate(x + [one] * 3 + norm + [zero] * 7):
        put(right, k, value)


def finish(block, sums, point_sums):
    _, x = split_parts(block)
    mom = [get(sums, i) for i in range(3)]
    dot = x[0] * mom[0] + x[1] * mom[1] + x[2] * mom[2] - (get(sums, 3) + get(sums, 4) + get(sums, 5))
    out = []
    for i in range(3):
        cross = sum(x[j] * (get(sums, 6 + 2 * (3 * i + j)) + get(sums, 7 + 2 * (3 * i + j))) for j in range(3))
        tail = get(sums, 24 + 3 * i) + get(sums, 25 + 3 * i) + get(sums, 26 + 3 * i)
        total = get(point_sums, i) + EPS_SQ * mom[i] + ((x[i] * dot - cross) + tail)
        out.append(total * STOKES_SCALE)
    return out


def near_kernel(ids_lane, to_first, first_ref, second_ref, out, field, left, right, sums, point_sums):
    own = first_ref.shape[0]
    if to_first:
        out[...] = jnp.zeros_like(out)

    def group(g, carry):
        rows = pl.ds(pl.multiple_of(g * GROUP, GROUP), GROUP)
        ids = second_ref[rows, ids_lane : ids_lane + 128].astype(f32)[:, :own]
        chosen = (ids == lax.broadcasted_iota(jnp.int32, (GROUP, own), 1).astype(f32)).astype(bf16)
        first = jnp.dot(chosen, first_ref[...], preferred_element_type=f32)
        second = second_ref[rows, : 6 * PANELS].astype(f32)
        source, target = (second, first) if to_first else (first, second)
        prepare_source(source, field, left)
        prepare_target(target, right)

        def slot(s, carry):
            def load(ref, count):
                return jnp.concatenate(
                    [ref[half, pl.ds(s, count, stride=GROUP), :] for half in range(2)], 1
                ).astype(bf16)

            def store(ref, count, value):
                for half in range(2):
                    ref[half, pl.ds(s, count, stride=GROUP), :] = value[:, half * 128 : (half + 1) * 128]

            shifted = lax.dot_general(
                load(left, POINT_ROWS),
                load(right, POINT_ROWS),
                (((0,), (0,)), ((), ())),
                preferred_element_type=f32,
            )
            inv = lax.rsqrt(shifted)
            cube = inv * inv * inv
            moments = load(field, FIELD_ROWS)
            store(sums, FIELD_ROWS, jnp.dot(moments, cube.astype(bf16), preferred_element_type=f32))
            store(point_sums, 8, jnp.dot(moments[:8], inv.astype(bf16), preferred_element_type=f32))
            return carry

        lax.fori_loop(0, GROUP, slot, 0, unroll=GROUP)
        for i, value in enumerate(finish(target, sums, point_sums)):
            lanes = slice(i * PANELS, (i + 1) * PANELS)
            if not to_first:
                out[rows, lanes] = value
                continue
            for piece in pieces(value, 3):
                out[:, lanes] += lax.dot_general(
                    chosen, piece.astype(bf16), (((0,), (0,)), ((), ())), preferred_element_type=f32
                )
        return carry

    lax.fori_loop(0, second_ref.shape[0] // GROUP, group, 0)


def near_sums(first, second, ids_lane, to_first):
    slots = second.shape[0]
    vmem = pl.BlockSpec(memory_space=pltpu.VMEM)

    def rows(count):
        return pltpu.VMEM((2, count * GROUP, 128), f32)

    return pl.pallas_call(
        functools.partial(near_kernel, ids_lane, to_first),
        out_shape=jax.ShapeDtypeStruct((first.shape[0] if to_first else slots, 3 * PANELS), f32),
        in_specs=[vmem] * 2,
        out_specs=vmem,
        scratch_shapes=[rows(FIELD_ROWS), rows(POINT_ROWS), rows(POINT_ROWS), rows(FIELD_ROWS), rows(8)],
        compiler_params=pltpu.CompilerParams(vmem_limit_bytes=32 << 20),
        cost_estimate=pl.CostEstimate(
            flops=slots * 2 * 64 * PANELS * PANELS, bytes_accessed=slots * 9216, transcendentals=0
        ),
    )(first, second)


def far_kernel(start, recv, parents, ends, factors, out, hits):
    parts = parents.shape[1]
    count = ends.shape[1]
    rank = 128 // parts
    for m in range(parts):
        hits[:, m * count : (m + 1) * count] = (parents[:, m : m + 1] == ends[...]).astype(f32).astype(bf16)
    slots = recv.shape[0]
    found = jnp.zeros((128, parts * count), f32)
    for r in range(hits.shape[0] // slots):
        found += lax.dot_general(
            recv[:, start + 128 * r : start + 128 * (r + 1)],
            hits[r * slots : (r + 1) * slots, :],
            (((0,), (0,)), ((), ())),
            preferred_element_type=f32,
        )
    at_ends = sum(found[m * rank : (m + 1) * rank, m * count : (m + 1) * count] for m in range(parts))
    sent = jnp.sum(factors[...] * at_ends[None], axis=1)
    sent = jnp.concatenate([sent[:, count // 2 :], sent[:, : count // 2]], axis=1)
    zero = jnp.zeros_like(sent)
    table = [
        jnp.concatenate([piece if m == k else zero for k in range(parts)], axis=1)
        for piece in pieces(sent, 2)
        for m in range(parts)
    ]
    both = lax.dot_general(
        hits[...],
        jnp.concatenate(table, axis=0).astype(bf16),
        (((1,), (1,)), ((), ())),
        preferred_element_type=f32,
    )
    out[...] = both[:, :128] + both[:, 128:]


def one_hot(ids, count):
    return (ids[:, None] == jnp.arange(count, dtype=ids.dtype)[None, :]).astype(f32)


def shards(density, coords, basis, transfer, parent, near_pairs, near_count, far_pairs, coupling):
    highest = lax.Precision.HIGHEST
    own, _, panels = density.shape
    rank = basis.shape[1]
    rows, cols = lax.axis_size("row"), lax.axis_size("col")
    half = cols // rows
    my_row, my_col = lax.axis_index("row"), lax.axis_index("col")
    slots = near_pairs.shape[1]
    per_pair = slots // cols
    block = slots // rows
    vmem = pl.BlockSpec(memory_space=pltpu.VMEM)

    swap = [
        (r * cols + half * p + h, p * cols + half * r + h)
        for r in range(rows)
        for p in range(rows)
        for h in range(half)
    ]
    flat = density.reshape(own, 3 * panels)
    data = jnp.concatenate([flat, coords.reshape(own, 3 * panels)], axis=1)
    first_data = lax.ppermute(data, BOTH, swap)

    moments = jnp.einsum("crk,ck->cr", basis, flat, preferred_element_type=f32)
    lifted = jnp.einsum("crs,cs->cr", transfer, moments, precision=highest).reshape(-1, 128)
    lift_rows = lifted.shape[0]
    live = jnp.arange(slots) < near_count[0]
    ids = jnp.where(live[None], near_pairs % own, -1).astype(f32)
    ids = ids.reshape(2, rows, block).transpose(1, 0, 2).reshape(rows, 1, 2 * block)
    message = jnp.concatenate(
        [
            jnp.broadcast_to(lifted[None], (rows, lift_rows, 128)),
            jnp.pad(ids, ((0, 0), (0, 0), (0, 128 - 2 * block))),
        ],
        axis=1,
    )
    first_data, message = lax.optimization_barrier((first_data, message))
    from_row = lax.all_to_all(message, "row", 0, 0, tiled=True)

    own_first = from_row[:, lift_rows, :block].reshape(-1)
    own_second = from_row[:, lift_rows, block : 2 * block].reshape(-1)
    place = jnp.arange(slots)
    same_owner = (place // block == my_row) & (half * my_row + place % block // per_pair == my_col)
    back_ids = jnp.where(same_owner & (own_first == own_second), -1.0, own_second)
    picked = jnp.dot(one_hot(own_second, own).astype(bf16), data, preferred_element_type=f32)
    row_lifted = from_row[:, :lift_rows, :].astype(bf16).transpose(1, 0, 2).reshape(lift_rows, -1)
    message = jnp.concatenate(
        [
            picked.astype(bf16),
            jnp.broadcast_to(own_first[:, None], (slots, 128)).astype(bf16),
            jnp.tile(row_lifted, (cols, 1)),
        ],
        axis=1,
    )
    second = lax.all_to_all(message, "col", 0, 0, tiled=True)
    ids_lane = 6 * panels

    factors = jnp.concatenate([coupling.transpose(1, 2, 0), coupling.transpose(2, 1, 0)], axis=2)
    partial = pl.pallas_call(
        functools.partial(far_kernel, ids_lane + 128),
        out_shape=jax.ShapeDtypeStruct((rows * slots, 128), f32),
        in_specs=[vmem] * 4,
        out_specs=vmem,
        scratch_shapes=[pltpu.VMEM((rows * slots, far_pairs.size * (128 // rank)), bf16)],
        compiler_params=pltpu.CompilerParams(vmem_limit_bytes=32 << 20),
    )(second, parent.reshape(-1, 128 // rank), far_pairs[::-1].reshape(1, -1), factors)
    first_data, partial = lax.optimization_barrier((first_data, partial))
    row_locals = lax.all_to_all(partial.reshape(rows, slots, 128), "row", 0, 0, tiled=True)

    to_second = near_sums(first_data, second, ids_lane, False)
    returned = lax.all_to_all(
        jnp.concatenate([to_second, row_locals.sum(axis=0)], axis=1), "col", 0, 0, tiled=True
    )
    first_data, to_second = lax.optimization_barrier((first_data, to_second))
    near_first = lax.ppermute(near_sums(first_data, second, ids_lane, True), BOTH, swap)
    near_second = jnp.einsum(
        "sc,sk->ck", one_hot(back_ids, own), returned[:, : 3 * panels], precision=highest
    )
    parent_locals = returned[:, 3 * panels :].reshape(cols, lift_rows, 128).sum(axis=0).reshape(own, rank)
    local_coef = jnp.einsum("csr,cs->cr", transfer, parent_locals, precision=highest)
    far_part = jnp.einsum("crk,cr->ck", basis.astype(f32), local_coef, precision=highest)
    return (near_first + (near_second + far_part)).reshape(own, 3, panels)


def solution(mesh):
    placed = (
        P(BOTH, None, None),
        P(BOTH, None, None),
        P(BOTH, None, None),
        P(BOTH, None, None),
        P(),
        P(None, BOTH),
        P(BOTH),
        P(None, BOTH),
        P(BOTH, None, None),
    )
    return jax.shard_map(
        shards, mesh=mesh, in_specs=placed, out_specs=P(BOTH, None, None), check_vma=False
    )
```

time: 115 us -> 103 us (0.90); the launches traced: 113 us -> 103 us
  blocking collectives: 0 us -> 7.19 us
  waiting for transfers between devices: 24 us -> 17.5 us
  local copies, waits for them, and re-layouts: 11.1 us -> 5.84 us
  starting transfers between devices: 37.7 us -> 32.5 us
    ppermute x1, waiting for transfers between devices: 10.2 us -> 1.69 us  [shards(): first_data = lax.ppermute(data, BOTH, swap)]
    all_to_all x0 -> x1, blocking collectives: none -> 7.19 us  [shards(): from_row = lax.all_to_all(message, 'row', 0, 0, tiled=True)]
    ppermute x1, starting transfers between devices: 2.59 us -> 8.77 us  [shards(): first_data = lax.ppermute(data, BOTH, swap)]
    all_to_all x1 -> x0, starting transfers between devices: 5.09 us -> none  [shards(): from_row = lax.all_to_all(message, 'row', 0, 0, tiled=True)]
    ppermute x1, waiting for transfers between devices: 1.83 us -> 6.03 us  [shards(): lax.ppermute(near_sums(first_data, second, ids_lane, True), BOTH, swap)]
    ppermute x1, starting transfers between devices: 10.9 us -> 6.89 us  [shards(): lax.ppermute(near_sums(first_data, second, ids_lane, True), BOTH, swap)]
    reshape x4 -> x3, local copies, waits for them, and re-layouts: 5.18 us -> 1.26 us  [the longest x1 0.65 us: shards(): return (near_first + (near_second + far_part)).reshape(own, 3, panels)]
    all_to_all x1 -> x0, waiting for transfers between devices: 3.07 us -> none  [shards(): from_row = lax.all_to_all(message, 'row', 0, 0, tiled=True)]
  transfers between devices with their start and end apart: 6 -> 5, of which waited for: 4 -> 3; matrix products, arithmetic and copies ran while one was open for 7% -> 7% of each run, Pallas kernels for 24% -> 29%
where the time goes in v3:
time: 103 us
  starting transfers between devices  32.5 us (32%)
  Pallas kernels  31.6 us (31%)
  waiting for transfers between devices  17.5 us (17%)
  blocking collectives  7.19 us (7%)
  local copies, waits for them, and re-layouts  5.84 us (6%)
  other arithmetic  3.72 us (4%)
  matrix products  3.35 us (3%)
    pallas_call x2, Pallas kernels, near_sums(): pl.pallas_call(functools.partial(near_kernel, ids_lane, to_first), out_sh...  29.8 us
    all_to_all x1, waiting for transfers between devices, shards(): second = lax.all_to_all(message, 'col', 0, 0, tiled=True)  9.78 us
    ppermute x1, starting transfers between devices, shards(): first_data = lax.ppermute(data, BOTH, swap)  8.77 us
    all_to_all x1, starting transfers between devices, shards(): lax.all_to_all(partial.reshape(rows, slots, 128), 'row', 0, 0, tiled=True)  7.36 us
    all_to_all x1, blocking collectives, shards(): from_row = lax.all_to_all(message, 'row', 0, 0, tiled=True)  7.19 us
    ppermute x1, starting transfers between devices, shards(): lax.ppermute(near_sums(first_data, second, ids_lane, True), BOTH, swap)  6.89 us
    ppermute x1, waiting for transfers between devices, shards(): lax.ppermute(near_sums(first_data, second, ids_lane, True), BOTH, swap)  6.03 us
    all_to_all x1, starting transfers between devices, shards(): second = lax.all_to_all(message, 'col', 0, 0, tiled=True)  5.88 us
  transfers between devices with their start and end apart: 5, of which 3 were waited for; matrix products, arithmetic and copies ran while one was open for 7% of the time, Pallas kernels for 29%

profile of v3, /device:TPU:7, one launch (start us, length us, event | category | flops | bytes accessed | tf_op | source)
XLA Modules:
  0.0 102.6 jit_solution(4527207559535852841)
XLA Ops:
  0.0 0.0 copy-start
  0.0 0.0 copy-start.3
  0.0 1.0 copy.35
  1.0 0.8 copy.34
  1.8 8.8 %collective-permute-start = (bf16[32,1536]{1,0:T(8,128)(2,1)S(1)}, bf16[32,1536]{1,0:T(8,128)(2,1)S(1)}, u32[]{:S(2)}, u32[]{:S(2)}) collective-permute-start(bf16[32,1536]{1,0:T(8,128)(2,1)S(1)} %constant_dynamic-update-slice_fusion), channel_id=1, source_target_pairs={{0,0},{1,1},{2,16},{3,17},{4,32},{5,33},{6,48},{7,49},{8,64},{9,65... | collective-permute-start | bytes 294920 | tf_op jit(solution)/shard_map/ppermute | solution.py:214
  10.6 0.8 copy.20
  12.1 0.7 fusion.8
  12.8 0.1 reshape.110
  12.8 0.1 reshape.111
  12.9 0.1 reshape.127
  13.0 0.0 copy-done
  13.0 0.5 convolution_bitcast_fusion
  13.5 0.0 copy-done.3
  13.5 0.9 fusion.10
  14.4 0.1 broadcast_in_dim.32
  14.6 1.7 %collective-permute-done.first_ref = bf16[32,1536]{1,0:T(8,128)(2,1)S(1)} collective-permute-done((bf16[32,1536]{1,0:T(8,128)(2,1)S(1)}, bf16[32,1536]{1,0:T(8,128)(2,1)S(1)}, u32[]{:S(2)}, u32[]{:S(2)}) %collective-permute-start) | collective-permute-done | bytes 98336 | tf_op jit(solution)/shard_map/ppermute | solution.py:214
  16.2 7.2 %all_to_all.30 = f32[8,9,128]{2,1,0:T(8,128)S(1)} all-to-all(f32[8,9,128]{2,1,0:T(8,128)S(1)} %select_maximum_fusion), channel_id=1, replica_groups=mesh['row'=8,'col'=16] {'row'}, dimensions={0} | all-to-all | bytes 73728 | tf_op jit(solution)/shard_map/all_to_all | solution.py:230
  23.5 0.1 convert_element_type.30
  23.5 0.1 slice_reduce_fusion.1
  23.6 0.1 eq.59
  23.7 0.3 fusion
  24.0 0.0 copy-start.6
  24.0 0.0 copy-start.5
  24.1 0.1 broadcast_in_dim.36
  24.2 0.0 copy-start.2
  24.2 0.9 pad_maximum_fusion
  25.1 5.9 %all-to-all-start.1 = ((bf16[16,8,2688]{2,1,0:T(8,128)(2,1)}), bf16[16,8,2688]{2,1,0:T(8,128)(2,1)S(1)}, u32[]{:S(2)}, u32[]{:S(2)}) async-start(bf16[16,8,2688]{2,1,0:T(8,128)(2,1)} %pad_maximum_fusion), calls=%async_computation.1 | async-start | bytes 1376256 | tf_op jit(solution)/shard_map/all_to_all | solution.py:247
  31.0 0.0 copy-done.6
  31.0 0.1 reshape.113.ends
  31.1 0.0 copy-done.5
  31.1 0.5 reshape.112.parents
  31.6 0.0 copy-done.2
  31.6 0.3 copy.40
  32.0 1.2 %pad_maximum_fusion.1.factors = f32[32,32,128]{2,1,0:T(8,128)S(1)} fusion(f32[32,32,64]{2,1,0:T(8,128)S(1)} %bitcast.63, f32[32,32,64]{2,1,0:T(8,128)} %bitcast.62), kind=kLoop, calls=%fused_computation.7 | loop fusion | flops 131072 | bytes 1048576 | tf_op jit(solution)/shard_map/concatenate | solution.py:250
  33.2 9.8 %all-to-all-done.1 = bf16[16,8,2688]{2,1,0:T(8,128)(2,1)S(1)} async-done(((bf16[16,8,2688]{2,1,0:T(8,128)(2,1)}), bf16[16,8,2688]{2,1,0:T(8,128)(2,1)S(1)}, u32[]{:S(2)}, u32[]{:S(2)}) %all-to-all-start.1) | async-done | bytes 688160 | tf_op jit(solution)/shard_map/all_to_all | solution.py:247
  43.0 1.8 %shard_map.91 = f32[1024,128]{1,0:T(8,128)S(1)} custom-call(bf16[128,2688]{1,0:T(8,128)(2,1)S(1)} %bitcast.58, s32[1024,4]{1,0:T(8,128)S(1)} %reshape.112.parents, s32[1,128]{1,0:T(1,128)S(1)} %reshape.113.ends, f32[32,32,128]{2,1,0:T(8,128)S(1)} %pad_maximum_fusion.1.factors), custom_call_target="tpu_custom_call" | custom-call | tf_op jit(solution)/shard_map/pallas_call | solution.py:251
  44.8 0.0 copy-start.1
  44.8 0.8 copy-done.1
  45.5 7.4 %all-to-all-start.2 = ((f32[8,128,128]{2,1,0:T(8,128)}), f32[8,128,128]{2,1,0:T(8,128)S(1)}, u32[]{:S(2)}, u32[]{:S(2)}) async-start(f32[8,128,128]{2,1,0:T(8,128)} %bitcast.61), calls=%async_computation.2 | async-start | bytes 1048576 | tf_op jit(solution)/shard_map/all_to_all | solution.py:260
  52.9 14.6 %shard_map.92 = f32[128,768]{1,0:T(8,128)S(1)} custom-call(bf16[32,1536]{1,0:T(8,128)(2,1)S(1)} %collective-permute-done.first_ref, bf16[128,2688]{1,0:T(8,128)(2,1)S(1)} %bitcast.59), custom_call_target="tpu_custom_call" | custom-call | flops 1073741824 | bytes 1179648 | tf_op jit(solution)/shard_map/pallas_call | solution.py:144
  67.5 0.0 all-to-all-done.2
  67.6 0.8 maximum_bitcast_fusion
  68.4 3.6 %all-to-all-start.3 = ((f32[16,8,896]{2,1,0:T(8,128)}), f32[16,8,896]{2,1,0:T(8,128)S(1)}, u32[]{:S(2)}, u32[]{:S(2)}) async-start(f32[16,8,896]{2,1,0:T(8,128)} %maximum_bitcast_fusion), calls=%async_computation.3 | async-start | bytes 917504 | tf_op jit(solution)/shard_map/all_to_all | solution.py:263
  71.9 0.1 reshape_squeeze.4
  72.0 0.0 copy-start.4
  72.1 15.2 %shard_map.93 = f32[32,768]{1,0:T(8,128)S(1)} custom-call(bf16[32,1536]{1,0:T(8,128)(2,1)S(1)} %collective-permute-done.first_ref, bf16[128,2688]{1,0:T(8,128)(2,1)S(1)} %bitcast.60), custom_call_target="tpu_custom_call" | custom-call | flops 1073741824 | bytes 1179648 | tf_op jit(solution)/shard_map/pallas_call | solution.py:144
  87.3 6.9 %collective-permute-start.1 = (f32[32,768]{1,0:T(8,128)S(1)}, f32[32,768]{1,0:T(8,128)S(1)}, u32[]{:S(2)}, u32[]{:S(2)}) collective-permute-start(f32[32,768]{1,0:T(8,128)S(1)} %shard_map.93), channel_id=1, source_target_pairs={{0,0},{1,1},{2,16},{3,17},{4,32},{5,33},{6,48},{7,49},{8,64},{9,65... | collective-permute-start | bytes 294920 | tf_op jit(solution)/shard_map/ppermute | solution.py:267
  94.2 0.0 all-to-all-done.3
  94.2 0.1 reshape.122
  94.3 0.0 copy-done.4
  94.3 0.5 convolution_bitcast_fusion.1
  94.8 0.7 fusion.11
  95.6 6.0 %collective-permute-done.1 = f32[32,768]{1,0:T(8,128)S(1)} collective-permute-done((f32[32,768]{1,0:T(8,128)S(1)}, f32[32,768]{1,0:T(8,128)S(1)}, u32[]{:S(2)}, u32[]{:S(2)}) %collective-permute-start.1) | collective-permute-done | bytes 98336 | tf_op jit(solution)/shard_map/ppermute | solution.py:267
  101.6 0.3 fusion.1
  101.9 0.7 copy.41
  (13 shorter events, 0.2 us)
Async XLA Ops:
  0.0 13.0 %copy-start = (bf16[32,32,768]{2,1,0:T(8,128)(2,1)S(1)}, bf16[32,32,768]{2,1,0:T(8,128)(2,1)}, u32[]{:S(2)}) copy-start(bf16[32,32,768]{2,1,0:T(8,128)(2,1)} %param.11) | copy-start | bytes 4718596
  0.0 13.5 %copy-start.3 = (f32[32,32,32]{2,1,0:T(8,128)S(1)}, f32[32,32,32]{2,1,0:T(8,128)}, u32[]{:S(2)}) copy-start(f32[32,32,32]{2,1,0:T(8,128)} %param.12) | copy-start | bytes 393220
  1.8 14.5 %collective-permute-start = (bf16[32,1536]{1,0:T(8,128)(2,1)S(1)}, bf16[32,1536]{1,0:T(8,128)(2,1)S(1)}, u32[]{:S(2)}, u32[]{:S(2)}) collective-permute-start(bf16[32,1536]{1,0:T(8,128)(2,1)S(1)} %constant_dynamic-update-slice_fusion), channel_id=1, source_target_pairs={{0,0},{1,1},{2,16},{3,17},{4,32},{5,33},{6,48},{7,49},{8,64},{9,65... | collective-permute-start | bytes 294920 | tf_op jit(solution)/shard_map/ppermute | solution.py:214
  24.0 7.0 %copy-start.6 = (s32[2,64]{1,0:T(2,128)S(1)}, s32[2,64]{1,0:T(2,128)}, u32[]{:S(2)}) copy-start(s32[2,64]{1,0:T(2,128)} %param.16) | copy-start | bytes 1540
  24.0 7.1 %copy-start.5 = (s32[4096]{0:T(1024)S(1)}, s32[4096]{0:T(1024)}, u32[]{:S(2)}) copy-start(s32[4096]{0:T(1024)} %param.13) | copy-start | bytes 49156
  24.2 7.5 %copy-start.2 = (f32[64,32,32]{0,2,1:T(8,128)S(1)}, f32[64,32,32]{0,2,1:T(8,128)}, u32[]{:S(2)}) copy-start(f32[64,32,32]{0,2,1:T(8,128)} %param.17) | copy-start | bytes 786436
  25.1 17.9 %all-to-all-start.1 = ((bf16[16,8,2688]{2,1,0:T(8,128)(2,1)}), bf16[16,8,2688]{2,1,0:T(8,128)(2,1)S(1)}, u32[]{:S(2)}, u32[]{:S(2)}) async-start(bf16[16,8,2688]{2,1,0:T(8,128)(2,1)} %pad_maximum_fusion), calls=%async_computation.1 | async-start | bytes 1376256 | tf_op jit(solution)/shard_map/all_to_all | solution.py:247
  44.8 0.8 copy-start.1
  45.5 22.0 %all-to-all-start.2 = ((f32[8,128,128]{2,1,0:T(8,128)}), f32[8,128,128]{2,1,0:T(8,128)S(1)}, u32[]{:S(2)}, u32[]{:S(2)}) async-start(f32[8,128,128]{2,1,0:T(8,128)} %bitcast.61), calls=%async_computation.2 | async-start | bytes 1048576 | tf_op jit(solution)/shard_map/all_to_all | solution.py:260
  68.4 25.8 %all-to-all-start.3 = ((f32[16,8,896]{2,1,0:T(8,128)}), f32[16,8,896]{2,1,0:T(8,128)S(1)}, u32[]{:S(2)}, u32[]{:S(2)}) async-start(f32[16,8,896]{2,1,0:T(8,128)} %maximum_bitcast_fusion), calls=%async_computation.3 | async-start | bytes 917504 | tf_op jit(solution)/shard_map/all_to_all | solution.py:263
  72.0 22.2 %copy-start.4 = (f32[32,32,32]{2,1,0:T(8,128)S(1)}, f32[32,32,32]{2,1,0:T(8,128)}, u32[]{:S(2)}) copy-start(f32[32,32,32]{2,1,0:T(8,128)} %param.12) | copy-start | bytes 393220
  87.3 14.3 %collective-permute-start.1 = (f32[32,768]{1,0:T(8,128)S(1)}, f32[32,768]{1,0:T(8,128)S(1)}, u32[]{:S(2)}, u32[]{:S(2)}) collective-permute-start(f32[32,768]{1,0:T(8,128)S(1)} %shard_map.93), channel_id=1, source_target_pairs={{0,0},{1,1},{2,16},{3,17},{4,32},{5,33},{6,48},{7,49},{8,64},{9,65... | collective-permute-start | bytes 294920 | tf_op jit(solution)/shard_map/ppermute | solution.py:267

commit v4 on v3

--- a/solution.py
+++ b/solution.py
@@ -13,8 +13,9 @@
 STOKES_SCALE = 1.0 / (8.0 * math.pi)
 BOTH = ("row", "col")
 GROUP = 16
+BATCH = 8
 PANELS = 256
-FIELD_ROWS = 40
+FIELD_ROWS = 32
 POINT_ROWS = 16
 f32, bf16 = jnp.float32, jnp.bfloat16
 
@@ -45,18 +46,18 @@
 def prepare_source(block, field, left):
     q, y = split_parts(block)
     one, zero = jnp.ones_like(q[0]), jnp.zeros_like(q[0])
-    norm = pieces(y[0] * y[0] + y[1] * y[1] + y[2] * y[2] + EPS_SQ / 2, 3)
+    square = y[0] * y[0] + y[1] * y[1] + y[2] * y[2]
     along = y[0] * q[0] + y[1] * q[1] + y[2] * q[2]
-    rows = list(q) + pieces(along, 3)
+    rows = list(q)
     for i in range(3):
         for j in range(3):
             rows += pieces(y[i] * q[j], 2)
     for i in range(3):
-        rows += pieces(y[i] * along, 3)
+        rows += pieces(square * q[i] + y[i] * along, 3)
     rows += [zero] * (FIELD_ROWS - len(rows))
     for k, value in enumerate(rows):
         put(field, k, value)
-    for k, value in enumerate([-2 * v for v in y] + norm + [one] * 3 + [zero] * 7):
+    for k, value in enumerate([-2 * v for v in y] + pieces(square + EPS_SQ / 2, 3) + [one] * 3 + [zero] * 7):
         put(left, k, value)
 
 
@@ -68,20 +69,21 @@
         put(right, k, value)
 
 
-def finish(block, sums, point_sums):
+def finish(block, sums):
     _, x = split_parts(block)
     mom = [get(sums, i) for i in range(3)]
-    dot = x[0] * mom[0] + x[1] * mom[1] + x[2] * mom[2] - (get(sums, 3) + get(sums, 4) + get(sums, 5))
+    cross = [[get(sums, 3 + 2 * (3 * i + j)) + get(sums, 4 + 2 * (3 * i + j)) for j in range(3)] for i in range(3)]
+    dot = x[0] * mom[0] + x[1] * mom[1] + x[2] * mom[2] - (cross[0][0] + cross[1][1] + cross[2][2])
+    square = x[0] * x[0] + x[1] * x[1] + x[2] * x[2] + 2 * EPS_SQ
     out = []
     for i in range(3):
-        cross = sum(x[j] * (get(sums, 6 + 2 * (3 * i + j)) + get(sums, 7 + 2 * (3 * i + j))) for j in range(3))
-        tail = get(sums, 24 + 3 * i) + get(sums, 25 + 3 * i) + get(sums, 26 + 3 * i)
-        total = get(point_sums, i) + EPS_SQ * mom[i] + ((x[i] * dot - cross) + tail)
-        out.append(total * STOKES_SCALE)
+        mixed = sum(x[j] * (cross[i][j] + 2 * cross[j][i]) for j in range(3))
+        tail = get(sums, 21 + 3 * i) + get(sums, 22 + 3 * i) + get(sums, 23 + 3 * i)
+        out.append(((square * mom[i] + x[i] * dot - mixed) + tail) * STOKES_SCALE)
     return out
 
 
-def near_kernel(ids_lane, to_first, first_ref, second_ref, out, field, left, right, sums, point_sums):
+def near_kernel(ids_lane, to_first, first_ref, second_ref, out, field, left, right, sums):
     own = first_ref.shape[0]
     if to_first:
         out[...] = jnp.zeros_like(out)
@@ -96,31 +98,31 @@
         prepare_source(source, field, left)
         prepare_target(target, right)
 
-        def slot(s, carry):
-            def load(ref, count):
-                return jnp.concatenate(
-                    [ref[half, pl.ds(s, count, stride=GROUP), :] for half in range(2)], 1
-                ).astype(bf16)
-
-            def store(ref, count, value):
+        def load(ref, count, s):
+            parts = [ref[half, pl.ds(s, count, stride=GROUP), :] for half in range(2)]
+            return jnp.concatenate(parts, 1).astype(bf16)
+
+        for start in range(0, GROUP, BATCH):
+            batch = range(start, start + BATCH)
+            shifted = [
+                lax.dot_general(
+                    load(left, POINT_ROWS, s),
+                    load(right, POINT_ROWS, s),
+                    (((0,), (0,)), ((), ())),
+                    preferred_element_type=f32,
+                )
+                for s in batch
+            ]
+            cubes = []
+            for value in shifted:
+                inv = lax.rsqrt(value)
+                cubes.append((inv * inv * inv).astype(bf16))
+            for s, cube in zip(batch, cubes):
+                total = jnp.dot(load(field, FIELD_ROWS, s), cube, preferred_element_type=f32)
                 for half in range(2):
-                    ref[half, pl.ds(s, count, stride=GROUP), :] = value[:, half * 128 : (half + 1) * 128]
-
-            shifted = lax.dot_general(
-                load(left, POINT_ROWS),
-                load(right, POINT_ROWS),
-                (((0,), (0,)), ((), ())),
-                preferred_element_type=f32,
-            )
-            inv = lax.rsqrt(shifted)
-            cube = inv * inv * inv
-            moments = load(field, FIELD_ROWS)
-            store(sums, FIELD_ROWS, jnp.dot(moments, cube.astype(bf16), preferred_element_type=f32))
-            store(point_sums, 8, jnp.dot(moments[:8], inv.astype(bf16), preferred_element_type=f32))
-            return carry
-
-        lax.fori_loop(0, GROUP, slot, 0, unroll=GROUP)
-        for i, value in enumerate(finish(target, sums, point_sums)):
+                    sums[half, pl.ds(s, FIELD_ROWS, stride=GROUP), :] = total[:, half * 128 : (half + 1) * 128]
+
+        for i, value in enumerate(finish(target, sums)):
             lanes = slice(i * PANELS, (i + 1) * PANELS)
             if not to_first:
                 out[rows, lanes] = value
@@ -146,7 +148,7 @@
         out_shape=jax.ShapeDtypeStruct((first.shape[0] if to_first else slots, 3 * PANELS), f32),
         in_specs=[vmem] * 2,
         out_specs=vmem,
-        scratch_shapes=[rows(FIELD_ROWS), rows(POINT_ROWS), rows(POINT_ROWS), rows(FIELD_ROWS), rows(8)],
+        scratch_shapes=[rows(FIELD_ROWS), rows(POINT_ROWS), rows(POINT_ROWS), rows(FIELD_ROWS)],
         compiler_params=pltpu.CompilerParams(vmem_limit_bytes=32 << 20),
         cost_estimate=pl.CostEstimate(
             flops=slots * 2 * 64 * PANELS * PANELS, bytes_accessed=slots * 9216, transcendentals=0
@@ -226,8 +228,8 @@
         ],
         axis=1,
     )
-    first_data, message = lax.optimization_barrier((first_data, message))
     from_row = lax.all_to_all(message, "row", 0, 0, tiled=True)
+    first_data, from_row = lax.optimization_barrier((first_data, from_row))
 
     own_first = from_row[:, lift_rows, :block].reshape(-1)
     own_second = from_row[:, lift_rows, block : 2 * block].reshape(-1)

time: 103 us -> 93 us (0.903)
  Pallas kernels: 31.6 us -> 25.3 us
  starting transfers between devices: 32.5 us -> 29.9 us
  waiting for transfers between devices: 17.5 us -> 16.1 us
    pallas_call x2, Pallas kernels: 29.8 us -> 23.5 us  [near_sums(): pl.pallas_call(functools.partial(near_kernel, ids_lane, to_first), out_sh...]
    all_to_all x1, starting transfers between devices: 5.88 us -> 3.6 us  [shards(): second = lax.all_to_all(message, 'col', 0, 0, tiled=True)]
    ppermute x1, waiting for transfers between devices: 1.69 us -> 0.01 us  [shards(): first_data = lax.ppermute(data, BOTH, swap)]
  transfers between devices with their start and end apart: 5 -> 5, of which waited for: 3 -> 2; matrix products, arithmetic and copies ran while one was open for 7% -> 8% of each run, Pallas kernels for 29% -> 25%
where the time goes in v4:
time: 93 us; the launch traced here: 92.4 us
  starting transfers between devices  29.9 us (32%)
  Pallas kernels  25.3 us (27%)
  waiting for transfers between devices  16.1 us (17%)
  blocking collectives  7.33 us (8%)
  local copies, waits for them, and re-layouts  5.84 us (6%)
  other arithmetic  3.72 us (4%)
  matrix products  3.35 us (4%)
    pallas_call x2, Pallas kernels, near_sums(): pl.pallas_call(functools.partial(near_kernel, ids_lane, to_first), out_sh...  23.5 us
    all_to_all x1, waiting for transfers between devices, shards(): second = lax.all_to_all(message, 'col', 0, 0, tiled=True)  10 us
    ppermute x1, starting transfers between devices, shards(): first_data = lax.ppermute(data, BOTH, swap)  8.77 us
    all_to_all x1, blocking collectives, shards(): from_row = lax.all_to_all(message, 'row', 0, 0, tiled=True)  7.33 us
    all_to_all x1, starting transfers between devices, shards(): lax.all_to_all(partial.reshape(rows, slots, 128), 'row', 0, 0, tiled=True)  7.06 us
    ppermute x1, starting transfers between devices, shards(): lax.ppermute(near_sums(first_data, second, ids_lane, True), BOTH, swap)  6.89 us
    ppermute x1, waiting for transfers between devices, shards(): lax.ppermute(near_sums(first_data, second, ids_lane, True), BOTH, swap)  6.03 us
    all_to_all x1, starting transfers between devices, shards(): second = lax.all_to_all(message, 'col', 0, 0, tiled=True)  3.6 us
  transfers between devices with their start and end apart: 5, of which 2 were waited for; matrix products, arithmetic and copies ran while one was open for 8% of the time, Pallas kernels for 25%

profile of v4, /device:TPU:7, one launch (start us, length us, event | category | flops | bytes accessed | tf_op | source)
XLA Modules:
  0.0 92.4 jit_solution(6944519989769741492)
XLA Ops:
  0.0 0.0 copy-start
  0.0 0.0 copy-start.3
  0.0 1.0 %copy.35 = bf16[3,4,8,256]{3,2,0,1:T(8,128)(2,1)S(1)} copy(bf16[3,4,8,256]{3,2,1,0:T(8,128)(2,1)} %bitcast.72) | data formatting | bytes 98304 | tf_op jit(solution)/shard_map/reshape | solution.py:215
  1.0 0.8 copy.34
  1.8 8.8 %collective-permute-start = (bf16[32,1536]{1,0:T(8,128)(2,1)S(1)}, bf16[32,1536]{1,0:T(8,128)(2,1)S(1)}, u32[]{:S(2)}, u32[]{:S(2)}) collective-permute-start(bf16[32,1536]{1,0:T(8,128)(2,1)S(1)} %constant_dynamic-update-slice_fusion), channel_id=1, source_target_pairs={{0,0},{1,1},{2,16},{3,17},{4,32},{5,33},{6,48},{7,49},{8,64},{9,65... | collective-permute-start | bytes 294920 | tf_op jit(solution)/shard_map/ppermute | solution.py:216
  10.6 0.8 copy.20
  12.1 0.7 fusion.8
  12.8 0.1 reshape.110
  12.8 0.1 reshape.111
  12.9 0.1 reshape.127
  13.0 0.0 copy-done
  13.0 0.5 convolution_bitcast_fusion
  13.5 0.0 copy-done.3
  13.5 0.9 %fusion.10 = f32[32,1,32]{2,1,0:T(1,128)S(1)} fusion(f32[32,32,1]{1,2,0:T(1,128)S(1)} %convolution_bitcast_fusion, f32[32,32,32]{2,1,0:T(8,128)S(1)} %copy-done.3), kind=kOutput, calls=%fused_computation.46 | convolution fusion | flops 393216 | bytes 139264 | tf_op jit(solution)/shard_map/crs,cs->cr/dot_general | solution.py:219
  14.4 0.1 broadcast_in_dim.32
  14.6 7.3 %all_to_all.30 = f32[8,9,128]{2,1,0:T(8,128)S(1)} all-to-all(f32[8,9,128]{2,1,0:T(8,128)S(1)} %select_maximum_fusion), channel_id=1, replica_groups=mesh['row'=8,'col'=16] {'row'}, dimensions={0} | all-to-all | bytes 73728 | tf_op jit(solution)/shard_map/all_to_all | solution.py:231
  21.9 0.0 collective-permute-done.first_ref
  21.9 0.1 slice_reduce_fusion.1
  22.0 0.1 convert_element_type.30
  22.1 0.1 eq.59
  22.2 0.3 fusion
  22.5 0.0 copy-start.6
  22.5 0.0 copy-start.5
  22.5 0.1 broadcast_in_dim.36
  22.6 0.0 copy-start.2
  22.6 0.9 pad_maximum_fusion
  23.5 3.6 %all-to-all-start.1 = ((bf16[16,8,2688]{2,1,0:T(8,128)(2,1)}), bf16[16,8,2688]{2,1,0:T(8,128)(2,1)S(1)}, u32[]{:S(2)}, u32[]{:S(2)}) async-start(bf16[16,8,2688]{2,1,0:T(8,128)(2,1)} %pad_maximum_fusion), calls=%async_computation.1 | async-start | bytes 1376256 | tf_op jit(solution)/shard_map/all_to_all | solution.py:249
  27.1 0.0 copy-done.6
  27.2 0.1 reshape.113.ends
  27.3 0.0 copy-done.5
  27.3 0.5 reshape.112.parents
  27.8 0.0 copy-done.2
  27.8 0.3 copy.40
  28.1 1.2 %pad_maximum_fusion.1.factors = f32[32,32,128]{2,1,0:T(8,128)S(1)} fusion(f32[32,32,64]{2,1,0:T(8,128)S(1)} %bitcast.63, f32[32,32,64]{2,1,0:T(8,128)} %bitcast.62), kind=kLoop, calls=%fused_computation.7 | loop fusion | flops 131072 | bytes 1048576 | tf_op jit(solution)/shard_map/concatenate | solution.py:252
  29.4 10.0 %all-to-all-done.1 = bf16[16,8,2688]{2,1,0:T(8,128)(2,1)S(1)} async-done(((bf16[16,8,2688]{2,1,0:T(8,128)(2,1)}), bf16[16,8,2688]{2,1,0:T(8,128)(2,1)S(1)}, u32[]{:S(2)}, u32[]{:S(2)}) %all-to-all-start.1) | async-done | bytes 688160 | tf_op jit(solution)/shard_map/all_to_all | solution.py:249
  39.4 1.8 %shard_map.91 = f32[1024,128]{1,0:T(8,128)S(1)} custom-call(bf16[128,2688]{1,0:T(8,128)(2,1)S(1)} %bitcast.58, s32[1024,4]{1,0:T(8,128)S(1)} %reshape.112.parents, s32[1,128]{1,0:T(1,128)S(1)} %reshape.113.ends, f32[32,32,128]{2,1,0:T(8,128)S(1)} %pad_maximum_fusion.1.factors), custom_call_target="tpu_custom_call" | custom-call | tf_op jit(solution)/shard_map/pallas_call | solution.py:253
  41.2 0.0 copy-start.1
  41.2 0.8 copy-done.1
  42.0 7.1 %all-to-all-start.2 = ((f32[8,128,128]{2,1,0:T(8,128)}), f32[8,128,128]{2,1,0:T(8,128)S(1)}, u32[]{:S(2)}, u32[]{:S(2)}) async-start(f32[8,128,128]{2,1,0:T(8,128)} %bitcast.61), calls=%async_computation.2 | async-start | bytes 1048576 | tf_op jit(solution)/shard_map/all_to_all | solution.py:262
  49.0 11.2 %shard_map.92 = f32[128,768]{1,0:T(8,128)S(1)} custom-call(bf16[32,1536]{1,0:T(8,128)(2,1)S(1)} %collective-permute-done.first_ref, bf16[128,2688]{1,0:T(8,128)(2,1)S(1)} %bitcast.59), custom_call_target="tpu_custom_call" | custom-call | flops 1073741824 | bytes 1179648 | tf_op jit(solution)/shard_map/pallas_call | solution.py:146
  60.3 0.0 all-to-all-done.2
  60.3 0.8 maximum_bitcast_fusion
  61.1 3.6 %all-to-all-start.3 = ((f32[16,8,896]{2,1,0:T(8,128)}), f32[16,8,896]{2,1,0:T(8,128)S(1)}, u32[]{:S(2)}, u32[]{:S(2)}) async-start(f32[16,8,896]{2,1,0:T(8,128)} %maximum_bitcast_fusion), calls=%async_computation.3 | async-start | bytes 917504 | tf_op jit(solution)/shard_map/all_to_all | solution.py:265
  64.7 0.1 reshape_squeeze.4
  64.8 0.0 copy-start.4
  64.8 12.3 %shard_map.93 = f32[32,768]{1,0:T(8,128)S(1)} custom-call(bf16[32,1536]{1,0:T(8,128)(2,1)S(1)} %collective-permute-done.first_ref, bf16[128,2688]{1,0:T(8,128)(2,1)S(1)} %bitcast.60), custom_call_target="tpu_custom_call" | custom-call | flops 1073741824 | bytes 1179648 | tf_op jit(solution)/shard_map/pallas_call | solution.py:146
  77.1 6.9 %collective-permute-start.1 = (f32[32,768]{1,0:T(8,128)S(1)}, f32[32,768]{1,0:T(8,128)S(1)}, u32[]{:S(2)}, u32[]{:S(2)}) collective-permute-start(f32[32,768]{1,0:T(8,128)S(1)} %shard_map.93), channel_id=1, source_target_pairs={{0,0},{1,1},{2,16},{3,17},{4,32},{5,33},{6,48},{7,49},{8,64},{9,65... | collective-permute-start | bytes 294920 | tf_op jit(solution)/shard_map/ppermute | solution.py:269
  84.0 0.0 all-to-all-done.3
  84.0 0.1 reshape.122
  84.1 0.0 copy-done.4
  84.1 0.5 convolution_bitcast_fusion.1
  84.6 0.7 fusion.11
  85.3 6.0 %collective-permute-done.1 = f32[32,768]{1,0:T(8,128)S(1)} collective-permute-done((f32[32,768]{1,0:T(8,128)S(1)}, f32[32,768]{1,0:T(8,128)S(1)}, u32[]{:S(2)}, u32[]{:S(2)}) %collective-permute-start.1) | collective-permute-done | bytes 98336 | tf_op jit(solution)/shard_map/ppermute | solution.py:269
  91.4 0.3 fusion.1
  91.7 0.7 copy.41
  (13 shorter events, 0.2 us)
Async XLA Ops:
  0.0 13.0 %copy-start = (bf16[32,32,768]{2,1,0:T(8,128)(2,1)S(1)}, bf16[32,32,768]{2,1,0:T(8,128)(2,1)}, u32[]{:S(2)}) copy-start(bf16[32,32,768]{2,1,0:T(8,128)(2,1)} %param.11) | copy-start | bytes 4718596
  0.0 13.5 %copy-start.3 = (f32[32,32,32]{2,1,0:T(8,128)S(1)}, f32[32,32,32]{2,1,0:T(8,128)}, u32[]{:S(2)}) copy-start(f32[32,32,32]{2,1,0:T(8,128)} %param.12) | copy-start | bytes 393220
  1.8 20.1 %collective-permute-start = (bf16[32,1536]{1,0:T(8,128)(2,1)S(1)}, bf16[32,1536]{1,0:T(8,128)(2,1)S(1)}, u32[]{:S(2)}, u32[]{:S(2)}) collective-permute-start(bf16[32,1536]{1,0:T(8,128)(2,1)S(1)} %constant_dynamic-update-slice_fusion), channel_id=1, source_target_pairs={{0,0},{1,1},{2,16},{3,17},{4,32},{5,33},{6,48},{7,49},{8,64},{9,65... | collective-permute-start | bytes 294920 | tf_op jit(solution)/shard_map/ppermute | solution.py:216
  22.5 4.7 %copy-start.6 = (s32[2,64]{1,0:T(2,128)S(1)}, s32[2,64]{1,0:T(2,128)}, u32[]{:S(2)}) copy-start(s32[2,64]{1,0:T(2,128)} %param.16) | copy-start | bytes 1540
  22.5 4.8 %copy-start.5 = (s32[4096]{0:T(1024)S(1)}, s32[4096]{0:T(1024)}, u32[]{:S(2)}) copy-start(s32[4096]{0:T(1024)} %param.13) | copy-start | bytes 49156
  22.6 5.2 %copy-start.2 = (f32[64,32,32]{0,2,1:T(8,128)S(1)}, f32[64,32,32]{0,2,1:T(8,128)}, u32[]{:S(2)}) copy-start(f32[64,32,32]{0,2,1:T(8,128)} %param.17) | copy-start | bytes 786436
  23.5 15.9 %all-to-all-start.1 = ((bf16[16,8,2688]{2,1,0:T(8,128)(2,1)}), bf16[16,8,2688]{2,1,0:T(8,128)(2,1)S(1)}, u32[]{:S(2)}, u32[]{:S(2)}) async-start(bf16[16,8,2688]{2,1,0:T(8,128)(2,1)} %pad_maximum_fusion), calls=%async_computation.1 | async-start | bytes 1376256 | tf_op jit(solution)/shard_map/all_to_all | solution.py:249
  41.2 0.8 copy-start.1
  42.0 18.3 %all-to-all-start.2 = ((f32[8,128,128]{2,1,0:T(8,128)}), f32[8,128,128]{2,1,0:T(8,128)S(1)}, u32[]{:S(2)}, u32[]{:S(2)}) async-start(f32[8,128,128]{2,1,0:T(8,128)} %bitcast.61), calls=%async_computation.2 | async-start | bytes 1048576 | tf_op jit(solution)/shard_map/all_to_all | solution.py:262
  61.1 22.8 %all-to-all-start.3 = ((f32[16,8,896]{2,1,0:T(8,128)}), f32[16,8,896]{2,1,0:T(8,128)S(1)}, u32[]{:S(2)}, u32[]{:S(2)}) async-start(f32[16,8,896]{2,1,0:T(8,128)} %maximum_bitcast_fusion), calls=%async_computation.3 | async-start | bytes 917504 | tf_op jit(solution)/shard_map/all_to_all | solution.py:265
  64.8 19.3 %copy-start.4 = (f32[32,32,32]{2,1,0:T(8,128)S(1)}, f32[32,32,32]{2,1,0:T(8,128)}, u32[]{:S(2)}) copy-start(f32[32,32,32]{2,1,0:T(8,128)} %param.12) | copy-start | bytes 393220
  77.1 14.3 %collective-permute-start.1 = (f32[32,768]{1,0:T(8,128)S(1)}, f32[32,768]{1,0:T(8,128)S(1)}, u32[]{:S(2)}, u32[]{:S(2)}) collective-permute-start(f32[32,768]{1,0:T(8,128)S(1)} %shard_map.93), channel_id=1, source_target_pairs={{0,0},{1,1},{2,16},{3,17},{4,32},{5,33},{6,48},{7,49},{8,64},{9,65... | collective-permute-start | bytes 294920 | tf_op jit(solution)/shard_map/ppermute | solution.py:269

commit v5 on v4

--- a/solution.py
+++ b/solution.py
@@ -57,6 +57,8 @@
     rows += [zero] * (FIELD_ROWS - len(rows))
     for k, value in enumerate(rows):
         put(field, k, value)
+    if left is None:
+        return
     for k, value in enumerate([-2 * v for v in y] + pieces(square + EPS_SQ / 2, 3) + [one] * 3 + [zero] * 7):
         put(left, k, value)
 
@@ -83,10 +85,9 @@
     return out
 
 
-def near_kernel(ids_lane, to_first, first_ref, second_ref, out, field, left, right, sums):
+def near_kernel(ids_lane, first_ref, second_ref, near_first, to_second, field_a, left, field_b, right, sums_a, sums_b):
     own = first_ref.shape[0]
-    if to_first:
-        out[...] = jnp.zeros_like(out)
+    near_first[...] = jnp.zeros_like(near_first)
 
     def group(g, carry):
         rows = pl.ds(pl.multiple_of(g * GROUP, GROUP), GROUP)
@@ -94,13 +95,20 @@
         chosen = (ids == lax.broadcasted_iota(jnp.int32, (GROUP, own), 1).astype(f32)).astype(bf16)
         first = jnp.dot(chosen, first_ref[...], preferred_element_type=f32)
         second = second_ref[rows, : 6 * PANELS].astype(f32)
-        source, target = (second, first) if to_first else (first, second)
-        prepare_source(source, field, left)
-        prepare_target(target, right)
+        prepare_source(first, field_a, left)
+        prepare_source(second, field_b, None)
+        prepare_target(second, right)
 
         def load(ref, count, s):
             parts = [ref[half, pl.ds(s, count, stride=GROUP), :] for half in range(2)]
             return jnp.concatenate(parts, 1).astype(bf16)
+
+        def apply(field, cube, dim, sums, s):
+            total = lax.dot_general(
+                load(field, FIELD_ROWS, s), cube, (((1,), (dim,)), ((), ())), preferred_element_type=f32
+            )
+            for half in range(2):
+                sums[half, pl.ds(s, FIELD_ROWS, stride=GROUP), :] = total[:, half * 128 : (half + 1) * 128]
 
         for start in range(0, GROUP, BATCH):
             batch = range(start, start + BATCH)
@@ -118,17 +126,15 @@
                 inv = lax.rsqrt(value)
                 cubes.append((inv * inv * inv).astype(bf16))
             for s, cube in zip(batch, cubes):
-                total = jnp.dot(load(field, FIELD_ROWS, s), cube, preferred_element_type=f32)
-                for half in range(2):
-                    sums[half, pl.ds(s, FIELD_ROWS, stride=GROUP), :] = total[:, half * 128 : (half + 1) * 128]
-
-        for i, value in enumerate(finish(target, sums)):
-            lanes = slice(i * PANELS, (i + 1) * PANELS)
-            if not to_first:
-                out[rows, lanes] = value
-                continue
+                apply(field_a, cube, 0, sums_b, s)
+            for s, cube in zip(batch, cubes):
+                apply(field_b, cube, 1, sums_a, s)
+
+        for i, value in enumerate(finish(second, sums_b)):
+            to_second[rows, i * PANELS : (i + 1) * PANELS] = value
+        for i, value in enumerate(finish(first, sums_a)):
             for piece in pieces(value, 3):
-                out[:, lanes] += lax.dot_general(
+                near_first[:, i * PANELS : (i + 1) * PANELS] += lax.dot_general(
                     chosen, piece.astype(bf16), (((0,), (0,)), ((), ())), preferred_element_type=f32
                 )
         return carry
@@ -136,7 +142,7 @@
     lax.fori_loop(0, second_ref.shape[0] // GROUP, group, 0)
 
 
-def near_sums(first, second, ids_lane, to_first):
+def near_sums(first, second, ids_lane):
     slots = second.shape[0]
     vmem = pl.BlockSpec(memory_space=pltpu.VMEM)
 
@@ -144,14 +150,17 @@
         return pltpu.VMEM((2, count * GROUP, 128), f32)
 
     return pl.pallas_call(
-        functools.partial(near_kernel, ids_lane, to_first),
-        out_shape=jax.ShapeDtypeStruct((first.shape[0] if to_first else slots, 3 * PANELS), f32),
+        functools.partial(near_kernel, ids_lane),
+        out_shape=[
+            jax.ShapeDtypeStruct((first.shape[0], 3 * PANELS), f32),
+            jax.ShapeDtypeStruct((slots, 3 * PANELS), f32),
+        ],
         in_specs=[vmem] * 2,
-        out_specs=vmem,
-        scratch_shapes=[rows(FIELD_ROWS), rows(POINT_ROWS), rows(POINT_ROWS), rows(FIELD_ROWS)],
+        out_specs=[vmem] * 2,
+        scratch_shapes=[rows(FIELD_ROWS), rows(POINT_ROWS)] * 2 + [rows(FIELD_ROWS)] * 2,
         compiler_params=pltpu.CompilerParams(vmem_limit_bytes=32 << 20),
         cost_estimate=pl.CostEstimate(
-            flops=slots * 2 * 64 * PANELS * PANELS, bytes_accessed=slots * 9216, transcendentals=0
+            flops=slots * 2 * 2 * 64 * PANELS * PANELS, bytes_accessed=slots * 9216, transcendentals=0
         ),
     )(first, second)
 
@@ -261,12 +270,11 @@
     first_data, partial = lax.optimization_barrier((first_data, partial))
     row_locals = lax.all_to_all(partial.reshape(rows, slots, 128), "row", 0, 0, tiled=True)
 
-    to_second = near_sums(first_data, second, ids_lane, False)
+    near_first, to_second = near_sums(first_data, second, ids_lane)
+    near_first = lax.ppermute(near_first, BOTH, swap)
     returned = lax.all_to_all(
         jnp.concatenate([to_second, row_locals.sum(axis=0)], axis=1), "col", 0, 0, tiled=True
     )
-    first_data, to_second = lax.optimization_barrier((first_data, to_second))
-    near_first = lax.ppermute(near_sums(first_data, second, ids_lane, True), BOTH, swap)
     near_second = jnp.einsum(
         "sc,sk->ck", one_hot(back_ids, own), returned[:, : 3 * panels], precision=highest
     )

time: 93 us -> 87 us (0.935)
  Pallas kernels: 25.3 us -> 20.1 us
    pallas_call x2 -> x1, Pallas kernels: 23.5 us -> 17.5 us  [near_sums(): pl.pallas_call(functools.partial(near_kernel, ids_lane), out_shape=[jax.S...]
    all_to_all x1, waiting for transfers between devices: 0.01 us -> 3.65 us  [shards(): lax.all_to_all(jnp.concatenate([to_second, row_locals.sum(axis=0)], axis=...]
    ppermute x1, waiting for transfers between devices: 6.03 us -> 2.38 us  [shards(): near_first = lax.ppermute(near_first, BOTH, swap)]
    unnamed x17 -> x15, local copies, waits for them, and re-layouts: 1.97 us -> 1.19 us
  transfers between devices with their start and end apart: 5 -> 5, of which waited for: 2 -> 3; matrix products, arithmetic and copies ran while one was open for 8% -> 8% of each run, Pallas kernels for 25% -> 20%
where the time goes in v5:
time: 87 us; the launch traced here: 86.4 us
  starting transfers between devices  29.9 us (34%)
  Pallas kernels  20.1 us (23%)
  waiting for transfers between devices  16.1 us (19%)
  blocking collectives  7.33 us (8%)
  local copies, waits for them, and re-layouts  5.07 us (6%)
  other arithmetic  3.71 us (4%)
  matrix products  3.35 us (4%)
  between operations  0.87 us (1%)
    pallas_call x1, Pallas kernels, near_sums(): pl.pallas_call(functools.partial(near_kernel, ids_lane), out_shape=[jax.S...  17.5 us
    all_to_all x1, waiting for transfers between devices, shards(): second = lax.all_to_all(message, 'col', 0, 0, tiled=True)  10 us
    ppermute x1, starting transfers between devices, shards(): first_data = lax.ppermute(data, BOTH, swap)  8.77 us
    all_to_all x1, blocking collectives, shards(): from_row = lax.all_to_all(message, 'row', 0, 0, tiled=True)  7.33 us
    all_to_all x1, starting transfers between devices, shards(): lax.all_to_all(partial.reshape(rows, slots, 128), 'row', 0, 0, tiled=True)  7.06 us
    ppermute x1, starting transfers between devices, shards(): near_first = lax.ppermute(near_first, BOTH, swap)  6.89 us
    all_to_all x1, waiting for transfers between devices, shards(): lax.all_to_all(jnp.concatenate([to_second, row_locals.sum(axis=0)], axis=...  3.65 us
    all_to_all x1, starting transfers between devices, shards(): second = lax.all_to_all(message, 'col', 0, 0, tiled=True)  3.6 us
  transfers between devices with their start and end apart: 5, of which 3 were waited for; matrix products, arithmetic and copies ran while one was open for 8% of the time, Pallas kernels for 20%

profile of v5, /device:TPU:7, one launch (start us, length us, event | category | flops | bytes accessed | tf_op | source)
XLA Modules:
  0.0 86.4 jit_solution(16051508364248316944)
XLA Ops:
  0.0 0.0 copy-start
  0.0 0.0 copy-start.2
  0.0 1.0 %copy.35 = bf16[3,4,8,256]{3,2,0,1:T(8,128)(2,1)S(1)} copy(bf16[3,4,8,256]{3,2,1,0:T(8,128)(2,1)} %bitcast.70) | data formatting | bytes 98304 | tf_op jit(solution)/shard_map/reshape | solution.py:224
  1.0 0.8 copy.34
  1.8 8.8 %collective-permute-start = (bf16[32,1536]{1,0:T(8,128)(2,1)S(1)}, bf16[32,1536]{1,0:T(8,128)(2,1)S(1)}, u32[]{:S(2)}, u32[]{:S(2)}) collective-permute-start(bf16[32,1536]{1,0:T(8,128)(2,1)S(1)} %constant_dynamic-update-slice_fusion), channel_id=1, source_target_pairs={{0,0},{1,1},{2,16},{3,17},{4,32},{5,33},{6,48},{7,49},{8,64},{9,65... | collective-permute-start | bytes 294920 | tf_op jit(solution)/shard_map/ppermute | solution.py:225
  10.6 0.8 copy.20
  12.1 0.7 fusion.8
  12.8 0.1 reshape.110
  12.8 0.1 reshape.111
  12.9 0.1 reshape.127
  13.0 0.0 copy-done
  13.0 0.5 convolution_bitcast_fusion
  13.5 0.0 copy-done.2
  13.5 0.9 %fusion.10 = f32[32,1,32]{2,1,0:T(1,128)S(1)} fusion(f32[32,32,1]{1,2,0:T(1,128)S(1)} %convolution_bitcast_fusion, f32[32,32,32]{2,1,0:T(8,128)S(1)} %copy-done.2), kind=kOutput, calls=%fused_computation.46 | convolution fusion | flops 393216 | bytes 139264 | tf_op jit(solution)/shard_map/crs,cs->cr/dot_general | solution.py:228
  14.4 0.1 broadcast_in_dim.32
  14.6 7.3 %all_to_all.30 = f32[8,9,128]{2,1,0:T(8,128)S(1)} all-to-all(f32[8,9,128]{2,1,0:T(8,128)S(1)} %select_maximum_fusion), channel_id=1, replica_groups=mesh['row'=8,'col'=16] {'row'}, dimensions={0} | all-to-all | bytes 73728 | tf_op jit(solution)/shard_map/all_to_all | solution.py:240
  21.9 0.0 collective-permute-done.first_ref
  21.9 0.1 slice_reduce_fusion.1
  22.0 0.1 convert_element_type.30
  22.1 0.1 eq.59
  22.2 0.3 fusion
  22.5 0.0 copy-start.5
  22.5 0.0 copy-start.4
  22.5 0.1 broadcast_in_dim.36
  22.6 0.0 copy-start.1
  22.6 0.9 %pad_maximum_fusion = bf16[16,8,2688]{2,1,0:T(8,128)(2,1)} fusion(bf16[16,8,1024]{2,1,0:T(8,128)(2,1)S(1)} %tile.9, bf16[16,8,128]{2,1,0:T(8,128)(2,1)S(1)} %broadcast_in_dim.36, bf16[16,8,1536]{2,1,0:T(8,128)(2,1)S(1)} %fusion), kind=kLoop, calls=%fused_computation.6 | loop fusion | flops 2064384 | bytes 1376256 | tf_op jit(solution)/shard_map/concatenate | solution.py:250
  23.5 3.6 %all-to-all-start.1 = ((bf16[16,8,2688]{2,1,0:T(8,128)(2,1)}), bf16[16,8,2688]{2,1,0:T(8,128)(2,1)S(1)}, u32[]{:S(2)}, u32[]{:S(2)}) async-start(bf16[16,8,2688]{2,1,0:T(8,128)(2,1)} %pad_maximum_fusion), calls=%async_computation.1 | async-start | bytes 1376256 | tf_op jit(solution)/shard_map/all_to_all | solution.py:258
  27.1 0.0 copy-done.5
  27.2 0.1 reshape.113.ends
  27.3 0.0 copy-done.4
  27.3 0.5 reshape.112.parents
  27.8 0.0 copy-done.1
  27.8 0.3 copy.40
  28.1 1.2 %pad_maximum_fusion.1.factors = f32[32,32,128]{2,1,0:T(8,128)S(1)} fusion(f32[32,32,64]{2,1,0:T(8,128)S(1)} %bitcast.61, f32[32,32,64]{2,1,0:T(8,128)} %bitcast.60), kind=kLoop, calls=%fused_computation.7 | loop fusion | flops 131072 | bytes 1048576 | tf_op jit(solution)/shard_map/concatenate | solution.py:261
  29.4 10.0 %all-to-all-done.1 = bf16[16,8,2688]{2,1,0:T(8,128)(2,1)S(1)} async-done(((bf16[16,8,2688]{2,1,0:T(8,128)(2,1)}), bf16[16,8,2688]{2,1,0:T(8,128)(2,1)S(1)}, u32[]{:S(2)}, u32[]{:S(2)}) %all-to-all-start.1) | async-done | bytes 688160 | tf_op jit(solution)/shard_map/all_to_all | solution.py:258
  39.4 2.5 %shard_map.91 = f32[1024,128]{1,0:T(8,128)} custom-call(bf16[128,2688]{1,0:T(8,128)(2,1)S(1)} %bitcast.58, s32[1024,4]{1,0:T(8,128)S(1)} %reshape.112.parents, s32[1,128]{1,0:T(1,128)S(1)} %reshape.113.ends, f32[32,32,128]{2,1,0:T(8,128)S(1)} %pad_maximum_fusion.1.factors), custom_call_target="tpu_custom_call" | custom-call | tf_op jit(solution)/shard_map/pallas_call | solution.py:262
  42.0 7.1 %all-to-all-start.2 = ((f32[8,128,128]{2,1,0:T(8,128)}), f32[8,128,128]{2,1,0:T(8,128)S(1)}, u32[]{:S(2)}, u32[]{:S(2)}) async-start(f32[8,128,128]{2,1,0:T(8,128)} %bitcast.14), calls=%async_computation.2 | async-start | bytes 1048576 | tf_op jit(solution)/shard_map/all_to_all | solution.py:271
  49.0 17.5 %shard_map.92 = (f32[32,768]{1,0:T(8,128)S(1)}, f32[128,768]{1,0:T(8,128)S(1)}) custom-call(bf16[32,1536]{1,0:T(8,128)(2,1)S(1)} %collective-permute-done.first_ref, bf16[128,2688]{1,0:T(8,128)(2,1)S(1)} %bitcast.59), custom_call_target="tpu_custom_call" | custom-call | flops 2147483648 | bytes 1179648 | tf_op jit(solution)/shard_map/pallas_call | solution.py:152
  66.5 0.0 copy-start.3
  66.6 0.0 all-to-all-done.2
  66.6 0.8 maximum_bitcast_fusion
  67.4 3.6 %all-to-all-start.3 = ((f32[16,8,896]{2,1,0:T(8,128)}), f32[16,8,896]{2,1,0:T(8,128)S(1)}, u32[]{:S(2)}, u32[]{:S(2)}) async-start(f32[16,8,896]{2,1,0:T(8,128)} %maximum_bitcast_fusion), calls=%async_computation.3 | async-start | bytes 917504 | tf_op jit(solution)/shard_map/all_to_all | solution.py:275
  71.0 0.1 reshape_squeeze.4
  71.1 6.9 %collective-permute-start.1 = (f32[32,768]{1,0:T(8,128)S(1)}, f32[32,768]{1,0:T(8,128)S(1)}, u32[]{:S(2)}, u32[]{:S(2)}) collective-permute-start(f32[32,768]{1,0:T(8,128)S(1)} %get-tuple-element.14), channel_id=1, source_target_pairs={{0,0},{1,1},{2,16},{3,17},{4,32},{5,33},{6,48},{7,49},{8,64},{9,65... | collective-permute-start | bytes 294920 | tf_op jit(solution)/shard_map/ppermute | solution.py:274
  78.0 3.7 %all-to-all-done.3 = f32[16,8,896]{2,1,0:T(8,128)S(1)} async-done(((f32[16,8,896]{2,1,0:T(8,128)}), f32[16,8,896]{2,1,0:T(8,128)S(1)}, u32[]{:S(2)}, u32[]{:S(2)}) %all-to-all-start.3) | async-done | bytes 458784 | tf_op jit(solution)/shard_map/all_to_all | solution.py:275
  81.6 0.1 reshape.122
  81.7 0.0 copy-done.3
  81.7 0.5 convolution_bitcast_fusion.1
  82.3 0.7 fusion.11
  83.0 2.4 %collective-permute-done.1 = f32[32,768]{1,0:T(8,128)S(1)} collective-permute-done((f32[32,768]{1,0:T(8,128)S(1)}, f32[32,768]{1,0:T(8,128)S(1)}, u32[]{:S(2)}, u32[]{:S(2)}) %collective-permute-start.1) | collective-permute-done | bytes 98336 | tf_op jit(solution)/shard_map/ppermute | solution.py:274
  85.4 0.3 fusion.1
  85.7 0.7 copy.41
  (13 shorter events, 0.2 us)
Async XLA Ops:
  0.0 13.0 %copy-start = (bf16[32,32,768]{2,1,0:T(8,128)(2,1)S(1)}, bf16[32,32,768]{2,1,0:T(8,128)(2,1)}, u32[]{:S(2)}) copy-start(bf16[32,32,768]{2,1,0:T(8,128)(2,1)} %param.11) | copy-start | bytes 4718596
  0.0 13.5 %copy-start.2 = (f32[32,32,32]{2,1,0:T(8,128)S(1)}, f32[32,32,32]{2,1,0:T(8,128)}, u32[]{:S(2)}) copy-start(f32[32,32,32]{2,1,0:T(8,128)} %param.12) | copy-start | bytes 393220
  1.8 20.1 %collective-permute-start = (bf16[32,1536]{1,0:T(8,128)(2,1)S(1)}, bf16[32,1536]{1,0:T(8,128)(2,1)S(1)}, u32[]{:S(2)}, u32[]{:S(2)}) collective-permute-start(bf16[32,1536]{1,0:T(8,128)(2,1)S(1)} %constant_dynamic-update-slice_fusion), channel_id=1, source_target_pairs={{0,0},{1,1},{2,16},{3,17},{4,32},{5,33},{6,48},{7,49},{8,64},{9,65... | collective-permute-start | bytes 294920 | tf_op jit(solution)/shard_map/ppermute | solution.py:225
  22.5 4.7 %copy-start.5 = (s32[2,64]{1,0:T(2,128)S(1)}, s32[2,64]{1,0:T(2,128)}, u32[]{:S(2)}) copy-start(s32[2,64]{1,0:T(2,128)} %param.16) | copy-start | bytes 1540
  22.5 4.8 %copy-start.4 = (s32[4096]{0:T(1024)S(1)}, s32[4096]{0:T(1024)}, u32[]{:S(2)}) copy-start(s32[4096]{0:T(1024)} %param.13) | copy-start | bytes 49156
  22.6 5.2 %copy-start.1 = (f32[64,32,32]{0,2,1:T(8,128)S(1)}, f32[64,32,32]{0,2,1:T(8,128)}, u32[]{:S(2)}) copy-start(f32[64,32,32]{0,2,1:T(8,128)} %param.17) | copy-start | bytes 786436
  23.5 15.9 %all-to-all-start.1 = ((bf16[16,8,2688]{2,1,0:T(8,128)(2,1)}), bf16[16,8,2688]{2,1,0:T(8,128)(2,1)S(1)}, u32[]{:S(2)}, u32[]{:S(2)}) async-start(bf16[16,8,2688]{2,1,0:T(8,128)(2,1)} %pad_maximum_fusion), calls=%async_computation.1 | async-start | bytes 1376256 | tf_op jit(solution)/shard_map/all_to_all | solution.py:258
  42.0 24.6 %all-to-all-start.2 = ((f32[8,128,128]{2,1,0:T(8,128)}), f32[8,128,128]{2,1,0:T(8,128)S(1)}, u32[]{:S(2)}, u32[]{:S(2)}) async-start(f32[8,128,128]{2,1,0:T(8,128)} %bitcast.14), calls=%async_computation.2 | async-start | bytes 1048576 | tf_op jit(solution)/shard_map/all_to_all | solution.py:271
  66.5 15.2 %copy-start.3 = (f32[32,32,32]{2,1,0:T(8,128)S(1)}, f32[32,32,32]{2,1,0:T(8,128)}, u32[]{:S(2)}) copy-start(f32[32,32,32]{2,1,0:T(8,128)} %param.12) | copy-start | bytes 393220
  67.4 14.2 %all-to-all-start.3 = ((f32[16,8,896]{2,1,0:T(8,128)}), f32[16,8,896]{2,1,0:T(8,128)S(1)}, u32[]{:S(2)}, u32[]{:S(2)}) async-start(f32[16,8,896]{2,1,0:T(8,128)} %maximum_bitcast_fusion), calls=%async_computation.3 | async-start | bytes 917504 | tf_op jit(solution)/shard_map/all_to_all | solution.py:275
  71.1 14.3 %collective-permute-start.1 = (f32[32,768]{1,0:T(8,128)S(1)}, f32[32,768]{1,0:T(8,128)S(1)}, u32[]{:S(2)}, u32[]{:S(2)}) collective-permute-start(f32[32,768]{1,0:T(8,128)S(1)} %get-tuple-element.14), channel_id=1, source_target_pairs={{0,0},{1,1},{2,16},{3,17},{4,32},{5,33},{6,48},{7,49},{8,64},{9,65... | collective-permute-start | bytes 294920 | tf_op jit(solution)/shard_map/ppermute | solution.py:274

commit v6 on v5

--- a/solution.py
+++ b/solution.py
@@ -198,12 +198,124 @@
     out[...] = both[:, :128] + both[:, 128:]
 
 
+def own_lanes(own, rank):
+    shape = (own, own * rank)
+    return lax.broadcasted_iota(jnp.int32, shape, 1) // rank == lax.broadcasted_iota(jnp.int32, shape, 0)
+
+
+def start_kernel(
+    count, pairs, density, coords, basis_hbm, transfer_hbm, data, message, clouds, basis, transfer, sems
+):
+    sources = (density, coords, basis_hbm, transfer_hbm)
+    targets = (clouds.at[:3], clouds.at[3:], basis, transfer)
+    copies = [pltpu.make_async_copy(a, b, sems.at[k]) for k, (a, b) in enumerate(zip(sources, targets))]
+    for copy in copies:
+        copy.start()
+    own, rank = density.shape[1], transfer.shape[1]
+    mine = own_lanes(own, rank)
+    across = (((1,), (1,)), ((), ()))
+    copies[0].wait()
+    copies[1].wait()
+    flat = jnp.concatenate([clouds[i] for i in range(3)], axis=1)
+    data[...] = jnp.concatenate([flat] + [clouds[i] for i in range(3, 6)], axis=1)
+    copies[2].wait()
+    every = jnp.where(mine, lax.dot_general(flat, basis[...], across, preferred_element_type=f32), 0.0)
+    folded = sum(every[:, k : k + 128] for k in range(0, own * rank, 128))
+    moments = sum(folded[:, k : k + rank] for k in range(0, 128, rank))
+    copies[3].wait()
+    lifted = lax.dot_general(
+        moments, transfer[...], across, precision=lax.Precision.HIGHEST, preferred_element_type=f32
+    )
+    lifted = jnp.sum(jnp.where(mine, lifted, 0.0), axis=0, keepdims=True)
+    ids = lax.rem(pairs[...], own)
+    live = lax.broadcasted_iota(jnp.int32, ids.shape, 1) < count[0]
+    rows = [lifted[:, k : k + 128] for k in range(0, own * rank, 128)]
+    block = jnp.concatenate(rows + [jnp.where(live, ids, -1).astype(f32)], axis=0)
+    for k in range(message.shape[0]):
+        message[k] = block
+
+
+def start(near_count, near_pairs, density, coords, basis, transfer, rows):
+    own, rank, width = basis.shape
+    panels = width // 3
+    vmem, hbm = pl.BlockSpec(memory_space=pltpu.VMEM), pl.BlockSpec(memory_space=pltpu.HBM)
+    return pl.pallas_call(
+        start_kernel,
+        out_shape=[
+            jax.ShapeDtypeStruct((own, 2 * width), density.dtype),
+            jax.ShapeDtypeStruct((rows, own * rank // 128 + 2, near_pairs.shape[1]), f32),
+        ],
+        in_specs=[pl.BlockSpec(memory_space=pltpu.SMEM), vmem] + [hbm] * 4,
+        out_specs=[vmem] * 2,
+        scratch_shapes=[
+            pltpu.VMEM((6, own, panels), density.dtype),
+            pltpu.VMEM((own * rank, width), basis.dtype),
+            pltpu.VMEM((own * rank, rank), f32),
+            pltpu.SemaphoreType.DMA((4,)),
+        ],
+        compiler_params=pltpu.CompilerParams(vmem_limit_bytes=60 << 20),
+    )(
+        near_count,
+        near_pairs,
+        density.transpose(1, 0, 2),
+        coords.transpose(1, 0, 2),
+        basis.reshape(own * rank, width),
+        transfer.reshape(own * rank, rank),
+    )
+
+
+def end_kernel(back, returned, near_first, basis, transfer, out, velocity, sems):
+    own, panels = velocity.shape[1:]
+    rank = transfer.shape[1]
+    mine = own_lanes(own, rank)
+    lift_rows = own * rank // 128
+    local = sum(returned[k : k + lift_rows, 3 * panels :] for k in range(0, returned.shape[0], lift_rows))
+    local = jnp.concatenate([local[k : k + 1] for k in range(lift_rows)], axis=1)
+    coef = jnp.dot(
+        jnp.where(mine, local, 0.0), transfer[...], precision=lax.Precision.HIGHEST, preferred_element_type=f32
+    )
+    coef = pieces(jnp.where(mine, jnp.concatenate([coef] * own, axis=1), 0.0), 3)
+    coef = jnp.concatenate(coef, axis=0).astype(bf16)
+    slot = lax.broadcasted_iota(jnp.int32, (own, back.shape[1]), 0).astype(f32)
+    chosen = (back[...] == slot).astype(f32).astype(bf16)
+    copies = []
+    for i in range(3):
+        lanes = slice(i * panels, (i + 1) * panels)
+        far = jnp.dot(coef, basis[:, lanes], preferred_element_type=f32)
+        total = far[:own] + far[own : 2 * own] + far[2 * own :]
+        for piece in pieces(returned[:, lanes], 3):
+            total += jnp.dot(chosen, piece.astype(bf16), preferred_element_type=f32)
+        velocity[i] = near_first[:, lanes] + total
+        copies.append(pltpu.make_async_copy(velocity.at[i], out.at[i], sems.at[i]))
+        copies[-1].start()
+    for copy in copies:
+        copy.wait()
+
+
+def end(back, returned, near_first, basis, transfer):
+    own, rank, width = basis.shape
+    shape = (3, own, width // 3)
+    return pl.pallas_call(
+        end_kernel,
+        out_shape=jax.ShapeDtypeStruct(shape, f32),
+        in_specs=[pl.BlockSpec(memory_space=pltpu.VMEM)] * 5,
+        out_specs=pl.BlockSpec(memory_space=pltpu.HBM),
+        scratch_shapes=[pltpu.VMEM(shape, f32), pltpu.SemaphoreType.DMA((3,))],
+        compiler_params=pltpu.CompilerParams(vmem_limit_bytes=8 << 20),
+    )(
+        back[None],
+        returned,
+        near_first,
+        basis.reshape(own * rank, width),
+        transfer.reshape(own * rank, rank),
+    ).transpose(1, 0, 2)
+
+
 def one_hot(ids, count):
     return (ids[:, None] == jnp.arange(count, dtype=ids.dtype)[None, :]).astype(f32)
 
 
 def shards(density, coords, basis, transfer, parent, near_pairs, near_count, far_pairs, coupling):
-    highest = lax.Precision.HIGHEST
     own, _, panels = density.shape
     rank = basis.shape[1]
     rows, cols = lax.axis_size("row"), lax.axis_size("col")
@@ -212,6 +324,7 @@
     slots = near_pairs.shape[1]
     per_pair = slots // cols
     block = slots // rows
+    lift_rows = own * rank // 128
     vmem = pl.BlockSpec(memory_space=pltpu.VMEM)
 
     swap = [
@@ -220,28 +333,13 @@
         for p in range(rows)
         for h in range(half)
     ]
-    flat = density.reshape(own, 3 * panels)
-    data = jnp.concatenate([flat, coords.reshape(own, 3 * panels)], axis=1)
+    data, message = start(near_count, near_pairs, density, coords, basis, transfer, rows)
+    from_row = lax.all_to_all(message, "row", 0, 0, tiled=True)
+    data, from_row = lax.optimization_barrier((data, from_row))
     first_data = lax.ppermute(data, BOTH, swap)
 
-    moments = jnp.einsum("crk,ck->cr", basis, flat, preferred_element_type=f32)
-    lifted = jnp.einsum("crs,cs->cr", transfer, moments, precision=highest).reshape(-1, 128)
-    lift_rows = lifted.shape[0]
-    live = jnp.arange(slots) < near_count[0]
-    ids = jnp.where(live[None], near_pairs % own, -1).astype(f32)
-    ids = ids.reshape(2, rows, block).transpose(1, 0, 2).reshape(rows, 1, 2 * block)
-    message = jnp.concatenate(
-        [
-            jnp.broadcast_to(lifted[None], (rows, lift_rows, 128)),
-            jnp.pad(ids, ((0, 0), (0, 0), (0, 128 - 2 * block))),
-        ],
-        axis=1,
-    )
-    from_row = lax.all_to_all(message, "row", 0, 0, tiled=True)
-    first_data, from_row = lax.optimization_barrier((first_data, from_row))
-
-    own_first = from_row[:, lift_rows, :block].reshape(-1)
-    own_second = from_row[:, lift_rows, block : 2 * block].reshape(-1)
+    ids = lax.dynamic_slice_in_dim(from_row[:, lift_rows:, :], my_row * block, block, 2)
+    own_first, own_second = ids[:, 0].reshape(-1), ids[:, 1].reshape(-1)
     place = jnp.arange(slots)
     same_owner = (place // block == my_row) & (half * my_row + place % block // per_pair == my_col)
     back_ids = jnp.where(same_owner & (own_first == own_second), -1.0, own_second)
@@ -257,6 +355,7 @@
     )
     second = lax.all_to_all(message, "col", 0, 0, tiled=True)
     ids_lane = 6 * panels
+    first_data, second = lax.optimization_barrier((first_data, second))
 
     factors = jnp.concatenate([coupling.transpose(1, 2, 0), coupling.transpose(2, 1, 0)], axis=2)
     partial = pl.pallas_call(
@@ -275,13 +374,7 @@
     returned = lax.all_to_all(
         jnp.concatenate([to_second, row_locals.sum(axis=0)], axis=1), "col", 0, 0, tiled=True
     )
-    near_second = jnp.einsum(
-        "sc,sk->ck", one_hot(back_ids, own), returned[:, : 3 * panels], precision=highest
-    )
-    parent_locals = returned[:, 3 * panels :].reshape(cols, lift_rows, 128).sum(axis=0).reshape(own, rank)
-    local_coef = jnp.einsum("csr,cs->cr", transfer, parent_locals, precision=highest)
-    far_part = jnp.einsum("crk,cr->ck", basis.astype(f32), local_coef, precision=highest)
-    return (near_first + (near_second + far_part)).reshape(own, 3, panels)
+    return end(back_ids, returned, near_first, basis, transfer)
 
 
 def solution(mesh):

time: 87 us -> 89.7 us (1.031)
  starting transfers between devices: 29.9 us -> 41.8 us
  blocking collectives: 7.33 us -> 0 us
  Pallas kernels: 20.1 us -> 25.7 us
  local copies, waits for them, and re-layouts: 5.07 us -> 2.66 us
  matrix products: 3.35 us -> 1.19 us
  other arithmetic: 3.71 us -> 1.95 us
  waiting for transfers between devices: 16.1 us -> 14.9 us
    all_to_all x1, waiting for transfers between devices: 10 us -> 0.01 us  [shards(): second = lax.all_to_all(message, 'col', 0, 0, tiled=True)]
    all_to_all x1 -> x0, blocking collectives: 7.33 us -> none  [shards(): from_row = lax.all_to_all(message, 'row', 0, 0, tiled=True)]
    pallas_call x0 -> x2, Pallas kernels: none -> 5.58 us  [the longest x1 4.06 us: start(): pl.pallas_call(start_kernel, out_shape=[jax.ShapeDtypeStruct((own, 2 * wi...]
    all_to_all x0 -> x1, starting transfers between devices: none -> 5.1 us  [shards(): from_row = lax.all_to_all(message, 'row', 0, 0, tiled=True)]
    ppermute x1, waiting for transfers between devices: 2.38 us -> 7.19 us  [shards(): near_first = lax.ppermute(near_first, BOTH, swap)]
    ppermute x1, waiting for transfers between devices: 0.01 us -> 4.6 us  [shards(): first_data = lax.ppermute(data, BOTH, swap)]
    all_to_all x1, starting transfers between devices: 3.6 us -> 7.9 us  [shards(): second = lax.all_to_all(message, 'col', 0, 0, tiled=True)]
    all_to_all x1, waiting for transfers between devices: 3.65 us -> 0.01 us  [shards(): lax.all_to_all(jnp.concatenate([to_second, row_locals.sum(axis=0)], axis=...]
  transfers between devices with their start and end apart: 5 -> 6, of which waited for: 3 -> 3; matrix products, arithmetic and copies ran while one was open for 8% -> 1% of each run, Pallas kernels for 20% -> 20%
where the time goes in v6:
time: 89.7 us; the launch traced here: 89.1 us
  starting transfers between devices  41.8 us (47%)
  Pallas kernels  25.7 us (29%)
  waiting for transfers between devices  14.9 us (17%)
  local copies, waits for them, and re-layouts  2.66 us (3%)
  other arithmetic  1.95 us (2%)
  matrix products  1.19 us (1%)
    pallas_call x1, Pallas kernels, near_sums(): pl.pallas_call(functools.partial(near_kernel, ids_lane), out_shape=[jax.S...  17.5 us
    ppermute x1, starting transfers between devices, shards(): first_data = lax.ppermute(data, BOTH, swap)  9.62 us
    all_to_all x1, starting transfers between devices, shards(): second = lax.all_to_all(message, 'col', 0, 0, tiled=True)  7.9 us
    ppermute x1, starting transfers between devices, shards(): near_first = lax.ppermute(near_first, BOTH, swap)  7.2 us
    ppermute x1, waiting for transfers between devices, shards(): near_first = lax.ppermute(near_first, BOTH, swap)  7.19 us
    all_to_all x1, starting transfers between devices, shards(): lax.all_to_all(partial.reshape(rows, slots, 128), 'row', 0, 0, tiled=True)  6.12 us
    all_to_all x1, starting transfers between devices, shards(): lax.all_to_all(jnp.concatenate([to_second, row_locals.sum(axis=0)], axis=...  5.88 us
    all_to_all x1, starting transfers between devices, shards(): from_row = lax.all_to_all(message, 'row', 0, 0, tiled=True)  5.1 us
  transfers between devices with their start and end apart: 6, of which 3 were waited for; matrix products, arithmetic and copies ran while one was open for 1% of the time, Pallas kernels for 20%

profile of v6, /device:TPU:7, one launch (start us, length us, event | category | flops | bytes accessed | tf_op | source)
XLA Modules:
  0.0 89.1 jit_solution(5510817501550618085)
XLA Ops:
  0.7 4.1 %shard_map.91 = (bf16[32,1536]{1,0:T(8,128)(2,1)}, f32[8,10,128]{2,1,0:T(8,128)}) custom-call(s32[1]{0:T(128)S(6)} %copy.14.count, s32[2,128]{1,0:T(2,128)} %pairs.1, bf16[3,32,256]{2,1,0:T(8,128)(2,1)} %bitcast.31, bf16[3,32,256]{2,1,0:T(8,128)(2,1)} %bitcast.32, bf16[1024,768]{1,0:T(8,128)(2,1)} %bitcast.22, f32[1024,32]{1,0:T(8,128)} %bitcast.26), custom_call_target="tpu_custom_call" | custom-call | tf_op jit(solution)/shard_map/pallas_call | solution.py:242
  4.7 5.1 %all-to-all-start = ((f32[8,10,128]{2,1,0:T(8,128)}), f32[8,10,128]{2,1,0:T(8,128)S(1)}, u32[]{:S(2)}, u32[]{:S(2)}) async-start(f32[8,10,128]{2,1,0:T(8,128)} %get-tuple-element.16), calls=%async_computation | async-start | bytes 131072 | tf_op jit(solution)/shard_map/all_to_all | solution.py:337
  9.8 3.1 %all-to-all-done = f32[8,10,128]{2,1,0:T(8,128)S(1)} async-done(((f32[8,10,128]{2,1,0:T(8,128)}), f32[8,10,128]{2,1,0:T(8,128)S(1)}, u32[]{:S(2)}, u32[]{:S(2)}) %all-to-all-start) | async-done | bytes 40992 | tf_op jit(solution)/shard_map/all_to_all | solution.py:337
  13.0 0.1 convert_reduce_fusion
  13.1 0.1 convert_element_type.22
  13.2 0.5 broadcast.160
  13.7 0.7 fusion.3
  14.3 0.1 eq.58
  14.4 1.2 %fusion = bf16[16,8,1536]{2,1,0:T(8,128)(2,1)S(1)} fusion(bf16[32,1536]{1,0:T(8,128)(2,1)} %get-tuple-element.18, f32[128]{0:T(128)S(1)} %eq.58), kind=kOutput, calls=%fused_computation.1 | convolution fusion | flops 12791808 | bytes 492032 | tf_op jit(solution)/shard_map/dot_general | solution.py:346
  15.6 0.1 broadcast_in_dim.12
  15.7 0.0 copy-start.5
  15.7 0.0 copy-start.4
  15.7 0.0 copy-start.2
  15.8 0.9 %pad_maximum_fusion = bf16[16,8,2688]{2,1,0:T(8,128)(2,1)} fusion(bf16[16,8,1024]{2,1,0:T(8,128)(2,1)S(1)} %tile.9, bf16[16,8,128]{2,1,0:T(8,128)(2,1)S(1)} %broadcast_in_dim.12, bf16[16,8,1536]{2,1,0:T(8,128)(2,1)S(1)} %fusion), kind=kLoop, calls=%fused_computation.2 | loop fusion | flops 2064384 | bytes 1376256 | tf_op jit(solution)/shard_map/concatenate | solution.py:348
  16.7 0.0 copy-start.3
  16.7 7.9 %all-to-all-start.1 = ((bf16[16,8,2688]{2,1,0:T(8,128)(2,1)}), bf16[16,8,2688]{2,1,0:T(8,128)(2,1)S(1)}, u32[]{:S(2)}, u32[]{:S(2)}) async-start(bf16[16,8,2688]{2,1,0:T(8,128)(2,1)} %pad_maximum_fusion), calls=%async_computation.1 | async-start | bytes 1376256 | tf_op jit(solution)/shard_map/all_to_all | solution.py:356
  24.6 0.0 copy-done.5
  24.6 0.1 reshape.175.ends
  24.7 0.0 copy-done.4
  24.7 0.5 reshape.174.parents
  25.2 0.0 copy-done.2
  25.2 0.3 copy.13
  25.6 0.0 copy-done.3
  25.6 9.6 %collective-permute-start = (bf16[32,1536]{1,0:T(8,128)(2,1)S(1)}, bf16[32,1536]{1,0:T(8,128)(2,1)S(1)}, u32[]{:S(2)}, u32[]{:S(2)}) collective-permute-start(bf16[32,1536]{1,0:T(8,128)(2,1)S(1)} %copy-done.3), channel_id=1, source_target_pairs={{0,0},{1,1},{2,16},{3,17},{4,32},{5,33},{6,48},{7,49},{8,64},{9,65... | collective-permute-start | bytes 294920 | tf_op jit(solution)/shard_map/ppermute | solution.py:339
  35.2 0.2 pad_maximum_fusion.1.factors
  35.4 4.6 %collective-permute-done.first_ref = bf16[32,1536]{1,0:T(8,128)(2,1)S(1)} collective-permute-done((bf16[32,1536]{1,0:T(8,128)(2,1)S(1)}, bf16[32,1536]{1,0:T(8,128)(2,1)S(1)}, u32[]{:S(2)}, u32[]{:S(2)}) %collective-permute-start) | collective-permute-done | bytes 98336 | tf_op jit(solution)/shard_map/ppermute | solution.py:339
  40.0 0.0 all-to-all-done.1
  40.0 2.6 %shard_map.92 = f32[1024,128]{1,0:T(8,128)} custom-call(bf16[128,2688]{1,0:T(8,128)(2,1)S(1)} %bitcast.24, s32[1024,4]{1,0:T(8,128)S(1)} %reshape.174.parents, s32[1,128]{1,0:T(1,128)S(1)} %reshape.175.ends, f32[32,32,128]{2,1,0:T(8,128)S(1)} %pad_maximum_fusion.1.factors), custom_call_target="tpu_custom_call" | custom-call | tf_op jit(solution)/shard_map/pallas_call | solution.py:361
  42.6 6.1 %all-to-all-start.2 = ((f32[8,128,128]{2,1,0:T(8,128)}), f32[8,128,128]{2,1,0:T(8,128)S(1)}, u32[]{:S(2)}, u32[]{:S(2)}) async-start(f32[8,128,128]{2,1,0:T(8,128)} %bitcast.10), calls=%async_computation.2 | async-start | bytes 1048576 | tf_op jit(solution)/shard_map/all_to_all | solution.py:370
  48.7 17.5 %shard_map.93 = (f32[32,768]{1,0:T(8,128)S(1)}, f32[128,768]{1,0:T(8,128)S(1)}) custom-call(bf16[32,1536]{1,0:T(8,128)(2,1)S(1)} %collective-permute-done.first_ref, bf16[128,2688]{1,0:T(8,128)(2,1)S(1)} %bitcast.25), custom_call_target="tpu_custom_call" | custom-call | flops 2147483648 | bytes 1179648 | tf_op jit(solution)/shard_map/pallas_call | solution.py:152
  66.2 0.0 copy-start
  66.2 0.0 copy-start.1
  66.2 0.0 all-to-all-done.2
  66.3 0.8 maximum_bitcast_fusion
  67.1 5.9 %all-to-all-start.3 = ((f32[16,8,896]{2,1,0:T(8,128)}), f32[16,8,896]{2,1,0:T(8,128)S(1)}, u32[]{:S(2)}, u32[]{:S(2)}) async-start(f32[16,8,896]{2,1,0:T(8,128)} %maximum_bitcast_fusion), calls=%async_computation.3 | async-start | bytes 917504 | tf_op jit(solution)/shard_map/all_to_all | solution.py:374
  72.9 0.1 reshape_squeeze.7
  73.0 0.1 reshape_squeeze.6
  73.1 7.2 %collective-permute-start.1 = (f32[32,768]{1,0:T(8,128)S(1)}, f32[32,768]{1,0:T(8,128)S(1)}, u32[]{:S(2)}, u32[]{:S(2)}) collective-permute-start(f32[32,768]{1,0:T(8,128)S(1)} %get-tuple-element.24), channel_id=1, source_target_pairs={{0,0},{1,1},{2,16},{3,17},{4,32},{5,33},{6,48},{7,49},{8,64},{9,65... | collective-permute-start | bytes 294920 | tf_op jit(solution)/shard_map/ppermute | solution.py:373
  80.3 7.2 %collective-permute-done.1.near_first = f32[32,768]{1,0:T(8,128)S(1)} collective-permute-done((f32[32,768]{1,0:T(8,128)S(1)}, f32[32,768]{1,0:T(8,128)S(1)}, u32[]{:S(2)}, u32[]{:S(2)}) %collective-permute-start.1) | collective-permute-done | bytes 98336 | tf_op jit(solution)/shard_map/ppermute | solution.py:373
  87.5 0.0 all-to-all-done.3
  87.5 0.0 copy-done
  87.5 0.0 copy-done.1
  87.5 1.5 %shard_map.94 = f32[3,32,256]{2,1,0:T(8,128)} custom-call(f32[1,128]{1,0:T(1,128)S(1)} %and_select_fusion.back, f32[128,896]{1,0:T(8,128)S(1)} %bitcast.28, f32[32,768]{1,0:T(8,128)S(1)} %collective-permute-done.1.near_first, bf16[1024,768]{1,0:T(8,128)(2,1)S(1)} %bitcast.23, f32[1024,32]{1,0:T(8,128)S(1)} %bitcast.27), custom_call_target="tpu_custom_call" | custom-call | tf_op jit(solution)/shard_map/pallas_call | solution.py:298
  (6 shorter events, 0.1 us)
Async XLA Ops:
  4.7 8.2 %all-to-all-start = ((f32[8,10,128]{2,1,0:T(8,128)}), f32[8,10,128]{2,1,0:T(8,128)S(1)}, u32[]{:S(2)}, u32[]{:S(2)}) async-start(f32[8,10,128]{2,1,0:T(8,128)} %get-tuple-element.16), calls=%async_computation | async-start | bytes 131072 | tf_op jit(solution)/shard_map/all_to_all | solution.py:337
  15.7 8.8 %copy-start.5 = (s32[2,64]{1,0:T(2,128)S(1)}, s32[2,64]{1,0:T(2,128)}, u32[]{:S(2)}) copy-start(s32[2,64]{1,0:T(2,128)} %param.16) | copy-start | bytes 1540
  15.7 9.0 %copy-start.4 = (s32[4096]{0:T(1024)S(1)}, s32[4096]{0:T(1024)}, u32[]{:S(2)}) copy-start(s32[4096]{0:T(1024)} %param.13) | copy-start | bytes 49156
  15.7 9.5 %copy-start.2 = (f32[64,32,32]{0,2,1:T(8,128)S(1)}, f32[64,32,32]{0,2,1:T(8,128)}, u32[]{:S(2)}) copy-start(f32[64,32,32]{0,2,1:T(8,128)} %param.17) | copy-start | bytes 786436
  16.7 8.9 %copy-start.3 = (bf16[32,1536]{1,0:T(8,128)(2,1)S(1)}, bf16[32,1536]{1,0:T(8,128)(2,1)}, u32[]{:S(2)}) copy-start(bf16[32,1536]{1,0:T(8,128)(2,1)} %get-tuple-element.18) | copy-start | bytes 294916
  16.7 23.3 %all-to-all-start.1 = ((bf16[16,8,2688]{2,1,0:T(8,128)(2,1)}), bf16[16,8,2688]{2,1,0:T(8,128)(2,1)S(1)}, u32[]{:S(2)}, u32[]{:S(2)}) async-start(bf16[16,8,2688]{2,1,0:T(8,128)(2,1)} %pad_maximum_fusion), calls=%async_computation.1 | async-start | bytes 1376256 | tf_op jit(solution)/shard_map/all_to_all | solution.py:356
  25.6 14.4 %collective-permute-start = (bf16[32,1536]{1,0:T(8,128)(2,1)S(1)}, bf16[32,1536]{1,0:T(8,128)(2,1)S(1)}, u32[]{:S(2)}, u32[]{:S(2)}) collective-permute-start(bf16[32,1536]{1,0:T(8,128)(2,1)S(1)} %copy-done.3), channel_id=1, source_target_pairs={{0,0},{1,1},{2,16},{3,17},{4,32},{5,33},{6,48},{7,49},{8,64},{9,65... | collective-permute-start | bytes 294920 | tf_op jit(solution)/shard_map/ppermute | solution.py:339
  42.6 23.7 %all-to-all-start.2 = ((f32[8,128,128]{2,1,0:T(8,128)}), f32[8,128,128]{2,1,0:T(8,128)S(1)}, u32[]{:S(2)}, u32[]{:S(2)}) async-start(f32[8,128,128]{2,1,0:T(8,128)} %bitcast.10), calls=%async_computation.2 | async-start | bytes 1048576 | tf_op jit(solution)/shard_map/all_to_all | solution.py:370
  66.2 21.3 %copy-start = (bf16[32,32,768]{2,1,0:T(8,128)(2,1)S(1)}, bf16[32,32,768]{2,1,0:T(8,128)(2,1)}, u32[]{:S(2)}) copy-start(bf16[32,32,768]{2,1,0:T(8,128)(2,1)} %param.11) | copy-start | bytes 4718596
  66.2 21.3 %copy-start.1 = (f32[32,32,32]{2,1,0:T(8,128)S(1)}, f32[32,32,32]{2,1,0:T(8,128)}, u32[]{:S(2)}) copy-start(f32[32,32,32]{2,1,0:T(8,128)} %param.12) | copy-start | bytes 393220
  67.1 20.5 %all-to-all-start.3 = ((f32[16,8,896]{2,1,0:T(8,128)}), f32[16,8,896]{2,1,0:T(8,128)S(1)}, u32[]{:S(2)}, u32[]{:S(2)}) async-start(f32[16,8,896]{2,1,0:T(8,128)} %maximum_bitcast_fusion), calls=%async_computation.3 | async-start | bytes 917504 | tf_op jit(solution)/shard_map/all_to_all | solution.py:374
  73.1 14.4 %collective-permute-start.1 = (f32[32,768]{1,0:T(8,128)S(1)}, f32[32,768]{1,0:T(8,128)S(1)}, u32[]{:S(2)}, u32[]{:S(2)}) collective-permute-start(f32[32,768]{1,0:T(8,128)S(1)} %get-tuple-element.24), channel_id=1, source_target_pairs={{0,0},{1,1},{2,16},{3,17},{4,32},{5,33},{6,48},{7,49},{8,64},{9,65... | collective-permute-start | bytes 294920 | tf_op jit(solution)/shard_map/ppermute | solution.py:373

commit v7 on v6

--- a/solution.py
+++ b/solution.py
@@ -203,62 +203,75 @@
     return lax.broadcasted_iota(jnp.int32, shape, 1) // rank == lax.broadcasted_iota(jnp.int32, shape, 0)
 
 
-def start_kernel(
-    count, pairs, density, coords, basis_hbm, transfer_hbm, data, message, clouds, basis, transfer, sems
-):
-    sources = (density, coords, basis_hbm, transfer_hbm)
-    targets = (clouds.at[:3], clouds.at[3:], basis, transfer)
+def join_kernel(density, coords, data):
+    panels = density.shape[2]
+    for k in range(3):
+        data[:, k * panels : (k + 1) * panels] = density[k]
+        data[:, (3 + k) * panels : (4 + k) * panels] = coords[k]
+
+
+def join(density, coords):
+    own, parts, panels = density.shape
+    vmem = pl.BlockSpec(memory_space=pltpu.VMEM)
+    return pl.pallas_call(
+        join_kernel,
+        out_shape=jax.ShapeDtypeStruct((own, 2 * parts * panels), density.dtype),
+        in_specs=[vmem] * 2,
+        out_specs=vmem,
+        compiler_params=pltpu.CompilerParams(vmem_limit_bytes=8 << 20),
+    )(density.transpose(1, 0, 2), coords.transpose(1, 0, 2))
+
+
+def start_kernel(count, pairs, density_hbm, basis_hbm, transfer_hbm, message, density, basis, transfer, sems):
+    sources = (density_hbm, basis_hbm, transfer_hbm)
+    targets = (density, basis, transfer)
     copies = [pltpu.make_async_copy(a, b, sems.at[k]) for k, (a, b) in enumerate(zip(sources, targets))]
     for copy in copies:
         copy.start()
     own, rank = density.shape[1], transfer.shape[1]
     mine = own_lanes(own, rank)
     across = (((1,), (1,)), ((), ()))
+    ids = lax.rem(pairs[...], own)
+    live = lax.broadcasted_iota(jnp.int32, ids.shape, 1) < count[0]
+    ids = jnp.where(live, ids, -1).astype(f32)
     copies[0].wait()
+    flat = jnp.concatenate([density[i] for i in range(3)], axis=1)
     copies[1].wait()
-    flat = jnp.concatenate([clouds[i] for i in range(3)], axis=1)
-    data[...] = jnp.concatenate([flat] + [clouds[i] for i in range(3, 6)], axis=1)
-    copies[2].wait()
     every = jnp.where(mine, lax.dot_general(flat, basis[...], across, preferred_element_type=f32), 0.0)
     folded = sum(every[:, k : k + 128] for k in range(0, own * rank, 128))
     moments = sum(folded[:, k : k + rank] for k in range(0, 128, rank))
-    copies[3].wait()
+    copies[2].wait()
     lifted = lax.dot_general(
         moments, transfer[...], across, precision=lax.Precision.HIGHEST, preferred_element_type=f32
     )
     lifted = jnp.sum(jnp.where(mine, lifted, 0.0), axis=0, keepdims=True)
-    ids = lax.rem(pairs[...], own)
-    live = lax.broadcasted_iota(jnp.int32, ids.shape, 1) < count[0]
-    rows = [lifted[:, k : k + 128] for k in range(0, own * rank, 128)]
-    block = jnp.concatenate(rows + [jnp.where(live, ids, -1).astype(f32)], axis=0)
-    for k in range(message.shape[0]):
-        message[k] = block
-
-
-def start(near_count, near_pairs, density, coords, basis, transfer, rows):
+    lifted = jnp.concatenate([lifted[:, k : k + 128] for k in range(0, own * rank, 128)], axis=0)
+    rows = message.shape[0]
+    block = ids.shape[1] // rows
+    for k in range(rows):
+        turned = jnp.concatenate([ids[:, k * block :], ids[:, : k * block]], axis=1) if k else ids
+        message[k] = jnp.concatenate([lifted, turned], axis=0)
+
+
+def start(near_count, near_pairs, density, basis, transfer, rows):
     own, rank, width = basis.shape
-    panels = width // 3
     vmem, hbm = pl.BlockSpec(memory_space=pltpu.VMEM), pl.BlockSpec(memory_space=pltpu.HBM)
     return pl.pallas_call(
         start_kernel,
-        out_shape=[
-            jax.ShapeDtypeStruct((own, 2 * width), density.dtype),
-            jax.ShapeDtypeStruct((rows, own * rank // 128 + 2, near_pairs.shape[1]), f32),
-        ],
-        in_specs=[pl.BlockSpec(memory_space=pltpu.SMEM), vmem] + [hbm] * 4,
-        out_specs=[vmem] * 2,
+        out_shape=jax.ShapeDtypeStruct((rows, own * rank // 128 + 2, near_pairs.shape[1]), f32),
+        in_specs=[pl.BlockSpec(memory_space=pltpu.SMEM), vmem] + [hbm] * 3,
+        out_specs=vmem,
         scratch_shapes=[
-            pltpu.VMEM((6, own, panels), density.dtype),
+            pltpu.VMEM((3, own, width // 3), density.dtype),
             pltpu.VMEM((own * rank, width), basis.dtype),
             pltpu.VMEM((own * rank, rank), f32),
-            pltpu.SemaphoreType.DMA((4,)),
+            pltpu.SemaphoreType.DMA((3,)),
         ],
         compiler_params=pltpu.CompilerParams(vmem_limit_bytes=60 << 20),
     )(
         near_count,
         near_pairs,
         density.transpose(1, 0, 2),
-        coords.transpose(1, 0, 2),
         basis.reshape(own * rank, width),
         transfer.reshape(own * rank, rank),
     )
@@ -333,13 +346,15 @@
         for p in range(rows)
         for h in range(half)
     ]
-    data, message = start(near_count, near_pairs, density, coords, basis, transfer, rows)
+    message = start(near_count, near_pairs, density, basis, transfer, rows)
+    density, coords, message = lax.optimization_barrier((density, coords, message))
     from_row = lax.all_to_all(message, "row", 0, 0, tiled=True)
-    data, from_row = lax.optimization_barrier((data, from_row))
+    data = join(density, coords)
     first_data = lax.ppermute(data, BOTH, swap)
-
-    ids = lax.dynamic_slice_in_dim(from_row[:, lift_rows:, :], my_row * block, block, 2)
-    own_first, own_second = ids[:, 0].reshape(-1), ids[:, 1].reshape(-1)
+    first_data, from_row = lax.optimization_barrier((first_data, from_row))
+
+    own_first = from_row[:, lift_rows, :block].reshape(-1)
+    own_second = from_row[:, lift_rows + 1, :block].reshape(-1)
     place = jnp.arange(slots)
     same_owner = (place // block == my_row) & (half * my_row + place % block // per_pair == my_col)
     back_ids = jnp.where(same_owner & (own_first == own_second), -1.0, own_second)
@@ -355,7 +370,6 @@
     )
     second = lax.all_to_all(message, "col", 0, 0, tiled=True)
     ids_lane = 6 * panels
-    first_data, second = lax.optimization_barrier((first_data, second))
 
     factors = jnp.concatenate([coupling.transpose(1, 2, 0), coupling.transpose(2, 1, 0)], axis=2)
     partial = pl.pallas_call(

time: 89.7 us -> 86.7 us (0.967)
  starting transfers between devices: 41.8 us -> 29.8 us
  blocking collectives: 0 us -> 7.55 us
  waiting for transfers between devices: 14.9 us -> 18.5 us
  local copies, waits for them, and re-layouts: 2.66 us -> 1.45 us
    all_to_all x1, waiting for transfers between devices: 0.01 us -> 11.1 us  [shards(): second = lax.all_to_all(message, 'col', 0, 0, tiled=True)]
    all_to_all x0 -> x1, blocking collectives: none -> 7.55 us  [shards(): from_row = lax.all_to_all(message, 'row', 0, 0, tiled=True)]
    all_to_all x1 -> x0, starting transfers between devices: 5.1 us -> none  [shards(): from_row = lax.all_to_all(message, 'row', 0, 0, tiled=True)]
    ppermute x1, waiting for transfers between devices: 4.6 us -> 0.01 us  [shards(): first_data = lax.ppermute(data, BOTH, swap)]
    all_to_all x1, starting transfers between devices: 7.9 us -> 3.6 us  [shards(): second = lax.all_to_all(message, 'col', 0, 0, tiled=True)]
    all_to_all x1 -> x0, waiting for transfers between devices: 3.14 us -> none  [shards(): from_row = lax.all_to_all(message, 'row', 0, 0, tiled=True)]
    all_to_all x1, starting transfers between devices: 5.88 us -> 3.56 us  [shards(): lax.all_to_all(jnp.concatenate([to_second, row_locals.sum(axis=0)], axis=...]
    slice x3 -> x1, local copies, waits for them, and re-layouts: 1.16 us -> 0.03 us  [shards(): own_first = from_row[:, lift_rows, :block].reshape(-1)]
  transfers between devices with their start and end apart: 6 -> 5, of which waited for: 3 -> 2; matrix products, arithmetic and copies ran while one was open for 1% -> 2% of each run, Pallas kernels for 20% -> 20%
where the time goes in v7:
time: 86.7 us; the launch traced here: 86.1 us
  starting transfers between devices  29.8 us (34%)
  Pallas kernels  25.7 us (30%)
  waiting for transfers between devices  18.5 us (21%)
  blocking collectives  7.55 us (9%)
  other arithmetic  1.94 us (2%)
  local copies, waits for them, and re-layouts  1.45 us (2%)
  between operations  0.87 us (1%)
    pallas_call x1, Pallas kernels, near_sums(): pl.pallas_call(functools.partial(near_kernel, ids_lane), out_shape=[jax.S...  17.6 us
    all_to_all x1, waiting for transfers between devices, shards(): second = lax.all_to_all(message, 'col', 0, 0, tiled=True)  11.1 us
    ppermute x1, starting transfers between devices, shards(): first_data = lax.ppermute(data, BOTH, swap)  8.77 us
    all_to_all x1, blocking collectives, shards(): from_row = lax.all_to_all(message, 'row', 0, 0, tiled=True)  7.55 us
    ppermute x1, waiting for transfers between devices, shards(): near_first = lax.ppermute(near_first, BOTH, swap)  7.42 us
    all_to_all x1, starting transfers between devices, shards(): lax.all_to_all(partial.reshape(rows, slots, 128), 'row', 0, 0, tiled=True)  7.05 us
    ppermute x1, starting transfers between devices, shards(): near_first = lax.ppermute(near_first, BOTH, swap)  6.85 us
    pallas_call x1, Pallas kernels, start(): pl.pallas_call(start_kernel, out_shape=jax.ShapeDtypeStruct((rows, own *...  4.04 us
  transfers between devices with their start and end apart: 5, of which 2 were waited for; matrix products, arithmetic and copies ran while one was open for 2% of the time, Pallas kernels for 20%

profile of v7, /device:TPU:7, one launch (start us, length us, event | category | flops | bytes accessed | tf_op | source)
XLA Modules:
  0.0 86.1 jit_solution(14694741253187521389)
XLA Ops:
  0.0 0.0 copy-start.2
  0.0 0.0 copy-start.3
  0.7 4.0 %shard_map.91 = f32[8,10,128]{2,1,0:T(8,128)} custom-call(s32[1]{0:T(128)S(6)} %copy.14.count, s32[2,128]{1,0:T(2,128)} %pairs.1, bf16[3,32,256]{2,1,0:T(8,128)(2,1)} %bitcast.30, bf16[1024,768]{1,0:T(8,128)(2,1)} %bitcast.23, f32[1024,32]{1,0:T(8,128)} %bitcast.27), custom_call_target="tpu_custom_call" | custom-call | tf_op jit(solution)/shard_map/pallas_call | solution.py:259
  4.7 0.0 copy-done.2
  4.7 0.0 copy-done.3
  4.7 8.8 %collective-permute-start = (bf16[32,1536]{1,0:T(8,128)(2,1)S(1)}, bf16[32,1536]{1,0:T(8,128)(2,1)S(1)}, u32[]{:S(2)}, u32[]{:S(2)}) collective-permute-start(bf16[32,1536]{1,0:T(8,128)(2,1)S(1)} %shard_map.92), channel_id=1, source_target_pairs={{0,0},{1,1},{2,16},{3,17},{4,32},{5,33},{6,48},{7,49},{8,64},{9,65... | collective-permute-start | bytes 294920 | tf_op jit(solution)/shard_map/ppermute | solution.py:353
  13.5 7.5 %all_to_all.29 = f32[8,10,128]{2,1,0:T(8,128)S(1)} all-to-all(f32[8,10,128]{2,1,0:T(8,128)} %shard_map.91), channel_id=1, replica_groups=mesh['row'=8,'col'=16] {'row'}, dimensions={0} | all-to-all | bytes 81920 | tf_op jit(solution)/shard_map/all_to_all | solution.py:351
  21.1 0.0 collective-permute-done.first_ref
  21.1 0.1 convert_element_type.22
  21.2 0.1 eq.58
  21.3 0.3 fusion
  21.6 0.1 broadcast_in_dim.12
  21.7 0.0 copy-start.6
  21.7 0.0 copy-start.5
  21.8 0.0 copy-start.4
  21.8 0.9 %pad_maximum_fusion = bf16[16,8,2688]{2,1,0:T(8,128)(2,1)} fusion(bf16[16,8,1024]{2,1,0:T(8,128)(2,1)S(1)} %tile.9, bf16[16,8,128]{2,1,0:T(8,128)(2,1)S(1)} %broadcast_in_dim.12, bf16[16,8,1536]{2,1,0:T(8,128)(2,1)S(1)} %fusion), kind=kLoop, calls=%fused_computation.2 | loop fusion | flops 2064384 | bytes 1376256 | tf_op jit(solution)/shard_map/concatenate | solution.py:363
  22.7 3.6 %all-to-all-start.1 = ((bf16[16,8,2688]{2,1,0:T(8,128)(2,1)}), bf16[16,8,2688]{2,1,0:T(8,128)(2,1)S(1)}, u32[]{:S(2)}, u32[]{:S(2)}) async-start(bf16[16,8,2688]{2,1,0:T(8,128)(2,1)} %pad_maximum_fusion), calls=%async_computation.1 | async-start | bytes 1376256 | tf_op jit(solution)/shard_map/all_to_all | solution.py:371
  26.3 0.0 copy-done.6
  26.3 0.1 reshape.175.ends
  26.4 0.0 copy-done.5
  26.4 0.5 reshape.174.parents
  26.9 0.0 copy-done.4
  26.9 0.3 copy.13
  27.3 0.2 pad_maximum_fusion.1.factors
  27.5 11.1 %all-to-all-done.1 = bf16[16,8,2688]{2,1,0:T(8,128)(2,1)S(1)} async-done(((bf16[16,8,2688]{2,1,0:T(8,128)(2,1)}), bf16[16,8,2688]{2,1,0:T(8,128)(2,1)S(1)}, u32[]{:S(2)}, u32[]{:S(2)}) %all-to-all-start.1) | async-done | bytes 688160 | tf_op jit(solution)/shard_map/all_to_all | solution.py:371
  38.6 2.5 %shard_map.93 = f32[1024,128]{1,0:T(8,128)} custom-call(bf16[128,2688]{1,0:T(8,128)(2,1)S(1)} %bitcast.25, s32[1024,4]{1,0:T(8,128)S(1)} %reshape.174.parents, s32[1,128]{1,0:T(1,128)S(1)} %reshape.175.ends, f32[32,32,128]{2,1,0:T(8,128)S(1)} %pad_maximum_fusion.1.factors), custom_call_target="tpu_custom_call" | custom-call | tf_op jit(solution)/shard_map/pallas_call | solution.py:375
  41.1 7.1 %all-to-all-start.2 = ((f32[8,128,128]{2,1,0:T(8,128)}), f32[8,128,128]{2,1,0:T(8,128)S(1)}, u32[]{:S(2)}, u32[]{:S(2)}) async-start(f32[8,128,128]{2,1,0:T(8,128)} %bitcast.11), calls=%async_computation.2 | async-start | bytes 1048576 | tf_op jit(solution)/shard_map/all_to_all | solution.py:384
  48.2 17.6 %shard_map.94 = (f32[32,768]{1,0:T(8,128)S(1)}, f32[128,768]{1,0:T(8,128)S(1)}) custom-call(bf16[32,1536]{1,0:T(8,128)(2,1)S(1)} %collective-permute-done.first_ref, bf16[128,2688]{1,0:T(8,128)(2,1)S(1)} %bitcast.26), custom_call_target="tpu_custom_call" | custom-call | flops 2147483648 | bytes 1179648 | tf_op jit(solution)/shard_map/pallas_call | solution.py:152
  65.7 0.0 copy-start
  65.7 0.0 copy-start.1
  65.7 0.0 all-to-all-done.2
  65.8 0.8 maximum_bitcast_fusion
  66.6 3.6 %all-to-all-start.3 = ((f32[16,8,896]{2,1,0:T(8,128)}), f32[16,8,896]{2,1,0:T(8,128)S(1)}, u32[]{:S(2)}, u32[]{:S(2)}) async-start(f32[16,8,896]{2,1,0:T(8,128)} %maximum_bitcast_fusion), calls=%async_computation.3 | async-start | bytes 917504 | tf_op jit(solution)/shard_map/all_to_all | solution.py:388
  70.1 0.1 reshape_squeeze.6
  70.2 0.1 reshape_squeeze.7
  70.3 6.8 %collective-permute-start.1 = (f32[32,768]{1,0:T(8,128)S(1)}, f32[32,768]{1,0:T(8,128)S(1)}, u32[]{:S(2)}, u32[]{:S(2)}) collective-permute-start(f32[32,768]{1,0:T(8,128)S(1)} %get-tuple-element.22), channel_id=1, source_target_pairs={{0,0},{1,1},{2,16},{3,17},{4,32},{5,33},{6,48},{7,49},{8,64},{9,65... | collective-permute-start | bytes 294920 | tf_op jit(solution)/shard_map/ppermute | solution.py:387
  77.2 7.4 %collective-permute-done.1.near_first = f32[32,768]{1,0:T(8,128)S(1)} collective-permute-done((f32[32,768]{1,0:T(8,128)S(1)}, f32[32,768]{1,0:T(8,128)S(1)}, u32[]{:S(2)}, u32[]{:S(2)}) %collective-permute-start.1) | collective-permute-done | bytes 98336 | tf_op jit(solution)/shard_map/ppermute | solution.py:387
  84.6 0.0 all-to-all-done.3
  84.6 0.0 copy-done
  84.6 0.0 copy-done.1
  84.6 1.5 %shard_map.95 = f32[3,32,256]{2,1,0:T(8,128)} custom-call(f32[1,128]{1,0:T(1,128)S(1)} %and_select_fusion.back, f32[128,896]{1,0:T(8,128)S(1)} %bitcast.29, f32[32,768]{1,0:T(8,128)S(1)} %collective-permute-done.1.near_first, bf16[1024,768]{1,0:T(8,128)(2,1)S(1)} %bitcast.24, f32[1024,32]{1,0:T(8,128)S(1)} %bitcast.28), custom_call_target="tpu_custom_call" | custom-call | tf_op jit(solution)/shard_map/pallas_call | solution.py:311
  (8 shorter events, 0.2 us)
Async XLA Ops:
  0.0 4.7 %copy-start.2 = (bf16[32,3,256]{2,0,1:T(8,128)(2,1)S(1)}, bf16[32,3,256]{2,0,1:T(8,128)(2,1)}, u32[]{:S(2)}) copy-start(bf16[32,3,256]{2,0,1:T(8,128)(2,1)} %param.9) | copy-start | bytes 147460
  0.0 4.7 %copy-start.3 = (bf16[32,3,256]{2,0,1:T(8,128)(2,1)S(1)}, bf16[32,3,256]{2,0,1:T(8,128)(2,1)}, u32[]{:S(2)}) copy-start(bf16[32,3,256]{2,0,1:T(8,128)(2,1)} %param.10) | copy-start | bytes 147460
  4.7 16.3 %collective-permute-start = (bf16[32,1536]{1,0:T(8,128)(2,1)S(1)}, bf16[32,1536]{1,0:T(8,128)(2,1)S(1)}, u32[]{:S(2)}, u32[]{:S(2)}) collective-permute-start(bf16[32,1536]{1,0:T(8,128)(2,1)S(1)} %shard_map.92), channel_id=1, source_target_pairs={{0,0},{1,1},{2,16},{3,17},{4,32},{5,33},{6,48},{7,49},{8,64},{9,65... | collective-permute-start | bytes 294920 | tf_op jit(solution)/shard_map/ppermute | solution.py:353
  21.7 4.5 %copy-start.6 = (s32[2,64]{1,0:T(2,128)S(1)}, s32[2,64]{1,0:T(2,128)}, u32[]{:S(2)}) copy-start(s32[2,64]{1,0:T(2,128)} %param.16) | copy-start | bytes 1540
  21.7 4.7 %copy-start.5 = (s32[4096]{0:T(1024)S(1)}, s32[4096]{0:T(1024)}, u32[]{:S(2)}) copy-start(s32[4096]{0:T(1024)} %param.13) | copy-start | bytes 49156
  21.8 5.2 %copy-start.4 = (f32[64,32,32]{0,2,1:T(8,128)S(1)}, f32[64,32,32]{0,2,1:T(8,128)}, u32[]{:S(2)}) copy-start(f32[64,32,32]{0,2,1:T(8,128)} %param.17) | copy-start | bytes 786436
  22.7 15.9 %all-to-all-start.1 = ((bf16[16,8,2688]{2,1,0:T(8,128)(2,1)}), bf16[16,8,2688]{2,1,0:T(8,128)(2,1)S(1)}, u32[]{:S(2)}, u32[]{:S(2)}) async-start(bf16[16,8,2688]{2,1,0:T(8,128)(2,1)} %pad_maximum_fusion), calls=%async_computation.1 | async-start | bytes 1376256 | tf_op jit(solution)/shard_map/all_to_all | solution.py:371
  41.1 24.6 %all-to-all-start.2 = ((f32[8,128,128]{2,1,0:T(8,128)}), f32[8,128,128]{2,1,0:T(8,128)S(1)}, u32[]{:S(2)}, u32[]{:S(2)}) async-start(f32[8,128,128]{2,1,0:T(8,128)} %bitcast.11), calls=%async_computation.2 | async-start | bytes 1048576 | tf_op jit(solution)/shard_map/all_to_all | solution.py:384
  65.7 18.9 %copy-start = (bf16[32,32,768]{2,1,0:T(8,128)(2,1)S(1)}, bf16[32,32,768]{2,1,0:T(8,128)(2,1)}, u32[]{:S(2)}) copy-start(bf16[32,32,768]{2,1,0:T(8,128)(2,1)} %param.11) | copy-start | bytes 4718596
  65.7 18.9 %copy-start.1 = (f32[32,32,32]{2,1,0:T(8,128)S(1)}, f32[32,32,32]{2,1,0:T(8,128)}, u32[]{:S(2)}) copy-start(f32[32,32,32]{2,1,0:T(8,128)} %param.12) | copy-start | bytes 393220
  66.6 18.0 %all-to-all-start.3 = ((f32[16,8,896]{2,1,0:T(8,128)}), f32[16,8,896]{2,1,0:T(8,128)S(1)}, u32[]{:S(2)}, u32[]{:S(2)}) async-start(f32[16,8,896]{2,1,0:T(8,128)} %maximum_bitcast_fusion), calls=%async_computation.3 | async-start | bytes 917504 | tf_op jit(solution)/shard_map/all_to_all | solution.py:388
  70.3 14.3 %collective-permute-start.1 = (f32[32,768]{1,0:T(8,128)S(1)}, f32[32,768]{1,0:T(8,128)S(1)}, u32[]{:S(2)}, u32[]{:S(2)}) collective-permute-start(f32[32,768]{1,0:T(8,128)S(1)} %get-tuple-element.22), channel_id=1, source_target_pairs={{0,0},{1,1},{2,16},{3,17},{4,32},{5,33},{6,48},{7,49},{8,64},{9,65... | collective-permute-start | bytes 294920 | tf_op jit(solution)/shard_map/ppermute | solution.py:387

commit v8 on v7

--- a/solution.py
+++ b/solution.py
@@ -165,12 +165,16 @@
     )(first, second)
 
 
-def far_kernel(start, recv, parents, ends, factors, out, hits):
-    parts = parents.shape[1]
+def hits_kernel(parents, ends, hits):
     count = ends.shape[1]
+    for m in range(parents.shape[1]):
+        hits[:, m * count : (m + 1) * count] = (parents[:, m : m + 1] == ends[...]).astype(f32).astype(bf16)
+
+
+def far_kernel(start, recv, hits, factors, out):
+    count = factors.shape[2]
+    parts = hits.shape[1] // count
     rank = 128 // parts
-    for m in range(parts):
-        hits[:, m * count : (m + 1) * count] = (parents[:, m : m + 1] == ends[...]).astype(f32).astype(bf16)
     slots = recv.shape[0]
     found = jnp.zeros((128, parts * count), f32)
     for r in range(hits.shape[0] // slots):
@@ -328,6 +332,12 @@
     return (ids[:, None] == jnp.arange(count, dtype=ids.dtype)[None, :]).astype(f32)
 
 
+def seat(p, r, h, rows):
+    hops = rows // 2
+    near = (2 * (p % 2) + h, 2 * (p % 2) + (3 * h - 1))[r % 2] % hops
+    return (r // 2 + hops // 2) % hops * hops + near
+
+
 def shards(density, coords, basis, transfer, parent, near_pairs, near_count, far_pairs, coupling):
     own, _, panels = density.shape
     rank = basis.shape[1]
@@ -341,11 +351,12 @@
     vmem = pl.BlockSpec(memory_space=pltpu.VMEM)
 
     swap = [
-        (r * cols + half * p + h, p * cols + half * r + h)
+        (r * cols + half * p + h, p * cols + seat(p, r, h, rows))
         for r in range(rows)
         for p in range(rows)
         for h in range(half)
     ]
+    home = [(there, here) for here, there in swap]
     message = start(near_count, near_pairs, density, basis, transfer, rows)
     density, coords, message = lax.optimization_barrier((density, coords, message))
     from_row = lax.all_to_all(message, "row", 0, 0, tiled=True)
@@ -353,11 +364,13 @@
     first_data = lax.ppermute(data, BOTH, swap)
     first_data, from_row = lax.optimization_barrier((first_data, from_row))
 
-    own_first = from_row[:, lift_rows, :block].reshape(-1)
-    own_second = from_row[:, lift_rows + 1, :block].reshape(-1)
-    place = jnp.arange(slots)
-    same_owner = (place // block == my_row) & (half * my_row + place % block // per_pair == my_col)
-    back_ids = jnp.where(same_owner & (own_first == own_second), -1.0, own_second)
+    ids = from_row[:, lift_rows:, :block].reshape(rows, 2, half, per_pair)
+    same_owner = (jnp.arange(rows)[:, None] == my_row) & (half * my_row + jnp.arange(half) == my_col)
+    back_ids = jnp.where(same_owner[:, :, None] & (ids[:, 0] == ids[:, 1]), -1.0, ids[:, 1])
+    ids = jnp.concatenate([ids, back_ids[:, None]], axis=1)
+    orders = [sorted((seat(p, r, h, rows), r, h) for r in range(rows) for h in range(half)) for p in range(2)]
+    even, odd = (jnp.stack([ids[r, :, h] for _, r, h in order], axis=1).reshape(3, slots) for order in orders)
+    own_first, own_second, back_ids = jnp.where(my_row % 2 == 0, even, odd)
     picked = jnp.dot(one_hot(own_second, own).astype(bf16), data, preferred_element_type=f32)
     row_lifted = from_row[:, :lift_rows, :].astype(bf16).transpose(1, 0, 2).reshape(lift_rows, -1)
     message = jnp.concatenate(
@@ -372,19 +385,26 @@
     ids_lane = 6 * panels
 
     factors = jnp.concatenate([coupling.transpose(1, 2, 0), coupling.transpose(2, 1, 0)], axis=2)
+    parents, from_row = lax.optimization_barrier((parent.reshape(-1, 128 // rank), from_row))
+    hits = pl.pallas_call(
+        hits_kernel,
+        out_shape=jax.ShapeDtypeStruct((rows * slots, far_pairs.size * (128 // rank)), bf16),
+        in_specs=[vmem] * 2,
+        out_specs=vmem,
+        compiler_params=pltpu.CompilerParams(vmem_limit_bytes=16 << 20),
+    )(parents, far_pairs[::-1].reshape(1, -1))
     partial = pl.pallas_call(
         functools.partial(far_kernel, ids_lane + 128),
         out_shape=jax.ShapeDtypeStruct((rows * slots, 128), f32),
-        in_specs=[vmem] * 4,
+        in_specs=[vmem] * 3,
         out_specs=vmem,
-        scratch_shapes=[pltpu.VMEM((rows * slots, far_pairs.size * (128 // rank)), bf16)],
-        compiler_params=pltpu.CompilerParams(vmem_limit_bytes=32 << 20),
-    )(second, parent.reshape(-1, 128 // rank), far_pairs[::-1].reshape(1, -1), factors)
+        compiler_params=pltpu.CompilerParams(vmem_limit_bytes=16 << 20),
+    )(second, hits, factors)
     first_data, partial = lax.optimization_barrier((first_data, partial))
     row_locals = lax.all_to_all(partial.reshape(rows, slots, 128), "row", 0, 0, tiled=True)
 
     near_first, to_second = near_sums(first_data, second, ids_lane)
-    near_first = lax.ppermute(near_first, BOTH, swap)
+    near_first = lax.ppermute(near_first, BOTH, home)
     returned = lax.all_to_all(
         jnp.concatenate([to_second, row_locals.sum(axis=0)], axis=1), "col", 0, 0, tiled=True
     )

time: 86.7 us -> 88.5 us (1.021)
  the two profiles are of different devices: /device:TPU:7 before, /device:TPU:1 now
where the time goes in v8:
time: 88.5 us; the launch traced here: 88 us
  starting transfers between devices  33.8 us (38%)
  Pallas kernels  25.6 us (29%)
  waiting for transfers between devices  23.8 us (27%)
  other arithmetic  2.15 us (2%)
  local copies, waits for them, and re-layouts  1.49 us (2%)
    pallas_call x1, Pallas kernels, near_sums(): pl.pallas_call(functools.partial(near_kernel, ids_lane), out_shape=[jax.S...  17.5 us
    ppermute x1, waiting for transfers between devices, shards(): near_first = lax.ppermute(near_first, BOTH, home)  10 us
    all_to_all x1, waiting for transfers between devices, shards(): second = lax.all_to_all(message, 'col', 0, 0, tiled=True)  10 us
    all_to_all x1, starting transfers between devices, shards(): lax.all_to_all(partial.reshape(rows, slots, 128), 'row', 0, 0, tiled=True)  6.72 us
    all_to_all x1, starting transfers between devices, shards(): second = lax.all_to_all(message, 'col', 0, 0, tiled=True)  6.62 us
    ppermute x1, starting transfers between devices, shards(): first_data = lax.ppermute(data, BOTH, swap)  6.02 us
    all_to_all x1, starting transfers between devices, shards(): from_row = lax.all_to_all(message, 'row', 0, 0, tiled=True)  5.81 us
    ppermute x1, starting transfers between devices, shards(): near_first = lax.ppermute(near_first, BOTH, home)  5.09 us
  transfers between devices with their start and end apart: 6, of which 3 were waited for; matrix products, arithmetic and copies ran while one was open for 2% of the time, Pallas kernels for 21%

profile of v8, /device:TPU:1, one launch (start us, length us, event | category | flops | bytes accessed | tf_op | source)
XLA Modules:
  0.0 88.0 jit_solution(15527779665020821532)
XLA Ops:
  0.0 0.0 copy-start.2
  0.0 0.0 copy-start.3
  0.7 4.0 %shard_map.91 = f32[8,10,128]{2,1,0:T(8,128)} custom-call(s32[1]{0:T(128)S(6)} %copy.25.count, s32[2,128]{1,0:T(2,128)} %pairs.1, bf16[3,32,256]{2,1,0:T(8,128)(2,1)} %bitcast.63, bf16[1024,768]{1,0:T(8,128)(2,1)} %bitcast.56, f32[1024,32]{1,0:T(8,128)} %bitcast.60), custom_call_target="tpu_custom_call" | custom-call | tf_op jit(solution)/shard_map/pallas_call | solution.py:263
  4.7 5.8 %all-to-all-start = ((f32[8,10,128]{2,1,0:T(8,128)}), f32[8,10,128]{2,1,0:T(8,128)S(1)}, u32[]{:S(2)}, u32[]{:S(2)}) async-start(f32[8,10,128]{2,1,0:T(8,128)} %shard_map.91), calls=%async_computation | async-start | bytes 131072 | tf_op jit(solution)/shard_map/all_to_all | solution.py:362
  10.5 0.0 copy-done.2
  10.5 0.0 copy-done.3
  10.5 6.0 %collective-permute-start = (bf16[32,1536]{1,0:T(8,128)(2,1)S(1)}, bf16[32,1536]{1,0:T(8,128)(2,1)S(1)}, u32[]{:S(2)}, u32[]{:S(2)}) collective-permute-start(bf16[32,1536]{1,0:T(8,128)(2,1)S(1)} %shard_map.92), channel_id=1, source_target_pairs={{0,8},{1,9},{2,26},{3,27},{4,40},{5,41},{6,58},{7,59},{8,72},{9,73... | collective-permute-start | bytes 294920 | tf_op jit(solution)/shard_map/ppermute | solution.py:364
  16.6 0.1 broadcast_and_fusion
  16.7 0.0 all-to-all-done
  16.7 3.7 %collective-permute-done.first_ref = bf16[32,1536]{1,0:T(8,128)(2,1)S(1)} collective-permute-done((bf16[32,1536]{1,0:T(8,128)(2,1)S(1)}, bf16[32,1536]{1,0:T(8,128)(2,1)S(1)}, u32[]{:S(2)}, u32[]{:S(2)}) %collective-permute-start) | collective-permute-done | bytes 98336 | tf_op jit(solution)/shard_map/ppermute | solution.py:364
  20.4 0.1 reshape.89
  20.5 0.1 fusion.4
  20.6 0.1 stack.7
  20.7 0.1 stack.6
  20.8 0.1 eq.51
  20.9 0.3 fusion
  21.2 0.1 broadcast_in_dim.7
  21.3 0.0 copy-start.6
  21.3 0.0 copy-start.5
  21.3 0.0 copy-start.4
  21.3 0.9 %pad_maximum_fusion = bf16[16,8,2688]{2,1,0:T(8,128)(2,1)} fusion(bf16[16,8,1024]{2,1,0:T(8,128)(2,1)S(1)} %tile.9, bf16[16,8,128]{2,1,0:T(8,128)(2,1)S(1)} %broadcast_in_dim.7, bf16[16,8,1536]{2,1,0:T(8,128)(2,1)S(1)} %fusion), kind=kLoop, calls=%fused_computation.2 | loop fusion | flops 2064384 | bytes 1376256 | tf_op jit(solution)/shard_map/concatenate | solution.py:376
  22.2 6.6 %all-to-all-start.1 = ((bf16[16,8,2688]{2,1,0:T(8,128)(2,1)}), bf16[16,8,2688]{2,1,0:T(8,128)(2,1)S(1)}, u32[]{:S(2)}, u32[]{:S(2)}) async-start(bf16[16,8,2688]{2,1,0:T(8,128)(2,1)} %pad_maximum_fusion), calls=%async_computation.1 | async-start | bytes 1376256 | tf_op jit(solution)/shard_map/all_to_all | solution.py:384
  28.9 0.0 copy-done.6
  28.9 0.1 reshape.91.ends
  29.0 0.0 copy-done.5
  29.0 0.5 reshape.90.parents
  29.5 0.0 copy-done.4
  29.5 0.3 copy.24
  29.9 0.2 pad_maximum_fusion.1.factors
  30.1 0.6 shard_map.93.hits
  30.7 10.0 %all-to-all-done.1 = bf16[16,8,2688]{2,1,0:T(8,128)(2,1)S(1)} async-done(((bf16[16,8,2688]{2,1,0:T(8,128)(2,1)}), bf16[16,8,2688]{2,1,0:T(8,128)(2,1)S(1)}, u32[]{:S(2)}, u32[]{:S(2)}) %all-to-all-start.1) | async-done | bytes 688160 | tf_op jit(solution)/shard_map/all_to_all | solution.py:384
  40.7 1.9 %shard_map.94 = f32[1024,128]{1,0:T(8,128)} custom-call(bf16[128,2688]{1,0:T(8,128)(2,1)S(1)} %bitcast.58, bf16[1024,512]{1,0:T(8,128)(2,1)S(1)} %shard_map.93.hits, f32[32,32,128]{2,1,0:T(8,128)S(1)} %pad_maximum_fusion.1.factors), custom_call_target="tpu_custom_call" | custom-call | tf_op jit(solution)/shard_map/pallas_call | solution.py:396
  42.5 6.7 %all-to-all-start.2 = ((f32[8,128,128]{2,1,0:T(8,128)}), f32[8,128,128]{2,1,0:T(8,128)S(1)}, u32[]{:S(2)}, u32[]{:S(2)}) async-start(f32[8,128,128]{2,1,0:T(8,128)} %bitcast.28), calls=%async_computation.2 | async-start | bytes 1048576 | tf_op jit(solution)/shard_map/all_to_all | solution.py:404
  49.3 17.5 %shard_map.95 = (f32[32,768]{1,0:T(8,128)S(1)}, f32[128,768]{1,0:T(8,128)S(1)}) custom-call(bf16[32,1536]{1,0:T(8,128)(2,1)S(1)} %collective-permute-done.first_ref, bf16[128,2688]{1,0:T(8,128)(2,1)S(1)} %bitcast.59), custom_call_target="tpu_custom_call" | custom-call | flops 2147483648 | bytes 1179648 | tf_op jit(solution)/shard_map/pallas_call | solution.py:152
  66.8 0.0 copy-start
  66.8 0.0 copy-start.1
  66.8 0.0 all-to-all-done.2
  66.8 0.8 maximum_bitcast_fusion
  67.6 3.6 %all-to-all-start.3 = ((f32[16,8,896]{2,1,0:T(8,128)}), f32[16,8,896]{2,1,0:T(8,128)S(1)}, u32[]{:S(2)}, u32[]{:S(2)}) async-start(f32[16,8,896]{2,1,0:T(8,128)} %maximum_bitcast_fusion), calls=%async_computation.3 | async-start | bytes 917504 | tf_op jit(solution)/shard_map/all_to_all | solution.py:408
  71.2 5.1 %collective-permute-start.1 = (f32[32,768]{1,0:T(8,128)S(1)}, f32[32,768]{1,0:T(8,128)S(1)}, u32[]{:S(2)}, u32[]{:S(2)}) collective-permute-start(f32[32,768]{1,0:T(8,128)S(1)} %get-tuple-element.24), channel_id=1, source_target_pairs={{8,0},{9,1},{26,2},{27,3},{40,4},{41,5},{58,6},{59,7},{72,8},{73,9... | collective-permute-start | bytes 294920 | tf_op jit(solution)/shard_map/ppermute | solution.py:407
  76.3 0.1 unstack.12.back
  76.4 10.0 %collective-permute-done.1.near_first = f32[32,768]{1,0:T(8,128)S(1)} collective-permute-done((f32[32,768]{1,0:T(8,128)S(1)}, f32[32,768]{1,0:T(8,128)S(1)}, u32[]{:S(2)}, u32[]{:S(2)}) %collective-permute-start.1) | collective-permute-done | bytes 98336 | tf_op jit(solution)/shard_map/ppermute | solution.py:407
  86.4 0.0 all-to-all-done.3
  86.4 0.0 copy-done
  86.4 0.0 copy-done.1
  86.4 1.5 %shard_map.96 = f32[3,32,256]{2,1,0:T(8,128)} custom-call(f32[1,128]{1,0:T(1,128)S(1)} %unstack.12.back, f32[128,896]{1,0:T(8,128)S(1)} %bitcast.62, f32[32,768]{1,0:T(8,128)S(1)} %collective-permute-done.1.near_first, bf16[1024,768]{1,0:T(8,128)(2,1)S(1)} %bitcast.57, f32[1024,32]{1,0:T(8,128)S(1)} %bitcast.61), custom_call_target="tpu_custom_call" | custom-call | tf_op jit(solution)/shard_map/pallas_call | solution.py:315
  (14 shorter events, 0.2 us)
Async XLA Ops:
  0.0 10.5 %copy-start.2 = (bf16[32,3,256]{2,0,1:T(8,128)(2,1)S(1)}, bf16[32,3,256]{2,0,1:T(8,128)(2,1)}, u32[]{:S(2)}) copy-start(bf16[32,3,256]{2,0,1:T(8,128)(2,1)} %param.9) | copy-start | bytes 147460
  0.0 10.5 %copy-start.3 = (bf16[32,3,256]{2,0,1:T(8,128)(2,1)S(1)}, bf16[32,3,256]{2,0,1:T(8,128)(2,1)}, u32[]{:S(2)}) copy-start(bf16[32,3,256]{2,0,1:T(8,128)(2,1)} %param.10) | copy-start | bytes 147460
  4.7 11.9 %all-to-all-start = ((f32[8,10,128]{2,1,0:T(8,128)}), f32[8,10,128]{2,1,0:T(8,128)S(1)}, u32[]{:S(2)}, u32[]{:S(2)}) async-start(f32[8,10,128]{2,1,0:T(8,128)} %shard_map.91), calls=%async_computation | async-start | bytes 131072 | tf_op jit(solution)/shard_map/all_to_all | solution.py:362
  10.5 9.8 %collective-permute-start = (bf16[32,1536]{1,0:T(8,128)(2,1)S(1)}, bf16[32,1536]{1,0:T(8,128)(2,1)S(1)}, u32[]{:S(2)}, u32[]{:S(2)}) collective-permute-start(bf16[32,1536]{1,0:T(8,128)(2,1)S(1)} %shard_map.92), channel_id=1, source_target_pairs={{0,8},{1,9},{2,26},{3,27},{4,40},{5,41},{6,58},{7,59},{8,72},{9,73... | collective-permute-start | bytes 294920 | tf_op jit(solution)/shard_map/ppermute | solution.py:364
  21.3 7.6 %copy-start.6 = (s32[2,64]{1,0:T(2,128)S(1)}, s32[2,64]{1,0:T(2,128)}, u32[]{:S(2)}) copy-start(s32[2,64]{1,0:T(2,128)} %param.16) | copy-start | bytes 1540
  21.3 7.7 %copy-start.5 = (s32[4096]{0:T(1024)S(1)}, s32[4096]{0:T(1024)}, u32[]{:S(2)}) copy-start(s32[4096]{0:T(1024)} %param.13) | copy-start | bytes 49156
  21.3 8.2 %copy-start.4 = (f32[64,32,32]{0,2,1:T(8,128)S(1)}, f32[64,32,32]{0,2,1:T(8,128)}, u32[]{:S(2)}) copy-start(f32[64,32,32]{0,2,1:T(8,128)} %param.17) | copy-start | bytes 786436
  22.2 18.4 %all-to-all-start.1 = ((bf16[16,8,2688]{2,1,0:T(8,128)(2,1)}), bf16[16,8,2688]{2,1,0:T(8,128)(2,1)S(1)}, u32[]{:S(2)}, u32[]{:S(2)}) async-start(bf16[16,8,2688]{2,1,0:T(8,128)(2,1)} %pad_maximum_fusion), calls=%async_computation.1 | async-start | bytes 1376256 | tf_op jit(solution)/shard_map/all_to_all | solution.py:384
  42.5 24.3 %all-to-all-start.2 = ((f32[8,128,128]{2,1,0:T(8,128)}), f32[8,128,128]{2,1,0:T(8,128)S(1)}, u32[]{:S(2)}, u32[]{:S(2)}) async-start(f32[8,128,128]{2,1,0:T(8,128)} %bitcast.28), calls=%async_computation.2 | async-start | bytes 1048576 | tf_op jit(solution)/shard_map/all_to_all | solution.py:404
  66.8 19.7 %copy-start = (bf16[32,32,768]{2,1,0:T(8,128)(2,1)S(1)}, bf16[32,32,768]{2,1,0:T(8,128)(2,1)}, u32[]{:S(2)}) copy-start(bf16[32,32,768]{2,1,0:T(8,128)(2,1)} %param.11) | copy-start | bytes 4718596
  66.8 19.7 %copy-start.1 = (f32[32,32,32]{2,1,0:T(8,128)S(1)}, f32[32,32,32]{2,1,0:T(8,128)}, u32[]{:S(2)}) copy-start(f32[32,32,32]{2,1,0:T(8,128)} %param.12) | copy-start | bytes 393220
  67.6 18.8 %all-to-all-start.3 = ((f32[16,8,896]{2,1,0:T(8,128)}), f32[16,8,896]{2,1,0:T(8,128)S(1)}, u32[]{:S(2)}, u32[]{:S(2)}) async-start(f32[16,8,896]{2,1,0:T(8,128)} %maximum_bitcast_fusion), calls=%async_computation.3 | async-start | bytes 917504 | tf_op jit(solution)/shard_map/all_to_all | solution.py:408
  71.2 15.2 %collective-permute-start.1 = (f32[32,768]{1,0:T(8,128)S(1)}, f32[32,768]{1,0:T(8,128)S(1)}, u32[]{:S(2)}, u32[]{:S(2)}) collective-permute-start(f32[32,768]{1,0:T(8,128)S(1)} %get-tuple-element.24), channel_id=1, source_target_pairs={{8,0},{9,1},{26,2},{27,3},{40,4},{41,5},{58,6},{59,7},{72,8},{73,9... | collective-permute-start | bytes 294920 | tf_op jit(solution)/shard_map/ppermute | solution.py:407

commit v9 on v8

--- a/solution.py
+++ b/solution.py
@@ -245,9 +245,12 @@
     folded = sum(every[:, k : k + 128] for k in range(0, own * rank, 128))
     moments = sum(folded[:, k : k + rank] for k in range(0, 128, rank))
     copies[2].wait()
-    lifted = lax.dot_general(
-        moments, transfer[...], across, precision=lax.Precision.HIGHEST, preferred_element_type=f32
-    )
+    wide = jnp.concatenate(pieces(moments, 3), axis=0).astype(bf16)
+    lifted = sum(
+        lax.dot_general(wide, piece.astype(bf16), across, preferred_element_type=f32)
+        for piece in pieces(transfer[...], 2)
+    )
+    lifted = lifted[:own] + lifted[own : 2 * own] + lifted[2 * own :]
     lifted = jnp.sum(jnp.where(mine, lifted, 0.0), axis=0, keepdims=True)
     lifted = jnp.concatenate([lifted[:, k : k + 128] for k in range(0, own * rank, 128)], axis=0)
     rows = message.shape[0]
@@ -281,6 +284,62 @@
     )
 
 
+def pick_kernel(orders, place, from_row, data, message_hbm, back, message, sems):
+    rows, lift_rows = from_row.shape[0], from_row.shape[1] - 2
+    own, wide = data.shape
+    slots = message.shape[0]
+    seats = len(orders[0])
+    per_pair = slots // seats
+    half = seats // rows
+
+    def send(begin, stop):
+        lanes = pl.ds(begin, stop - begin)
+        copy = pltpu.make_async_copy(message.at[:, lanes], message_hbm.at[:, lanes], sems.at[min(begin, 1)])
+        copy.start()
+        return copy
+
+    for r in range(rows):
+        lifted = from_row[r, :lift_rows, :]
+        lanes = slice(wide + 128 * (r + 1), wide + 128 * (r + 2))
+        message[:, lanes] = jnp.concatenate([lifted] * (slots // lift_rows), axis=0).astype(bf16)
+    copies = [send(wide + 128, message.shape[1])]
+    lane = lax.broadcasted_iota(jnp.int32, (1, 128), 1)
+    triples = []
+    for r in range(rows):
+        first, second = from_row[r, lift_rows : lift_rows + 1, :], from_row[r, lift_rows + 1 :, :]
+        same = (place[0] == r) & (half * place[0] + lane // per_pair == place[1]) & (first == second)
+        triples.append(jnp.concatenate([first, second, jnp.where(same, -1.0, second)], axis=0))
+    even, odd = (
+        jnp.concatenate([triples[r][:, h * per_pair : (h + 1) * per_pair] for r, h in order], axis=1)
+        for order in orders
+    )
+    ids = jnp.where(place[0] % 2 == 0, even, odd)
+    back[...] = ids[2:]
+    down = (((0,), (0,)), ((), ()))
+    cluster = lax.broadcasted_iota(jnp.int32, (own, slots), 0).astype(f32)
+    first, second = ((ids[k : k + 1] == cluster).astype(f32).astype(bf16) for k in range(2))
+    message[:, :wide] = lax.dot_general(second, data[...], down, preferred_element_type=f32).astype(bf16)
+    names = (lax.broadcasted_iota(jnp.int32, (own, 128), 0) + 1).astype(f32).astype(bf16)
+    names = lax.dot_general(first, names, down, preferred_element_type=f32) - 1.0
+    message[:, wide : wide + 128] = names.astype(bf16)
+    copies.append(send(0, wide + 128))
+    for copy in copies:
+        copy.wait()
+
+
+def pick(place, from_row, data, slots, orders):
+    vmem = pl.BlockSpec(memory_space=pltpu.VMEM)
+    wide = data.shape[1] + 128 * (1 + from_row.shape[0])
+    return pl.pallas_call(
+        functools.partial(pick_kernel, orders),
+        out_shape=[jax.ShapeDtypeStruct((slots, wide), bf16), jax.ShapeDtypeStruct((1, slots), f32)],
+        in_specs=[pl.BlockSpec(memory_space=pltpu.SMEM)] + [vmem] * 2,
+        out_specs=[pl.BlockSpec(memory_space=pltpu.HBM), vmem],
+        scratch_shapes=[pltpu.VMEM((slots, wide), bf16), pltpu.SemaphoreType.DMA((2,))],
+        compiler_params=pltpu.CompilerParams(vmem_limit_bytes=8 << 20),
+    )(place, from_row, data)
+
+
 def end_kernel(back, returned, near_first, basis, transfer, out, velocity, sems):
     own, panels = velocity.shape[1:]
     rank = transfer.shape[1]
@@ -320,7 +379,7 @@
         scratch_shapes=[pltpu.VMEM(shape, f32), pltpu.SemaphoreType.DMA((3,))],
         compiler_params=pltpu.CompilerParams(vmem_limit_bytes=8 << 20),
     )(
-        back[None],
+        back,
         returned,
         near_first,
         basis.reshape(own * rank, width),
@@ -328,10 +387,6 @@
     ).transpose(1, 0, 2)
 
 
-def one_hot(ids, count):
-    return (ids[:, None] == jnp.arange(count, dtype=ids.dtype)[None, :]).astype(f32)
-
-
 def seat(p, r, h, rows):
     hops = rows // 2
     near = (2 * (p % 2) + h, 2 * (p % 2) + (3 * h - 1))[r % 2] % hops
@@ -343,11 +398,7 @@
     rank = basis.shape[1]
     rows, cols = lax.axis_size("row"), lax.axis_size("col")
     half = cols // rows
-    my_row, my_col = lax.axis_index("row"), lax.axis_index("col")
     slots = near_pairs.shape[1]
-    per_pair = slots // cols
-    block = slots // rows
-    lift_rows = own * rank // 128
     vmem = pl.BlockSpec(memory_space=pltpu.VMEM)
 
     swap = [
@@ -362,25 +413,11 @@
     from_row = lax.all_to_all(message, "row", 0, 0, tiled=True)
     data = join(density, coords)
     first_data = lax.ppermute(data, BOTH, swap)
-    first_data, from_row = lax.optimization_barrier((first_data, from_row))
-
-    ids = from_row[:, lift_rows:, :block].reshape(rows, 2, half, per_pair)
-    same_owner = (jnp.arange(rows)[:, None] == my_row) & (half * my_row + jnp.arange(half) == my_col)
-    back_ids = jnp.where(same_owner[:, :, None] & (ids[:, 0] == ids[:, 1]), -1.0, ids[:, 1])
-    ids = jnp.concatenate([ids, back_ids[:, None]], axis=1)
+
+    place = jnp.stack([lax.axis_index("row"), lax.axis_index("col")])
     orders = [sorted((seat(p, r, h, rows), r, h) for r in range(rows) for h in range(half)) for p in range(2)]
-    even, odd = (jnp.stack([ids[r, :, h] for _, r, h in order], axis=1).reshape(3, slots) for order in orders)
-    own_first, own_second, back_ids = jnp.where(my_row % 2 == 0, even, odd)
-    picked = jnp.dot(one_hot(own_second, own).astype(bf16), data, preferred_element_type=f32)
-    row_lifted = from_row[:, :lift_rows, :].astype(bf16).transpose(1, 0, 2).reshape(lift_rows, -1)
-    message = jnp.concatenate(
-        [
-            picked.astype(bf16),
-            jnp.broadcast_to(own_first[:, None], (slots, 128)).astype(bf16),
-            jnp.tile(row_lifted, (cols, 1)),
-        ],
-        axis=1,
-    )
+    orders = [[(r, h) for _, r, h in order] for order in orders]
+    message, back_ids = pick(place, from_row, data, slots, orders)
     second = lax.all_to_all(message, "col", 0, 0, tiled=True)
     ids_lane = 6 * panels
 

time: 88.5 us -> 85.6 us (0.967)
  waiting for transfers between devices: 23.8 us -> 21 us
  Pallas kernels: 25.6 us -> 27 us
  other arithmetic: 2.15 us -> 1.12 us
    all_to_all x1, waiting for transfers between devices: 0.01 us -> 4.76 us  [shards(): from_row = lax.all_to_all(message, 'row', 0, 0, tiled=True)]
    all_to_all x1, waiting for transfers between devices: 10 us -> 6.12 us  [shards(): second = lax.all_to_all(message, 'col', 0, 0, tiled=True)]
    ppermute x1, waiting for transfers between devices: 3.72 us -> 0.01 us  [shards(): first_data = lax.ppermute(data, BOTH, swap)]
    all_to_all x1, starting transfers between devices: 6.72 us -> 4.7 us  [shards(): lax.all_to_all(partial.reshape(rows, slots, 128), 'row', 0, 0, tiled=True)]
    pallas_call x0 -> x1, Pallas kernels: none -> 1.75 us  [pick(): pl.pallas_call(functools.partial(pick_kernel, orders), out_shape=[jax.Sha...]
    all_to_all x1, starting transfers between devices: 6.62 us -> 7.78 us  [shards(): second = lax.all_to_all(message, 'col', 0, 0, tiled=True)]
    concatenate x1 -> x0, other arithmetic: 0.91 us -> none  [shards(): jnp.concatenate([picked.astype(bf16), jnp.broadcast_to(own_first[:, None]...]
  transfers between devices with their start and end apart: 6 -> 6, of which waited for: 3 -> 3; matrix products, arithmetic and copies ran while one was open for 2% -> 1% of each run, Pallas kernels for 21% -> 24%
where the time goes in v9:
time: 85.6 us; the launch traced here: 85 us
  starting transfers between devices  34.1 us (40%)
  Pallas kernels  27 us (32%)
  waiting for transfers between devices  21 us (25%)
  other arithmetic  1.12 us (1%)
  local copies, waits for them, and re-layouts  0.98 us (1%)
    pallas_call x1, Pallas kernels, near_sums(): pl.pallas_call(functools.partial(near_kernel, ids_lane), out_shape=[jax.S...  17.6 us
    ppermute x1, waiting for transfers between devices, shards(): near_first = lax.ppermute(near_first, BOTH, home)  10.1 us
    all_to_all x1, starting transfers between devices, shards(): second = lax.all_to_all(message, 'col', 0, 0, tiled=True)  7.78 us
    ppermute x1, starting transfers between devices, shards(): first_data = lax.ppermute(data, BOTH, swap)  6.2 us
    all_to_all x1, waiting for transfers between devices, shards(): second = lax.all_to_all(message, 'col', 0, 0, tiled=True)  6.12 us
    all_to_all x1, starting transfers between devices, shards(): from_row = lax.all_to_all(message, 'row', 0, 0, tiled=True)  5.94 us
    ppermute x1, starting transfers between devices, shards(): near_first = lax.ppermute(near_first, BOTH, home)  5.19 us
    all_to_all x1, waiting for transfers between devices, shards(): from_row = lax.all_to_all(message, 'row', 0, 0, tiled=True)  4.76 us
  transfers between devices with their start and end apart: 6, of which 3 were waited for; matrix products, arithmetic and copies ran while one was open for 1% of the time, Pallas kernels for 24%

profile of v9, /device:TPU:1, one launch (start us, length us, event | category | flops | bytes accessed | tf_op | source)
XLA Modules:
  0.0 85.0 jit_solution(1111481789371824405)
XLA Ops:
  0.0 0.0 copy-start.2
  0.0 0.0 copy-start.3
  0.7 0.0 copy-start.5
  0.7 3.7 %shard_map.91 = f32[8,10,128]{2,1,0:T(8,128)} custom-call(s32[1]{0:T(128)S(6)} %copy.14.count, s32[2,128]{1,0:T(2,128)} %pairs.1, bf16[3,32,256]{2,1,0:T(8,128)(2,1)} %bitcast.25, bf16[1024,768]{1,0:T(8,128)(2,1)} %bitcast.18, f32[1024,32]{1,0:T(8,128)} %bitcast.22), custom_call_target="tpu_custom_call" | custom-call | tf_op jit(solution)/shard_map/pallas_call | solution.py:266
  4.4 0.0 copy-start.6
  4.4 0.0 copy-start.4
  4.4 5.9 %all-to-all-start = ((f32[8,10,128]{2,1,0:T(8,128)}), f32[8,10,128]{2,1,0:T(8,128)S(1)}, u32[]{:S(2)}, u32[]{:S(2)}) async-start(f32[8,10,128]{2,1,0:T(8,128)} %shard_map.91), calls=%async_computation | async-start | bytes 131072 | tf_op jit(solution)/shard_map/all_to_all | solution.py:413
  10.4 0.1 pad_add_fusion.place
  10.5 0.0 copy-done.2
  10.5 0.0 copy-done.3
  10.5 4.8 %all-to-all-done.from_row = f32[8,10,128]{2,1,0:T(8,128)S(1)} async-done(((f32[8,10,128]{2,1,0:T(8,128)}), f32[8,10,128]{2,1,0:T(8,128)S(1)}, u32[]{:S(2)}, u32[]{:S(2)}) %all-to-all-start) | async-done | bytes 40992 | tf_op jit(solution)/shard_map/all_to_all | solution.py:413
  15.2 1.7 %shard_map.93 = (bf16[128,2688]{1,0:T(8,128)(2,1)}, f32[1,128]{1,0:T(1,128)S(1)}) custom-call(s32[2]{0:T(128)S(1)} %pad_add_fusion.place, f32[8,10,128]{2,1,0:T(8,128)S(1)} %all-to-all-done.from_row, bf16[32,1536]{1,0:T(8,128)(2,1)S(1)} %shard_map.92.data), custom_call_target="tpu_custom_call" | custom-call | tf_op jit(solution)/shard_map/pallas_call | solution.py:333
  17.0 7.8 %all-to-all-start.1 = ((bf16[16,8,2688]{2,1,0:T(8,128)(2,1)}), bf16[16,8,2688]{2,1,0:T(8,128)(2,1)S(1)}, u32[]{:S(2)}, u32[]{:S(2)}) async-start(bf16[16,8,2688]{2,1,0:T(8,128)(2,1)} %bitcast.7), calls=%async_computation.1 | async-start | bytes 1376256 | tf_op jit(solution)/shard_map/all_to_all | solution.py:421
  24.8 6.2 %collective-permute-start = (bf16[32,1536]{1,0:T(8,128)(2,1)S(1)}, bf16[32,1536]{1,0:T(8,128)(2,1)S(1)}, u32[]{:S(2)}, u32[]{:S(2)}) collective-permute-start(bf16[32,1536]{1,0:T(8,128)(2,1)S(1)} %shard_map.92.data), channel_id=1, source_target_pairs={{0,8},{1,9},{2,26},{3,27},{4,40},{5,41},{6,58},{7,59},{8,72},{9,73... | collective-permute-start | bytes 294920 | tf_op jit(solution)/shard_map/ppermute | solution.py:415
  31.0 0.0 copy-done.5
  31.0 0.5 reshape.23.parents
  31.5 0.0 copy-done.6
  31.6 0.1 reshape.24.ends
  31.6 0.0 copy-done.4
  31.6 0.3 copy.13
  32.0 0.2 pad_maximum_fusion.factors
  32.2 0.6 shard_map.94.hits
  32.8 6.1 %all-to-all-done.1 = bf16[16,8,2688]{2,1,0:T(8,128)(2,1)S(1)} async-done(((bf16[16,8,2688]{2,1,0:T(8,128)(2,1)}), bf16[16,8,2688]{2,1,0:T(8,128)(2,1)S(1)}, u32[]{:S(2)}, u32[]{:S(2)}) %all-to-all-start.1) | async-done | bytes 688160 | tf_op jit(solution)/shard_map/all_to_all | solution.py:421
  38.9 1.8 %shard_map.95 = f32[1024,128]{1,0:T(8,128)} custom-call(bf16[128,2688]{1,0:T(8,128)(2,1)S(1)} %bitcast.20, bf16[1024,512]{1,0:T(8,128)(2,1)S(1)} %shard_map.94.hits, f32[32,32,128]{2,1,0:T(8,128)S(1)} %pad_maximum_fusion.factors), custom_call_target="tpu_custom_call" | custom-call | tf_op jit(solution)/shard_map/pallas_call | solution.py:433
  40.7 0.0 collective-permute-done.first_ref
  40.7 4.7 %all-to-all-start.2 = ((f32[8,128,128]{2,1,0:T(8,128)}), f32[8,128,128]{2,1,0:T(8,128)S(1)}, u32[]{:S(2)}, u32[]{:S(2)}) async-start(f32[8,128,128]{2,1,0:T(8,128)} %bitcast.11), calls=%async_computation.2 | async-start | bytes 1048576 | tf_op jit(solution)/shard_map/all_to_all | solution.py:441
  45.4 17.6 %shard_map.96 = (f32[32,768]{1,0:T(8,128)S(1)}, f32[128,768]{1,0:T(8,128)S(1)}) custom-call(bf16[32,1536]{1,0:T(8,128)(2,1)S(1)} %collective-permute-done.first_ref, bf16[128,2688]{1,0:T(8,128)(2,1)S(1)} %bitcast.21), custom_call_target="tpu_custom_call" | custom-call | flops 2147483648 | bytes 1179648 | tf_op jit(solution)/shard_map/pallas_call | solution.py:152
  63.0 0.0 copy-start
  63.0 0.0 copy-start.1
  63.0 0.0 all-to-all-done.2
  63.1 0.8 maximum_bitcast_fusion
  63.9 4.3 %all-to-all-start.3 = ((f32[16,8,896]{2,1,0:T(8,128)}), f32[16,8,896]{2,1,0:T(8,128)S(1)}, u32[]{:S(2)}, u32[]{:S(2)}) async-start(f32[16,8,896]{2,1,0:T(8,128)} %maximum_bitcast_fusion), calls=%async_computation.3 | async-start | bytes 917504 | tf_op jit(solution)/shard_map/all_to_all | solution.py:445
  68.2 5.2 %collective-permute-start.1 = (f32[32,768]{1,0:T(8,128)S(1)}, f32[32,768]{1,0:T(8,128)S(1)}, u32[]{:S(2)}, u32[]{:S(2)}) collective-permute-start(f32[32,768]{1,0:T(8,128)S(1)} %get-tuple-element.24), channel_id=1, source_target_pairs={{8,0},{9,1},{26,2},{27,3},{40,4},{41,5},{58,6},{59,7},{72,8},{73,9... | collective-permute-start | bytes 294920 | tf_op jit(solution)/shard_map/ppermute | solution.py:444
  73.4 10.1 %collective-permute-done.1.near_first = f32[32,768]{1,0:T(8,128)S(1)} collective-permute-done((f32[32,768]{1,0:T(8,128)S(1)}, f32[32,768]{1,0:T(8,128)S(1)}, u32[]{:S(2)}, u32[]{:S(2)}) %collective-permute-start.1) | collective-permute-done | bytes 98336 | tf_op jit(solution)/shard_map/ppermute | solution.py:444
  83.4 0.0 all-to-all-done.3
  83.4 0.0 copy-done
  83.4 0.0 copy-done.1
  83.4 1.5 %shard_map.97 = f32[3,32,256]{2,1,0:T(8,128)} custom-call(f32[1,128]{1,0:T(1,128)S(1)} %get-tuple-element.18.back, f32[128,896]{1,0:T(8,128)S(1)} %bitcast.24, f32[32,768]{1,0:T(8,128)S(1)} %collective-permute-done.1.near_first, bf16[1024,768]{1,0:T(8,128)(2,1)S(1)} %bitcast.19, f32[1024,32]{1,0:T(8,128)S(1)} %bitcast.23), custom_call_target="tpu_custom_call" | custom-call | tf_op jit(solution)/shard_map/pallas_call | solution.py:374
  (3 shorter events, 0.1 us)
Async XLA Ops:
  0.0 10.5 %copy-start.2 = (bf16[32,3,256]{2,0,1:T(8,128)(2,1)S(1)}, bf16[32,3,256]{2,0,1:T(8,128)(2,1)}, u32[]{:S(2)}) copy-start(bf16[32,3,256]{2,0,1:T(8,128)(2,1)} %param.9) | copy-start | bytes 147460
  0.0 10.5 %copy-start.3 = (bf16[32,3,256]{2,0,1:T(8,128)(2,1)S(1)}, bf16[32,3,256]{2,0,1:T(8,128)(2,1)}, u32[]{:S(2)}) copy-start(bf16[32,3,256]{2,0,1:T(8,128)(2,1)} %param.10) | copy-start | bytes 147460
  0.7 30.3 %copy-start.5 = (s32[4096]{0:T(1024)S(1)}, s32[4096]{0:T(1024)}, u32[]{:S(2)}) copy-start(s32[4096]{0:T(1024)} %param.13) | copy-start | bytes 49156
  4.4 27.1 %copy-start.6 = (s32[2,64]{1,0:T(2,128)S(1)}, s32[2,64]{1,0:T(2,128)}, u32[]{:S(2)}) copy-start(s32[2,64]{1,0:T(2,128)} %param.16) | copy-start | bytes 1540
  4.4 27.2 %copy-start.4 = (f32[64,32,32]{0,2,1:T(8,128)S(1)}, f32[64,32,32]{0,2,1:T(8,128)}, u32[]{:S(2)}) copy-start(f32[64,32,32]{0,2,1:T(8,128)} %param.17) | copy-start | bytes 786436
  4.4 10.8 %all-to-all-start = ((f32[8,10,128]{2,1,0:T(8,128)}), f32[8,10,128]{2,1,0:T(8,128)S(1)}, u32[]{:S(2)}, u32[]{:S(2)}) async-start(f32[8,10,128]{2,1,0:T(8,128)} %shard_map.91), calls=%async_computation | async-start | bytes 131072 | tf_op jit(solution)/shard_map/all_to_all | solution.py:413
  17.0 21.9 %all-to-all-start.1 = ((bf16[16,8,2688]{2,1,0:T(8,128)(2,1)}), bf16[16,8,2688]{2,1,0:T(8,128)(2,1)S(1)}, u32[]{:S(2)}, u32[]{:S(2)}) async-start(bf16[16,8,2688]{2,1,0:T(8,128)(2,1)} %bitcast.7), calls=%async_computation.1 | async-start | bytes 1376256 | tf_op jit(solution)/shard_map/all_to_all | solution.py:421
  24.8 16.0 %collective-permute-start = (bf16[32,1536]{1,0:T(8,128)(2,1)S(1)}, bf16[32,1536]{1,0:T(8,128)(2,1)S(1)}, u32[]{:S(2)}, u32[]{:S(2)}) collective-permute-start(bf16[32,1536]{1,0:T(8,128)(2,1)S(1)} %shard_map.92.data), channel_id=1, source_target_pairs={{0,8},{1,9},{2,26},{3,27},{4,40},{5,41},{6,58},{7,59},{8,72},{9,73... | collective-permute-start | bytes 294920 | tf_op jit(solution)/shard_map/ppermute | solution.py:415
  40.7 22.3 %all-to-all-start.2 = ((f32[8,128,128]{2,1,0:T(8,128)}), f32[8,128,128]{2,1,0:T(8,128)S(1)}, u32[]{:S(2)}, u32[]{:S(2)}) async-start(f32[8,128,128]{2,1,0:T(8,128)} %bitcast.11), calls=%async_computation.2 | async-start | bytes 1048576 | tf_op jit(solution)/shard_map/all_to_all | solution.py:441
  63.0 20.4 %copy-start = (bf16[32,32,768]{2,1,0:T(8,128)(2,1)S(1)}, bf16[32,32,768]{2,1,0:T(8,128)(2,1)}, u32[]{:S(2)}) copy-start(bf16[32,32,768]{2,1,0:T(8,128)(2,1)} %param.11) | copy-start | bytes 4718596
  63.0 20.4 %copy-start.1 = (f32[32,32,32]{2,1,0:T(8,128)S(1)}, f32[32,32,32]{2,1,0:T(8,128)}, u32[]{:S(2)}) copy-start(f32[32,32,32]{2,1,0:T(8,128)} %param.12) | copy-start | bytes 393220
  63.9 19.6 %all-to-all-start.3 = ((f32[16,8,896]{2,1,0:T(8,128)}), f32[16,8,896]{2,1,0:T(8,128)S(1)}, u32[]{:S(2)}, u32[]{:S(2)}) async-start(f32[16,8,896]{2,1,0:T(8,128)} %maximum_bitcast_fusion), calls=%async_computation.3 | async-start | bytes 917504 | tf_op jit(solution)/shard_map/all_to_all | solution.py:445
  68.2 15.3 %collective-permute-start.1 = (f32[32,768]{1,0:T(8,128)S(1)}, f32[32,768]{1,0:T(8,128)S(1)}, u32[]{:S(2)}, u32[]{:S(2)}) collective-permute-start(f32[32,768]{1,0:T(8,128)S(1)} %get-tuple-element.24), channel_id=1, source_target_pairs={{8,0},{9,1},{26,2},{27,3},{40,4},{41,5},{58,6},{59,7},{72,8},{73,9... | collective-permute-start | bytes 294920 | tf_op jit(solution)/shard_map/ppermute | solution.py:444

commit v10 on v9

--- a/solution.py
+++ b/solution.py
@@ -227,12 +227,14 @@
 
 
 def start_kernel(count, pairs, density_hbm, basis_hbm, transfer_hbm, message, density, basis, transfer, sems):
-    sources = (density_hbm, basis_hbm, transfer_hbm)
-    targets = (density, basis, transfer)
+    own, rank = density.shape[1], transfer.shape[1]
+    step = 256
+    chunks = [pl.ds(k, step) for k in range(0, own * rank, step)]
+    sources = [density_hbm] + [basis_hbm.at[c] for c in chunks] + [transfer_hbm]
+    targets = [density] + [basis.at[c] for c in chunks] + [transfer]
     copies = [pltpu.make_async_copy(a, b, sems.at[k]) for k, (a, b) in enumerate(zip(sources, targets))]
     for copy in copies:
         copy.start()
-    own, rank = density.shape[1], transfer.shape[1]
     mine = own_lanes(own, rank)
     across = (((1,), (1,)), ((), ()))
     ids = lax.rem(pairs[...], own)
@@ -240,11 +242,14 @@
     ids = jnp.where(live, ids, -1).astype(f32)
     copies[0].wait()
     flat = jnp.concatenate([density[i] for i in range(3)], axis=1)
-    copies[1].wait()
-    every = jnp.where(mine, lax.dot_general(flat, basis[...], across, preferred_element_type=f32), 0.0)
-    folded = sum(every[:, k : k + 128] for k in range(0, own * rank, 128))
+    folded = jnp.zeros((own, 128), f32)
+    for k, chunk in enumerate(chunks):
+        copies[1 + k].wait()
+        every = lax.dot_general(flat, basis[chunk, :], across, preferred_element_type=f32)
+        every = jnp.where(mine[:, k * step : (k + 1) * step], every, 0.0)
+        folded += sum(every[:, m : m + 128] for m in range(0, step, 128))
     moments = sum(folded[:, k : k + rank] for k in range(0, 128, rank))
-    copies[2].wait()
+    copies[-1].wait()
     wide = jnp.concatenate(pieces(moments, 3), axis=0).astype(bf16)
     lifted = sum(
         lax.dot_general(wide, piece.astype(bf16), across, preferred_element_type=f32)
@@ -272,7 +277,7 @@
             pltpu.VMEM((3, own, width // 3), density.dtype),
             pltpu.VMEM((own * rank, width), basis.dtype),
             pltpu.VMEM((own * rank, rank), f32),
-            pltpu.SemaphoreType.DMA((3,)),
+            pltpu.SemaphoreType.DMA((own * rank // 256 + 2,)),
         ],
         compiler_params=pltpu.CompilerParams(vmem_limit_bytes=60 << 20),
     )(
@@ -347,9 +352,11 @@
     lift_rows = own * rank // 128
     local = sum(returned[k : k + lift_rows, 3 * panels :] for k in range(0, returned.shape[0], lift_rows))
     local = jnp.concatenate([local[k : k + 1] for k in range(lift_rows)], axis=1)
-    coef = jnp.dot(
-        jnp.where(mine, local, 0.0), transfer[...], precision=lax.Precision.HIGHEST, preferred_element_type=f32
-    )
+    wide = jnp.concatenate(pieces(jnp.where(mine, local, 0.0), 3), axis=0).astype(bf16)
+    coef = sum(
+        jnp.dot(wide, piece.astype(bf16), preferred_element_type=f32) for piece in pieces(transfer[...], 3)
+    )
+    coef = coef[:own] + coef[own : 2 * own] + coef[2 * own :]
     coef = pieces(jnp.where(mine, jnp.concatenate([coef] * own, axis=1), 0.0), 3)
     coef = jnp.concatenate(coef, axis=0).astype(bf16)
     slot = lax.broadcasted_iota(jnp.int32, (own, back.shape[1]), 0).astype(f32)
@@ -413,6 +420,7 @@
     from_row = lax.all_to_all(message, "row", 0, 0, tiled=True)
     data = join(density, coords)
     first_data = lax.ppermute(data, BOTH, swap)
+    first_data, from_row = lax.optimization_barrier((first_data, from_row))
 
     place = jnp.stack([lax.axis_index("row"), lax.axis_index("col")])
     orders = [sorted((seat(p, r, h, rows), r, h) for r in range(rows) for h in range(half)) for p in range(2)]

time: 85.6 us -> 85.2 us (level)
  starting transfers between devices: 34.1 us -> 29.5 us
  waiting for transfers between devices: 21 us -> 24.8 us
    all_to_all x1, waiting for transfers between devices: 6.12 us -> 10.2 us  [shards(): second = lax.all_to_all(message, 'col', 0, 0, tiled=True)]
    all_to_all x1, starting transfers between devices: 7.78 us -> 4.42 us  [shards(): second = lax.all_to_all(message, 'col', 0, 0, tiled=True)]
    all_to_all x1, starting transfers between devices: 5.94 us -> 3.3 us  [shards(): from_row = lax.all_to_all(message, 'row', 0, 0, tiled=True)]
    ppermute x1, starting transfers between devices: 6.2 us -> 7.52 us  [shards(): first_data = lax.ppermute(data, BOTH, swap)]
    all_to_all x1, starting transfers between devices: 4.7 us -> 5.61 us  [shards(): lax.all_to_all(partial.reshape(rows, slots, 128), 'row', 0, 0, tiled=True)]
  transfers between devices with their start and end apart: 6 -> 6, of which waited for: 3 -> 3; matrix products, arithmetic and copies ran while one was open for 1% -> 1% of each run, Pallas kernels for 24% -> 21%
where the time goes in v10:
time: 85.2 us; the launch traced here: 84.6 us
  starting transfers between devices  29.5 us (35%)
  Pallas kernels  27.4 us (32%)
  waiting for transfers between devices  24.8 us (29%)
  other arithmetic  1.12 us (1%)
  local copies, waits for them, and re-layouts  0.98 us (1%)
    pallas_call x1, Pallas kernels, near_sums(): pl.pallas_call(functools.partial(near_kernel, ids_lane), out_shape=[jax.S...  17.6 us
    all_to_all x1, waiting for transfers between devices, shards(): second = lax.all_to_all(message, 'col', 0, 0, tiled=True)  10.2 us
    ppermute x1, waiting for transfers between devices, shards(): near_first = lax.ppermute(near_first, BOTH, home)  10.1 us
    ppermute x1, starting transfers between devices, shards(): first_data = lax.ppermute(data, BOTH, swap)  7.52 us
    all_to_all x1, starting transfers between devices, shards(): lax.all_to_all(partial.reshape(rows, slots, 128), 'row', 0, 0, tiled=True)  5.61 us
    ppermute x1, starting transfers between devices, shards(): near_first = lax.ppermute(near_first, BOTH, home)  5.09 us
    all_to_all x1, waiting for transfers between devices, shards(): from_row = lax.all_to_all(message, 'row', 0, 0, tiled=True)  4.47 us
    all_to_all x1, starting transfers between devices, shards(): second = lax.all_to_all(message, 'col', 0, 0, tiled=True)  4.42 us
  transfers between devices with their start and end apart: 6, of which 3 were waited for; matrix products, arithmetic and copies ran while one was open for 1% of the time, Pallas kernels for 21%

profile of v10, /device:TPU:1, one launch (start us, length us, event | category | flops | bytes accessed | tf_op | source)
XLA Modules:
  0.0 84.6 jit_solution(15133571131686768246)
XLA Ops:
  0.0 0.0 copy-start.2
  0.0 0.0 copy-start.3
  0.7 0.0 copy-start.5
  0.7 4.1 %shard_map.91 = f32[8,10,128]{2,1,0:T(8,128)} custom-call(s32[1]{0:T(128)S(6)} %copy.14.count, s32[2,128]{1,0:T(2,128)} %pairs.1, bf16[3,32,256]{2,1,0:T(8,128)(2,1)} %bitcast.25, bf16[1024,768]{1,0:T(8,128)(2,1)} %bitcast.18, f32[1024,32]{1,0:T(8,128)} %bitcast.22), custom_call_target="tpu_custom_call" | custom-call | tf_op jit(solution)/shard_map/pallas_call | solution.py:271
  4.8 0.0 copy-start.6
  4.8 0.0 copy-start.4
  4.8 0.0 copy-done.2
  4.8 0.0 copy-done.3
  4.8 7.5 %collective-permute-start = (bf16[32,1536]{1,0:T(8,128)(2,1)S(1)}, bf16[32,1536]{1,0:T(8,128)(2,1)S(1)}, u32[]{:S(2)}, u32[]{:S(2)}) collective-permute-start(bf16[32,1536]{1,0:T(8,128)(2,1)S(1)} %shard_map.92.data), channel_id=1, source_target_pairs={{0,8},{1,9},{2,26},{3,27},{4,40},{5,41},{6,58},{7,59},{8,72},{9,73... | collective-permute-start | bytes 294920 | tf_op jit(solution)/shard_map/ppermute | solution.py:422
  12.3 3.3 %all-to-all-start = ((f32[8,10,128]{2,1,0:T(8,128)}), f32[8,10,128]{2,1,0:T(8,128)S(1)}, u32[]{:S(2)}, u32[]{:S(2)}) async-start(f32[8,10,128]{2,1,0:T(8,128)} %shard_map.91), calls=%async_computation | async-start | bytes 131072 | tf_op jit(solution)/shard_map/all_to_all | solution.py:420
  15.7 0.1 pad_add_fusion.place
  15.7 4.5 %all-to-all-done.from_row = f32[8,10,128]{2,1,0:T(8,128)S(1)} async-done(((f32[8,10,128]{2,1,0:T(8,128)}), f32[8,10,128]{2,1,0:T(8,128)S(1)}, u32[]{:S(2)}, u32[]{:S(2)}) %all-to-all-start) | async-done | bytes 40992 | tf_op jit(solution)/shard_map/all_to_all | solution.py:420
  20.2 0.0 collective-permute-done.first_ref
  20.2 1.7 %shard_map.93 = (bf16[128,2688]{1,0:T(8,128)(2,1)}, f32[1,128]{1,0:T(1,128)S(1)}) custom-call(s32[2]{0:T(128)S(1)} %pad_add_fusion.place, f32[8,10,128]{2,1,0:T(8,128)S(1)} %all-to-all-done.from_row, bf16[32,1536]{1,0:T(8,128)(2,1)S(1)} %shard_map.92.data), custom_call_target="tpu_custom_call" | custom-call | tf_op jit(solution)/shard_map/pallas_call | solution.py:338
  21.9 4.4 %all-to-all-start.1 = ((bf16[16,8,2688]{2,1,0:T(8,128)(2,1)}), bf16[16,8,2688]{2,1,0:T(8,128)(2,1)S(1)}, u32[]{:S(2)}, u32[]{:S(2)}) async-start(bf16[16,8,2688]{2,1,0:T(8,128)(2,1)} %bitcast.7), calls=%async_computation.1 | async-start | bytes 1376256 | tf_op jit(solution)/shard_map/all_to_all | solution.py:429
  26.4 0.0 copy-done.5
  26.4 0.5 reshape.23.parents
  26.9 0.0 copy-done.6
  27.0 0.1 reshape.24.ends
  27.0 0.0 copy-done.4
  27.0 0.3 copy.13
  27.3 0.2 pad_maximum_fusion.factors
  27.6 0.6 shard_map.94.hits
  28.2 10.2 %all-to-all-done.1 = bf16[16,8,2688]{2,1,0:T(8,128)(2,1)S(1)} async-done(((bf16[16,8,2688]{2,1,0:T(8,128)(2,1)}), bf16[16,8,2688]{2,1,0:T(8,128)(2,1)S(1)}, u32[]{:S(2)}, u32[]{:S(2)}) %all-to-all-start.1) | async-done | bytes 688160 | tf_op jit(solution)/shard_map/all_to_all | solution.py:429
  38.4 1.9 %shard_map.95 = f32[1024,128]{1,0:T(8,128)} custom-call(bf16[128,2688]{1,0:T(8,128)(2,1)S(1)} %bitcast.20, bf16[1024,512]{1,0:T(8,128)(2,1)S(1)} %shard_map.94.hits, f32[32,32,128]{2,1,0:T(8,128)S(1)} %pad_maximum_fusion.factors), custom_call_target="tpu_custom_call" | custom-call | tf_op jit(solution)/shard_map/pallas_call | solution.py:441
  40.2 5.6 %all-to-all-start.2 = ((f32[8,128,128]{2,1,0:T(8,128)}), f32[8,128,128]{2,1,0:T(8,128)S(1)}, u32[]{:S(2)}, u32[]{:S(2)}) async-start(f32[8,128,128]{2,1,0:T(8,128)} %bitcast.11), calls=%async_computation.2 | async-start | bytes 1048576 | tf_op jit(solution)/shard_map/all_to_all | solution.py:449
  45.8 17.6 %shard_map.96 = (f32[32,768]{1,0:T(8,128)S(1)}, f32[128,768]{1,0:T(8,128)S(1)}) custom-call(bf16[32,1536]{1,0:T(8,128)(2,1)S(1)} %collective-permute-done.first_ref, bf16[128,2688]{1,0:T(8,128)(2,1)S(1)} %bitcast.21), custom_call_target="tpu_custom_call" | custom-call | flops 2147483648 | bytes 1179648 | tf_op jit(solution)/shard_map/pallas_call | solution.py:152
  63.4 0.0 copy-start
  63.4 0.0 copy-start.1
  63.4 0.0 all-to-all-done.2
  63.5 0.8 maximum_bitcast_fusion
  64.3 3.6 %all-to-all-start.3 = ((f32[16,8,896]{2,1,0:T(8,128)}), f32[16,8,896]{2,1,0:T(8,128)S(1)}, u32[]{:S(2)}, u32[]{:S(2)}) async-start(f32[16,8,896]{2,1,0:T(8,128)} %maximum_bitcast_fusion), calls=%async_computation.3 | async-start | bytes 917504 | tf_op jit(solution)/shard_map/all_to_all | solution.py:453
  67.9 5.1 %collective-permute-start.1 = (f32[32,768]{1,0:T(8,128)S(1)}, f32[32,768]{1,0:T(8,128)S(1)}, u32[]{:S(2)}, u32[]{:S(2)}) collective-permute-start(f32[32,768]{1,0:T(8,128)S(1)} %get-tuple-element.28), channel_id=1, source_target_pairs={{8,0},{9,1},{26,2},{27,3},{40,4},{41,5},{58,6},{59,7},{72,8},{73,9... | collective-permute-start | bytes 294920 | tf_op jit(solution)/shard_map/ppermute | solution.py:452
  72.9 10.1 %collective-permute-done.1.near_first = f32[32,768]{1,0:T(8,128)S(1)} collective-permute-done((f32[32,768]{1,0:T(8,128)S(1)}, f32[32,768]{1,0:T(8,128)S(1)}, u32[]{:S(2)}, u32[]{:S(2)}) %collective-permute-start.1) | collective-permute-done | bytes 98336 | tf_op jit(solution)/shard_map/ppermute | solution.py:452
  83.1 0.0 all-to-all-done.3
  83.1 0.0 copy-done
  83.1 0.0 copy-done.1
  83.1 1.5 %shard_map.97 = f32[3,32,256]{2,1,0:T(8,128)} custom-call(f32[1,128]{1,0:T(1,128)S(1)} %get-tuple-element.21.back, f32[128,896]{1,0:T(8,128)S(1)} %bitcast.24, f32[32,768]{1,0:T(8,128)S(1)} %collective-permute-done.1.near_first, bf16[1024,768]{1,0:T(8,128)(2,1)S(1)} %bitcast.19, f32[1024,32]{1,0:T(8,128)S(1)} %bitcast.23), custom_call_target="tpu_custom_call" | custom-call | tf_op jit(solution)/shard_map/pallas_call | solution.py:381
  (3 shorter events, 0.1 us)
Async XLA Ops:
  0.0 4.8 %copy-start.2 = (bf16[32,3,256]{2,0,1:T(8,128)(2,1)S(1)}, bf16[32,3,256]{2,0,1:T(8,128)(2,1)}, u32[]{:S(2)}) copy-start(bf16[32,3,256]{2,0,1:T(8,128)(2,1)} %param.9) | copy-start | bytes 147460
  0.0 4.8 %copy-start.3 = (bf16[32,3,256]{2,0,1:T(8,128)(2,1)S(1)}, bf16[32,3,256]{2,0,1:T(8,128)(2,1)}, u32[]{:S(2)}) copy-start(bf16[32,3,256]{2,0,1:T(8,128)(2,1)} %param.10) | copy-start | bytes 147460
  0.7 25.7 %copy-start.5 = (s32[4096]{0:T(1024)S(1)}, s32[4096]{0:T(1024)}, u32[]{:S(2)}) copy-start(s32[4096]{0:T(1024)} %param.13) | copy-start | bytes 49156
  4.8 22.2 %copy-start.6 = (s32[2,64]{1,0:T(2,128)S(1)}, s32[2,64]{1,0:T(2,128)}, u32[]{:S(2)}) copy-start(s32[2,64]{1,0:T(2,128)} %param.16) | copy-start | bytes 1540
  4.8 22.3 %copy-start.4 = (f32[64,32,32]{0,2,1:T(8,128)S(1)}, f32[64,32,32]{0,2,1:T(8,128)}, u32[]{:S(2)}) copy-start(f32[64,32,32]{0,2,1:T(8,128)} %param.17) | copy-start | bytes 786436
  4.8 15.4 %collective-permute-start = (bf16[32,1536]{1,0:T(8,128)(2,1)S(1)}, bf16[32,1536]{1,0:T(8,128)(2,1)S(1)}, u32[]{:S(2)}, u32[]{:S(2)}) collective-permute-start(bf16[32,1536]{1,0:T(8,128)(2,1)S(1)} %shard_map.92.data), channel_id=1, source_target_pairs={{0,8},{1,9},{2,26},{3,27},{4,40},{5,41},{6,58},{7,59},{8,72},{9,73... | collective-permute-start | bytes 294920 | tf_op jit(solution)/shard_map/ppermute | solution.py:422
  12.3 7.9 %all-to-all-start = ((f32[8,10,128]{2,1,0:T(8,128)}), f32[8,10,128]{2,1,0:T(8,128)S(1)}, u32[]{:S(2)}, u32[]{:S(2)}) async-start(f32[8,10,128]{2,1,0:T(8,128)} %shard_map.91), calls=%async_computation | async-start | bytes 131072 | tf_op jit(solution)/shard_map/all_to_all | solution.py:420
  21.9 16.4 %all-to-all-start.1 = ((bf16[16,8,2688]{2,1,0:T(8,128)(2,1)}), bf16[16,8,2688]{2,1,0:T(8,128)(2,1)S(1)}, u32[]{:S(2)}, u32[]{:S(2)}) async-start(bf16[16,8,2688]{2,1,0:T(8,128)(2,1)} %bitcast.7), calls=%async_computation.1 | async-start | bytes 1376256 | tf_op jit(solution)/shard_map/all_to_all | solution.py:429
  40.2 23.2 %all-to-all-start.2 = ((f32[8,128,128]{2,1,0:T(8,128)}), f32[8,128,128]{2,1,0:T(8,128)S(1)}, u32[]{:S(2)}, u32[]{:S(2)}) async-start(f32[8,128,128]{2,1,0:T(8,128)} %bitcast.11), calls=%async_computation.2 | async-start | bytes 1048576 | tf_op jit(solution)/shard_map/all_to_all | solution.py:449
  63.4 19.7 %copy-start = (bf16[32,32,768]{2,1,0:T(8,128)(2,1)S(1)}, bf16[32,32,768]{2,1,0:T(8,128)(2,1)}, u32[]{:S(2)}) copy-start(bf16[32,32,768]{2,1,0:T(8,128)(2,1)} %param.11) | copy-start | bytes 4718596
  63.4 19.7 %copy-start.1 = (f32[32,32,32]{2,1,0:T(8,128)S(1)}, f32[32,32,32]{2,1,0:T(8,128)}, u32[]{:S(2)}) copy-start(f32[32,32,32]{2,1,0:T(8,128)} %param.12) | copy-start | bytes 393220
  64.3 18.8 %all-to-all-start.3 = ((f32[16,8,896]{2,1,0:T(8,128)}), f32[16,8,896]{2,1,0:T(8,128)S(1)}, u32[]{:S(2)}, u32[]{:S(2)}) async-start(f32[16,8,896]{2,1,0:T(8,128)} %maximum_bitcast_fusion), calls=%async_computation.3 | async-start | bytes 917504 | tf_op jit(solution)/shard_map/all_to_all | solution.py:453
  67.9 15.2 %collective-permute-start.1 = (f32[32,768]{1,0:T(8,128)S(1)}, f32[32,768]{1,0:T(8,128)S(1)}, u32[]{:S(2)}, u32[]{:S(2)}) collective-permute-start(f32[32,768]{1,0:T(8,128)S(1)} %get-tuple-element.28), channel_id=1, source_target_pairs={{8,0},{9,1},{26,2},{27,3},{40,4},{41,5},{58,6},{59,7},{72,8},{73,9... | collective-permute-start | bytes 294920 | tf_op jit(solution)/shard_map/ppermute | solution.py:452

commit v11 on v10

--- a/solution.py
+++ b/solution.py
@@ -85,7 +85,9 @@
     return out
 
 
-def near_kernel(ids_lane, first_ref, second_ref, near_first, to_second, field_a, left, field_b, right, sums_a, sums_b):
+def near_kernel(
+    ids_lane, first_ref, second_ref, near_first, out_hbm, to_second, field_a, left, field_b, right, sums_a, sums_b, sem
+):
     own = first_ref.shape[0]
     near_first[...] = jnp.zeros_like(near_first)
 
@@ -132,6 +134,7 @@
 
         for i, value in enumerate(finish(second, sums_b)):
             to_second[rows, i * PANELS : (i + 1) * PANELS] = value
+        pltpu.make_async_copy(to_second.at[rows], out_hbm.at[rows, pl.ds(0, 3 * PANELS)], sem).start()
         for i, value in enumerate(finish(first, sums_a)):
             for piece in pieces(value, 3):
                 near_first[:, i * PANELS : (i + 1) * PANELS] += lax.dot_general(
@@ -140,6 +143,7 @@
         return carry
 
     lax.fori_loop(0, second_ref.shape[0] // GROUP, group, 0)
+    pltpu.make_async_copy(to_second, out_hbm.at[:, pl.ds(0, 3 * PANELS)], sem).wait()
 
 
 def near_sums(first, second, ids_lane):
@@ -153,11 +157,14 @@
         functools.partial(near_kernel, ids_lane),
         out_shape=[
             jax.ShapeDtypeStruct((first.shape[0], 3 * PANELS), f32),
-            jax.ShapeDtypeStruct((slots, 3 * PANELS), f32),
+            jax.ShapeDtypeStruct((slots, 3 * PANELS + 128), f32),
         ],
         in_specs=[vmem] * 2,
-        out_specs=[vmem] * 2,
-        scratch_shapes=[rows(FIELD_ROWS), rows(POINT_ROWS)] * 2 + [rows(FIELD_ROWS)] * 2,
+        out_specs=[vmem, pl.BlockSpec(memory_space=pltpu.HBM)],
+        scratch_shapes=[pltpu.VMEM((slots, 3 * PANELS), f32)]
+        + [rows(FIELD_ROWS), rows(POINT_ROWS)] * 2
+        + [rows(FIELD_ROWS)] * 2
+        + [pltpu.SemaphoreType.DMA],
         compiler_params=pltpu.CompilerParams(vmem_limit_bytes=32 << 20),
         cost_estimate=pl.CostEstimate(
             flops=slots * 2 * 2 * 64 * PANELS * PANELS, bytes_accessed=slots * 9216, transcendentals=0
@@ -171,7 +178,7 @@
         hits[:, m * count : (m + 1) * count] = (parents[:, m : m + 1] == ends[...]).astype(f32).astype(bf16)
 
 
-def far_kernel(start, recv, hits, factors, out):
+def far_kernel(start, recv, hits, factors, out_hbm, out, sems):
     count = factors.shape[2]
     parts = hits.shape[1] // count
     rank = 128 // parts
@@ -193,13 +200,16 @@
         for piece in pieces(sent, 2)
         for m in range(parts)
     ]
-    both = lax.dot_general(
-        hits[...],
-        jnp.concatenate(table, axis=0).astype(bf16),
-        (((1,), (1,)), ((), ())),
-        preferred_element_type=f32,
-    )
-    out[...] = both[:, :128] + both[:, 128:]
+    table = jnp.concatenate(table, axis=0).astype(bf16)
+    copies = []
+    for k in range(0, out.shape[0], 256):
+        rows = pl.ds(k, 256)
+        both = lax.dot_general(hits[rows, :], table, (((1,), (1,)), ((), ())), preferred_element_type=f32)
+        out[rows, :] = both[:, :128] + both[:, 128:]
+        copies.append(pltpu.make_async_copy(out.at[rows], out_hbm.at[rows], sems.at[len(copies)]))
+        copies[-1].start()
+    for copy in copies:
+        copy.wait()
 
 
 def own_lanes(own, rank):
@@ -226,20 +236,19 @@
     )(density.transpose(1, 0, 2), coords.transpose(1, 0, 2))
 
 
-def start_kernel(count, pairs, density_hbm, basis_hbm, transfer_hbm, message, density, basis, transfer, sems):
+def start_kernel(
+    count_hbm, pairs_hbm, density_hbm, basis_hbm, transfer_hbm, message, count, pairs, density, basis, transfer, sems
+):
     own, rank = density.shape[1], transfer.shape[1]
     step = 256
     chunks = [pl.ds(k, step) for k in range(0, own * rank, step)]
-    sources = [density_hbm] + [basis_hbm.at[c] for c in chunks] + [transfer_hbm]
-    targets = [density] + [basis.at[c] for c in chunks] + [transfer]
+    sources = [density_hbm] + [basis_hbm.at[c] for c in chunks] + [transfer_hbm, count_hbm, pairs_hbm]
+    targets = [density] + [basis.at[c] for c in chunks] + [transfer, count, pairs]
     copies = [pltpu.make_async_copy(a, b, sems.at[k]) for k, (a, b) in enumerate(zip(sources, targets))]
     for copy in copies:
         copy.start()
     mine = own_lanes(own, rank)
     across = (((1,), (1,)), ((), ()))
-    ids = lax.rem(pairs[...], own)
-    live = lax.broadcasted_iota(jnp.int32, ids.shape, 1) < count[0]
-    ids = jnp.where(live, ids, -1).astype(f32)
     copies[0].wait()
     flat = jnp.concatenate([density[i] for i in range(3)], axis=1)
     folded = jnp.zeros((own, 128), f32)
@@ -249,7 +258,7 @@
         every = jnp.where(mine[:, k * step : (k + 1) * step], every, 0.0)
         folded += sum(every[:, m : m + 128] for m in range(0, step, 128))
     moments = sum(folded[:, k : k + rank] for k in range(0, 128, rank))
-    copies[-1].wait()
+    copies[-3].wait()
     wide = jnp.concatenate(pieces(moments, 3), axis=0).astype(bf16)
     lifted = sum(
         lax.dot_general(wide, piece.astype(bf16), across, preferred_element_type=f32)
@@ -258,6 +267,11 @@
     lifted = lifted[:own] + lifted[own : 2 * own] + lifted[2 * own :]
     lifted = jnp.sum(jnp.where(mine, lifted, 0.0), axis=0, keepdims=True)
     lifted = jnp.concatenate([lifted[:, k : k + 128] for k in range(0, own * rank, 128)], axis=0)
+    copies[-2].wait()
+    copies[-1].wait()
+    ids = lax.rem(pairs[...], own)
+    live = lax.broadcasted_iota(jnp.int32, ids.shape, 1) < count[0, 0]
+    ids = jnp.where(live, ids, -1).astype(f32)
     rows = message.shape[0]
     block = ids.shape[1] // rows
     for k in range(rows):
@@ -271,17 +285,19 @@
     return pl.pallas_call(
         start_kernel,
         out_shape=jax.ShapeDtypeStruct((rows, own * rank // 128 + 2, near_pairs.shape[1]), f32),
-        in_specs=[pl.BlockSpec(memory_space=pltpu.SMEM), vmem] + [hbm] * 3,
+        in_specs=[hbm] * 5,
         out_specs=vmem,
         scratch_shapes=[
+            pltpu.SMEM((1, 1), jnp.int32),
+            pltpu.VMEM(near_pairs.shape, jnp.int32),
             pltpu.VMEM((3, own, width // 3), density.dtype),
             pltpu.VMEM((own * rank, width), basis.dtype),
             pltpu.VMEM((own * rank, rank), f32),
-            pltpu.SemaphoreType.DMA((own * rank // 256 + 2,)),
+            pltpu.SemaphoreType.DMA((own * rank // 256 + 4,)),
         ],
         compiler_params=pltpu.CompilerParams(vmem_limit_bytes=60 << 20),
     )(
-        near_count,
+        near_count.reshape(1, 1),
         near_pairs,
         density.transpose(1, 0, 2),
         basis.reshape(own * rank, width),
@@ -442,7 +458,8 @@
         functools.partial(far_kernel, ids_lane + 128),
         out_shape=jax.ShapeDtypeStruct((rows * slots, 128), f32),
         in_specs=[vmem] * 3,
-        out_specs=vmem,
+        out_specs=pl.BlockSpec(memory_space=pltpu.HBM),
+        scratch_shapes=[pltpu.VMEM((rows * slots, 128), f32), pltpu.SemaphoreType.DMA((rows * slots // 256,))],
         compiler_params=pltpu.CompilerParams(vmem_limit_bytes=16 << 20),
     )(second, hits, factors)
     first_data, partial = lax.optimization_barrier((first_data, partial))
@@ -450,9 +467,8 @@
 
     near_first, to_second = near_sums(first_data, second, ids_lane)
     near_first = lax.ppermute(near_first, BOTH, home)
-    returned = lax.all_to_all(
-        jnp.concatenate([to_second, row_locals.sum(axis=0)], axis=1), "col", 0, 0, tiled=True
-    )
+    message = lax.dynamic_update_slice(to_second, row_locals.sum(axis=0), (0, 3 * panels))
+    returned = lax.all_to_all(message, "col", 0, 0, tiled=True)
     return end(back_ids, returned, near_first, basis, transfer)
 
 

time: 85.2 us -> 84.4 us (level)
  transfers between devices with their start and end apart: 6 -> 6, of which waited for: 3 -> 3; matrix products, arithmetic and copies ran while one was open for 1% -> 1% of each run, Pallas kernels for 21% -> 22%
where the time goes in v11:
time: 84.4 us; the launch traced here: 83.9 us
  starting transfers between devices  29.5 us (35%)
  Pallas kernels  26.8 us (32%)
  waiting for transfers between devices  24.8 us (29%)
  local copies, waits for them, and re-layouts  1.62 us (2%)
    pallas_call x1, Pallas kernels, near_sums(): pl.pallas_call(functools.partial(near_kernel, ids_lane), out_shape=[jax.S...  17.7 us
    all_to_all x1, waiting for transfers between devices, shards(): second = lax.all_to_all(message, 'col', 0, 0, tiled=True)  10.2 us
    ppermute x1, waiting for transfers between devices, shards(): near_first = lax.ppermute(near_first, BOTH, home)  10.1 us
    ppermute x1, starting transfers between devices, shards(): first_data = lax.ppermute(data, BOTH, swap)  7.52 us
    all_to_all x1, starting transfers between devices, shards(): lax.all_to_all(partial.reshape(rows, slots, 128), 'row', 0, 0, tiled=True)  5.64 us
    ppermute x1, starting transfers between devices, shards(): near_first = lax.ppermute(near_first, BOTH, home)  5.1 us
    all_to_all x1, waiting for transfers between devices, shards(): from_row = lax.all_to_all(message, 'row', 0, 0, tiled=True)  4.47 us
    all_to_all x1, starting transfers between devices, shards(): second = lax.all_to_all(message, 'col', 0, 0, tiled=True)  4.42 us
  transfers between devices with their start and end apart: 6, of which 3 were waited for; matrix products, arithmetic and copies ran while one was open for 1% of the time, Pallas kernels for 22%

profile of v11, /device:TPU:1, one launch (start us, length us, event | category | flops | bytes accessed | tf_op | source)
XLA Modules:
  0.0 83.9 jit_solution(12423825414798661710)
XLA Ops:
  0.0 0.0 copy-start.2
  0.0 0.0 copy-start.3
  0.7 0.0 copy-start.5
  0.7 3.5 %shard_map.91 = f32[8,10,128]{2,1,0:T(8,128)} custom-call(s32[1,1]{1,0:T(1,128)} %bitcast.18.count_hbm, s32[2,128]{1,0:T(2,128)} %pairs_hbm.1, bf16[3,32,256]{2,1,0:T(8,128)(2,1)} %bitcast.26, bf16[1024,768]{1,0:T(8,128)(2,1)} %bitcast.19, f32[1024,32]{1,0:T(8,128)} %bitcast.23), custom_call_target="tpu_custom_call" | custom-call | tf_op jit(solution)/shard_map/pallas_call | solution.py:285
  4.2 0.0 copy-start.6
  4.2 0.0 copy-start.4
  4.2 0.0 copy-done.2
  4.2 0.0 copy-done.3
  4.2 7.5 %collective-permute-start = (bf16[32,1536]{1,0:T(8,128)(2,1)S(1)}, bf16[32,1536]{1,0:T(8,128)(2,1)S(1)}, u32[]{:S(2)}, u32[]{:S(2)}) collective-permute-start(bf16[32,1536]{1,0:T(8,128)(2,1)S(1)} %shard_map.92.data), channel_id=1, source_target_pairs={{0,8},{1,9},{2,26},{3,27},{4,40},{5,41},{6,58},{7,59},{8,72},{9,73... | collective-permute-start | bytes 294920 | tf_op jit(solution)/shard_map/ppermute | solution.py:438
  11.8 3.3 %all-to-all-start = ((f32[8,10,128]{2,1,0:T(8,128)}), f32[8,10,128]{2,1,0:T(8,128)S(1)}, u32[]{:S(2)}, u32[]{:S(2)}) async-start(f32[8,10,128]{2,1,0:T(8,128)} %shard_map.91), calls=%async_computation | async-start | bytes 131072 | tf_op jit(solution)/shard_map/all_to_all | solution.py:436
  15.1 0.1 pad_add_fusion.place
  15.2 4.5 %all-to-all-done.from_row = f32[8,10,128]{2,1,0:T(8,128)S(1)} async-done(((f32[8,10,128]{2,1,0:T(8,128)}), f32[8,10,128]{2,1,0:T(8,128)S(1)}, u32[]{:S(2)}, u32[]{:S(2)}) %all-to-all-start) | async-done | bytes 40992 | tf_op jit(solution)/shard_map/all_to_all | solution.py:436
  19.6 0.0 collective-permute-done.first_ref
  19.6 1.7 %shard_map.93 = (bf16[128,2688]{1,0:T(8,128)(2,1)}, f32[1,128]{1,0:T(1,128)S(1)}) custom-call(s32[2]{0:T(128)S(1)} %pad_add_fusion.place, f32[8,10,128]{2,1,0:T(8,128)S(1)} %all-to-all-done.from_row, bf16[32,1536]{1,0:T(8,128)(2,1)S(1)} %shard_map.92.data), custom_call_target="tpu_custom_call" | custom-call | tf_op jit(solution)/shard_map/pallas_call | solution.py:354
  21.4 4.4 %all-to-all-start.1 = ((bf16[16,8,2688]{2,1,0:T(8,128)(2,1)}), bf16[16,8,2688]{2,1,0:T(8,128)(2,1)S(1)}, u32[]{:S(2)}, u32[]{:S(2)}) async-start(bf16[16,8,2688]{2,1,0:T(8,128)(2,1)} %bitcast.8), calls=%async_computation.1 | async-start | bytes 1376256 | tf_op jit(solution)/shard_map/all_to_all | solution.py:445
  25.8 0.0 copy-done.5
  25.8 0.5 reshape.27.parents
  26.4 0.0 copy-done.6
  26.4 0.1 reshape.28.ends
  26.5 0.0 copy-done.4
  26.5 0.3 copy.13
  26.8 0.2 pad_maximum_fusion.factors
  27.0 0.6 shard_map.94.hits
  27.6 10.2 %all-to-all-done.1 = bf16[16,8,2688]{2,1,0:T(8,128)(2,1)S(1)} async-done(((bf16[16,8,2688]{2,1,0:T(8,128)(2,1)}), bf16[16,8,2688]{2,1,0:T(8,128)(2,1)S(1)}, u32[]{:S(2)}, u32[]{:S(2)}) %all-to-all-start.1) | async-done | bytes 688160 | tf_op jit(solution)/shard_map/all_to_all | solution.py:445
  37.8 1.8 %shard_map.95 = f32[1024,128]{1,0:T(8,128)} custom-call(bf16[128,2688]{1,0:T(8,128)(2,1)S(1)} %bitcast.21, bf16[1024,512]{1,0:T(8,128)(2,1)S(1)} %shard_map.94.hits, f32[32,32,128]{2,1,0:T(8,128)S(1)} %pad_maximum_fusion.factors), custom_call_target="tpu_custom_call" | custom-call | tf_op jit(solution)/shard_map/pallas_call | solution.py:457
  39.6 5.6 %all-to-all-start.2 = ((f32[8,128,128]{2,1,0:T(8,128)}), f32[8,128,128]{2,1,0:T(8,128)S(1)}, u32[]{:S(2)}, u32[]{:S(2)}) async-start(f32[8,128,128]{2,1,0:T(8,128)} %bitcast.12), calls=%async_computation.2 | async-start | bytes 1048576 | tf_op jit(solution)/shard_map/all_to_all | solution.py:466
  45.2 0.0 copy-start.1
  45.2 17.7 %shard_map.96 = (f32[32,768]{1,0:T(8,128)S(1)}, f32[128,896]{1,0:T(8,128)}) custom-call(bf16[32,1536]{1,0:T(8,128)(2,1)S(1)} %collective-permute-done.first_ref, bf16[128,2688]{1,0:T(8,128)(2,1)S(1)} %bitcast.22), custom_call_target="tpu_custom_call" | custom-call | flops 2147483648 | bytes 1179648 | tf_op jit(solution)/shard_map/pallas_call | solution.py:156
  62.9 0.0 copy-start
  62.9 0.0 all-to-all-done.2
  63.0 0.6 constant_dynamic-update-slice_fusion
  63.6 3.6 %all-to-all-start.3 = ((f32[16,8,896]{2,1,0:T(8,128)}), f32[16,8,896]{2,1,0:T(8,128)S(1)}, u32[]{:S(2)}, u32[]{:S(2)}) async-start(f32[16,8,896]{2,1,0:T(8,128)} %bitcast.13), calls=%async_computation.3 | async-start | bytes 917504 | tf_op jit(solution)/shard_map/all_to_all | solution.py:471
  67.2 5.1 %collective-permute-start.1 = (f32[32,768]{1,0:T(8,128)S(1)}, f32[32,768]{1,0:T(8,128)S(1)}, u32[]{:S(2)}, u32[]{:S(2)}) collective-permute-start(f32[32,768]{1,0:T(8,128)S(1)} %get-tuple-element.28), channel_id=1, source_target_pairs={{8,0},{9,1},{26,2},{27,3},{40,4},{41,5},{58,6},{59,7},{72,8},{73,9... | collective-permute-start | bytes 294920 | tf_op jit(solution)/shard_map/ppermute | solution.py:469
  72.3 10.1 %collective-permute-done.1.near_first = f32[32,768]{1,0:T(8,128)S(1)} collective-permute-done((f32[32,768]{1,0:T(8,128)S(1)}, f32[32,768]{1,0:T(8,128)S(1)}, u32[]{:S(2)}, u32[]{:S(2)}) %collective-permute-start.1) | collective-permute-done | bytes 98336 | tf_op jit(solution)/shard_map/ppermute | solution.py:469
  82.4 0.0 all-to-all-done.3
  82.4 0.0 copy-done.1
  82.4 0.0 copy-done
  82.4 1.5 %shard_map.97 = f32[3,32,256]{2,1,0:T(8,128)} custom-call(f32[1,128]{1,0:T(1,128)S(1)} %get-tuple-element.21.back, f32[128,896]{1,0:T(8,128)S(1)} %bitcast.25, f32[32,768]{1,0:T(8,128)S(1)} %collective-permute-done.1.near_first, bf16[1024,768]{1,0:T(8,128)(2,1)S(1)} %bitcast.20, f32[1024,32]{1,0:T(8,128)S(1)} %bitcast.24), custom_call_target="tpu_custom_call" | custom-call | tf_op jit(solution)/shard_map/pallas_call | solution.py:397
  (3 shorter events, 0.1 us)
Async XLA Ops:
  0.0 4.2 %copy-start.2 = (bf16[32,3,256]{2,0,1:T(8,128)(2,1)S(1)}, bf16[32,3,256]{2,0,1:T(8,128)(2,1)}, u32[]{:S(2)}) copy-start(bf16[32,3,256]{2,0,1:T(8,128)(2,1)} %param.9) | copy-start | bytes 147460
  0.0 4.2 %copy-start.3 = (bf16[32,3,256]{2,0,1:T(8,128)(2,1)S(1)}, bf16[32,3,256]{2,0,1:T(8,128)(2,1)}, u32[]{:S(2)}) copy-start(bf16[32,3,256]{2,0,1:T(8,128)(2,1)} %param.10) | copy-start | bytes 147460
  0.7 25.1 %copy-start.5 = (s32[4096]{0:T(1024)S(1)}, s32[4096]{0:T(1024)}, u32[]{:S(2)}) copy-start(s32[4096]{0:T(1024)} %param.13) | copy-start | bytes 49156
  4.2 22.2 %copy-start.6 = (s32[2,64]{1,0:T(2,128)S(1)}, s32[2,64]{1,0:T(2,128)}, u32[]{:S(2)}) copy-start(s32[2,64]{1,0:T(2,128)} %param.16) | copy-start | bytes 1540
  4.2 22.3 %copy-start.4 = (f32[64,32,32]{0,2,1:T(8,128)S(1)}, f32[64,32,32]{0,2,1:T(8,128)}, u32[]{:S(2)}) copy-start(f32[64,32,32]{0,2,1:T(8,128)} %param.17) | copy-start | bytes 786436
  4.2 15.4 %collective-permute-start = (bf16[32,1536]{1,0:T(8,128)(2,1)S(1)}, bf16[32,1536]{1,0:T(8,128)(2,1)S(1)}, u32[]{:S(2)}, u32[]{:S(2)}) collective-permute-start(bf16[32,1536]{1,0:T(8,128)(2,1)S(1)} %shard_map.92.data), channel_id=1, source_target_pairs={{0,8},{1,9},{2,26},{3,27},{4,40},{5,41},{6,58},{7,59},{8,72},{9,73... | collective-permute-start | bytes 294920 | tf_op jit(solution)/shard_map/ppermute | solution.py:438
  11.8 7.9 %all-to-all-start = ((f32[8,10,128]{2,1,0:T(8,128)}), f32[8,10,128]{2,1,0:T(8,128)S(1)}, u32[]{:S(2)}, u32[]{:S(2)}) async-start(f32[8,10,128]{2,1,0:T(8,128)} %shard_map.91), calls=%async_computation | async-start | bytes 131072 | tf_op jit(solution)/shard_map/all_to_all | solution.py:436
  21.4 16.5 %all-to-all-start.1 = ((bf16[16,8,2688]{2,1,0:T(8,128)(2,1)}), bf16[16,8,2688]{2,1,0:T(8,128)(2,1)S(1)}, u32[]{:S(2)}, u32[]{:S(2)}) async-start(bf16[16,8,2688]{2,1,0:T(8,128)(2,1)} %bitcast.8), calls=%async_computation.1 | async-start | bytes 1376256 | tf_op jit(solution)/shard_map/all_to_all | solution.py:445
  39.6 23.3 %all-to-all-start.2 = ((f32[8,128,128]{2,1,0:T(8,128)}), f32[8,128,128]{2,1,0:T(8,128)S(1)}, u32[]{:S(2)}, u32[]{:S(2)}) async-start(f32[8,128,128]{2,1,0:T(8,128)} %bitcast.12), calls=%async_computation.2 | async-start | bytes 1048576 | tf_op jit(solution)/shard_map/all_to_all | solution.py:466
  45.2 37.2 %copy-start.1 = (f32[32,32,32]{2,1,0:T(8,128)S(1)}, f32[32,32,32]{2,1,0:T(8,128)}, u32[]{:S(2)}) copy-start(f32[32,32,32]{2,1,0:T(8,128)} %param.12) | copy-start | bytes 393220
  62.9 19.5 %copy-start = (bf16[32,32,768]{2,1,0:T(8,128)(2,1)S(1)}, bf16[32,32,768]{2,1,0:T(8,128)(2,1)}, u32[]{:S(2)}) copy-start(bf16[32,32,768]{2,1,0:T(8,128)(2,1)} %param.11) | copy-start | bytes 4718596
  63.6 18.8 %all-to-all-start.3 = ((f32[16,8,896]{2,1,0:T(8,128)}), f32[16,8,896]{2,1,0:T(8,128)S(1)}, u32[]{:S(2)}, u32[]{:S(2)}) async-start(f32[16,8,896]{2,1,0:T(8,128)} %bitcast.13), calls=%async_computation.3 | async-start | bytes 917504 | tf_op jit(solution)/shard_map/all_to_all | solution.py:471
  67.2 15.2 %collective-permute-start.1 = (f32[32,768]{1,0:T(8,128)S(1)}, f32[32,768]{1,0:T(8,128)S(1)}, u32[]{:S(2)}, u32[]{:S(2)}) collective-permute-start(f32[32,768]{1,0:T(8,128)S(1)} %get-tuple-element.28), channel_id=1, source_target_pairs={{8,0},{9,1},{26,2},{27,3},{40,4},{41,5},{58,6},{59,7},{72,8},{73,9... | collective-permute-start | bytes 294920 | tf_op jit(solution)/shard_map/ppermute | solution.py:469

commit v12 on v11

--- a/solution.py
+++ b/solution.py
@@ -85,64 +85,68 @@
     return out
 
 
-def near_kernel(
-    ids_lane, first_ref, second_ref, near_first, out_hbm, to_second, field_a, left, field_b, right, sums_a, sums_b, sem
-):
+def near_kernel(ids_lane, first_ref, second_ref, near_first, out_hbm, to_second, sem, *scratch):
     own = first_ref.shape[0]
     near_first[...] = jnp.zeros_like(near_first)
-
-    def group(g, carry):
-        rows = pl.ds(pl.multiple_of(g * GROUP, GROUP), GROUP)
-        ids = second_ref[rows, ids_lane : ids_lane + 128].astype(f32)[:, :own]
-        chosen = (ids == lax.broadcasted_iota(jnp.int32, (GROUP, own), 1).astype(f32)).astype(bf16)
-        first = jnp.dot(chosen, first_ref[...], preferred_element_type=f32)
-        second = second_ref[rows, : 6 * PANELS].astype(f32)
-        prepare_source(first, field_a, left)
-        prepare_source(second, field_b, None)
-        prepare_target(second, right)
-
-        def load(ref, count, s):
-            parts = [ref[half, pl.ds(s, count, stride=GROUP), :] for half in range(2)]
-            return jnp.concatenate(parts, 1).astype(bf16)
-
-        def apply(field, cube, dim, sums, s):
-            total = lax.dot_general(
-                load(field, FIELD_ROWS, s), cube, (((1,), (dim,)), ((), ())), preferred_element_type=f32
-            )
-            for half in range(2):
-                sums[half, pl.ds(s, FIELD_ROWS, stride=GROUP), :] = total[:, half * 128 : (half + 1) * 128]
-
-        for start in range(0, GROUP, BATCH):
-            batch = range(start, start + BATCH)
-            shifted = [
-                lax.dot_general(
-                    load(left, POINT_ROWS, s),
-                    load(right, POINT_ROWS, s),
-                    (((0,), (0,)), ((), ())),
-                    preferred_element_type=f32,
-                )
-                for s in batch
-            ]
-            cubes = []
-            for value in shifted:
-                inv = lax.rsqrt(value)
-                cubes.append((inv * inv * inv).astype(bf16))
-            for s, cube in zip(batch, cubes):
-                apply(field_a, cube, 0, sums_b, s)
-            for s, cube in zip(batch, cubes):
-                apply(field_b, cube, 1, sums_a, s)
-
-        for i, value in enumerate(finish(second, sums_b)):
-            to_second[rows, i * PANELS : (i + 1) * PANELS] = value
-        pltpu.make_async_copy(to_second.at[rows], out_hbm.at[rows, pl.ds(0, 3 * PANELS)], sem).start()
-        for i, value in enumerate(finish(first, sums_a)):
-            for piece in pieces(value, 3):
-                near_first[:, i * PANELS : (i + 1) * PANELS] += lax.dot_general(
-                    chosen, piece.astype(bf16), (((0,), (0,)), ((), ())), preferred_element_type=f32
-                )
+    sets = scratch[: len(scratch) // 2], scratch[len(scratch) // 2 :]
+
+    def load(ref, count, s):
+        parts = [ref[half, pl.ds(s, count, stride=GROUP), :] for half in range(2)]
+        return jnp.concatenate(parts, 1).astype(bf16)
+
+    def apply(field, cube, dim, sums, s):
+        total = lax.dot_general(
+            load(field, FIELD_ROWS, s), cube, (((1,), (dim,)), ((), ())), preferred_element_type=f32
+        )
+        for half in range(2):
+            sums[half, pl.ds(s, FIELD_ROWS, stride=GROUP), :] = total[:, half * 128 : (half + 1) * 128]
+
+    def two_groups(g, carry):
+        begun = []
+        for k, (field_a, left, field_b, right, _, _) in enumerate(sets):
+            rows = pl.ds(pl.multiple_of((2 * g + k) * GROUP, GROUP), GROUP)
+            ids = second_ref[rows, ids_lane : ids_lane + 128].astype(f32)[:, :own]
+            chosen = (ids == lax.broadcasted_iota(jnp.int32, (GROUP, own), 1).astype(f32)).astype(bf16)
+            first = jnp.dot(chosen, first_ref[...], preferred_element_type=f32)
+            second = second_ref[rows, : 6 * PANELS].astype(f32)
+            prepare_source(first, field_a, left)
+            prepare_source(second, field_b, None)
+            prepare_target(second, right)
+            begun.append((rows, chosen, first, second))
+
+        for field_a, left, field_b, right, sums_a, sums_b in sets:
+            for start in range(0, GROUP, BATCH):
+                batch = range(start, start + BATCH)
+                shifted = [
+                    lax.dot_general(
+                        load(left, POINT_ROWS, s),
+                        load(right, POINT_ROWS, s),
+                        (((0,), (0,)), ((), ())),
+                        preferred_element_type=f32,
+                    )
+                    for s in batch
+                ]
+                cubes = []
+                for value in shifted:
+                    inv = lax.rsqrt(value)
+                    cubes.append((inv * inv * inv).astype(bf16))
+                for s, cube in zip(batch, cubes):
+                    apply(field_a, cube, 0, sums_b, s)
+                for s, cube in zip(batch, cubes):
+                    apply(field_b, cube, 1, sums_a, s)
+
+        for (rows, chosen, first, second), (*_, sums_a, sums_b) in zip(begun, sets):
+            for i, value in enumerate(finish(second, sums_b)):
+                to_second[rows, i * PANELS : (i + 1) * PANELS] = value
+            pltpu.make_async_copy(to_second.at[rows], out_hbm.at[rows, pl.ds(0, 3 * PANELS)], sem).start()
+            for i, value in enumerate(finish(first, sums_a)):
+                for piece in pieces(value, 3):
+                    near_first[:, i * PANELS : (i + 1) * PANELS] += lax.dot_general(
+                        chosen, piece.astype(bf16), (((0,), (0,)), ((), ())), preferred_element_type=f32
+                    )
         return carry
 
-    lax.fori_loop(0, second_ref.shape[0] // GROUP, group, 0)
+    lax.fori_loop(0, second_ref.shape[0] // (2 * GROUP), two_groups, 0)
     pltpu.make_async_copy(to_second, out_hbm.at[:, pl.ds(0, 3 * PANELS)], sem).wait()
 
 
@@ -161,10 +165,8 @@
         ],
         in_specs=[vmem] * 2,
         out_specs=[vmem, pl.BlockSpec(memory_space=pltpu.HBM)],
-        scratch_shapes=[pltpu.VMEM((slots, 3 * PANELS), f32)]
-        + [rows(FIELD_ROWS), rows(POINT_ROWS)] * 2
-        + [rows(FIELD_ROWS)] * 2
-        + [pltpu.SemaphoreType.DMA],
+        scratch_shapes=[pltpu.VMEM((slots, 3 * PANELS), f32), pltpu.SemaphoreType.DMA]
+        + ([rows(FIELD_ROWS), rows(POINT_ROWS)] * 2 + [rows(FIELD_ROWS)] * 2) * 2,
         compiler_params=pltpu.CompilerParams(vmem_limit_bytes=32 << 20),
         cost_estimate=pl.CostEstimate(
             flops=slots * 2 * 2 * 64 * PANELS * PANELS, bytes_accessed=slots * 9216, transcendentals=0

time: 84.4 us -> 82.6 us (0.979)
  Pallas kernels: 26.8 us -> 25 us
    pallas_call x1, Pallas kernels: 17.7 us -> 15.9 us  [near_sums(): pl.pallas_call(functools.partial(near_kernel, ids_lane), out_shape=[jax.S...]
  transfers between devices with their start and end apart: 6 -> 6, of which waited for: 3 -> 3; matrix products, arithmetic and copies ran while one was open for 1% -> 1% of each run, Pallas kernels for 22% -> 20%
where the time goes in v12:
time: 82.6 us; the launch traced here: 82.1 us
  starting transfers between devices  29.5 us (36%)
  Pallas kernels  25 us (30%)
  waiting for transfers between devices  24.8 us (30%)
  local copies, waits for them, and re-layouts  1.62 us (2%)
  between operations  0.84 us (1%)
    pallas_call x1, Pallas kernels, near_sums(): pl.pallas_call(functools.partial(near_kernel, ids_lane), out_shape=[jax.S...  15.9 us
    all_to_all x1, waiting for transfers between devices, shards(): second = lax.all_to_all(message, 'col', 0, 0, tiled=True)  10.2 us
    ppermute x1, waiting for transfers between devices, shards(): near_first = lax.ppermute(near_first, BOTH, home)  10.1 us
    ppermute x1, starting transfers between devices, shards(): first_data = lax.ppermute(data, BOTH, swap)  7.52 us
    all_to_all x1, starting transfers between devices, shards(): lax.all_to_all(partial.reshape(rows, slots, 128), 'row', 0, 0, tiled=True)  5.64 us
    ppermute x1, starting transfers between devices, shards(): near_first = lax.ppermute(near_first, BOTH, home)  5.09 us
    all_to_all x1, waiting for transfers between devices, shards(): from_row = lax.all_to_all(message, 'row', 0, 0, tiled=True)  4.47 us
    all_to_all x1, starting transfers between devices, shards(): second = lax.all_to_all(message, 'col', 0, 0, tiled=True)  4.42 us
  transfers between devices with their start and end apart: 6, of which 3 were waited for; matrix products, arithmetic and copies ran while one was open for 1% of the time, Pallas kernels for 20%

profile of v12, /device:TPU:1, one launch (start us, length us, event | category | flops | bytes accessed | tf_op | source)
XLA Modules:
  0.0 82.1 jit_solution(9854702173446932313)
XLA Ops:
  0.0 0.0 copy-start.2
  0.0 0.0 copy-start.3
  0.7 0.0 copy-start.5
  0.7 3.5 %shard_map.91 = f32[8,10,128]{2,1,0:T(8,128)} custom-call(s32[1,1]{1,0:T(1,128)} %bitcast.18.count_hbm, s32[2,128]{1,0:T(2,128)} %pairs_hbm.1, bf16[3,32,256]{2,1,0:T(8,128)(2,1)} %bitcast.26, bf16[1024,768]{1,0:T(8,128)(2,1)} %bitcast.19, f32[1024,32]{1,0:T(8,128)} %bitcast.23), custom_call_target="tpu_custom_call" | custom-call | tf_op jit(solution)/shard_map/pallas_call | solution.py:287
  4.2 0.0 copy-start.6
  4.2 0.0 copy-start.4
  4.2 0.0 copy-done.2
  4.2 0.0 copy-done.3
  4.2 7.5 %collective-permute-start = (bf16[32,1536]{1,0:T(8,128)(2,1)S(1)}, bf16[32,1536]{1,0:T(8,128)(2,1)S(1)}, u32[]{:S(2)}, u32[]{:S(2)}) collective-permute-start(bf16[32,1536]{1,0:T(8,128)(2,1)S(1)} %shard_map.92.data), channel_id=1, source_target_pairs={{0,8},{1,9},{2,26},{3,27},{4,40},{5,41},{6,58},{7,59},{8,72},{9,73... | collective-permute-start | bytes 294920 | tf_op jit(solution)/shard_map/ppermute | solution.py:440
  11.8 3.3 %all-to-all-start = ((f32[8,10,128]{2,1,0:T(8,128)}), f32[8,10,128]{2,1,0:T(8,128)S(1)}, u32[]{:S(2)}, u32[]{:S(2)}) async-start(f32[8,10,128]{2,1,0:T(8,128)} %shard_map.91), calls=%async_computation | async-start | bytes 131072 | tf_op jit(solution)/shard_map/all_to_all | solution.py:438
  15.1 0.1 pad_add_fusion.place
  15.2 4.5 %all-to-all-done.from_row = f32[8,10,128]{2,1,0:T(8,128)S(1)} async-done(((f32[8,10,128]{2,1,0:T(8,128)}), f32[8,10,128]{2,1,0:T(8,128)S(1)}, u32[]{:S(2)}, u32[]{:S(2)}) %all-to-all-start) | async-done | bytes 40992 | tf_op jit(solution)/shard_map/all_to_all | solution.py:438
  19.6 0.0 collective-permute-done.first_ref
  19.6 1.7 %shard_map.93 = (bf16[128,2688]{1,0:T(8,128)(2,1)}, f32[1,128]{1,0:T(1,128)S(1)}) custom-call(s32[2]{0:T(128)S(1)} %pad_add_fusion.place, f32[8,10,128]{2,1,0:T(8,128)S(1)} %all-to-all-done.from_row, bf16[32,1536]{1,0:T(8,128)(2,1)S(1)} %shard_map.92.data), custom_call_target="tpu_custom_call" | custom-call | tf_op jit(solution)/shard_map/pallas_call | solution.py:356
  21.4 4.4 %all-to-all-start.1 = ((bf16[16,8,2688]{2,1,0:T(8,128)(2,1)}), bf16[16,8,2688]{2,1,0:T(8,128)(2,1)S(1)}, u32[]{:S(2)}, u32[]{:S(2)}) async-start(bf16[16,8,2688]{2,1,0:T(8,128)(2,1)} %bitcast.8), calls=%async_computation.1 | async-start | bytes 1376256 | tf_op jit(solution)/shard_map/all_to_all | solution.py:447
  25.8 0.0 copy-done.5
  25.8 0.5 reshape.27.parents
  26.4 0.0 copy-done.6
  26.4 0.1 reshape.28.ends
  26.5 0.0 copy-done.4
  26.5 0.3 copy.13
  26.8 0.2 pad_maximum_fusion.factors
  27.0 0.6 shard_map.94.hits
  27.6 10.2 %all-to-all-done.1 = bf16[16,8,2688]{2,1,0:T(8,128)(2,1)S(1)} async-done(((bf16[16,8,2688]{2,1,0:T(8,128)(2,1)}), bf16[16,8,2688]{2,1,0:T(8,128)(2,1)S(1)}, u32[]{:S(2)}, u32[]{:S(2)}) %all-to-all-start.1) | async-done | bytes 688160 | tf_op jit(solution)/shard_map/all_to_all | solution.py:447
  37.8 1.8 %shard_map.95 = f32[1024,128]{1,0:T(8,128)} custom-call(bf16[128,2688]{1,0:T(8,128)(2,1)S(1)} %bitcast.21, bf16[1024,512]{1,0:T(8,128)(2,1)S(1)} %shard_map.94.hits, f32[32,32,128]{2,1,0:T(8,128)S(1)} %pad_maximum_fusion.factors), custom_call_target="tpu_custom_call" | custom-call | tf_op jit(solution)/shard_map/pallas_call | solution.py:459
  39.6 5.6 %all-to-all-start.2 = ((f32[8,128,128]{2,1,0:T(8,128)}), f32[8,128,128]{2,1,0:T(8,128)S(1)}, u32[]{:S(2)}, u32[]{:S(2)}) async-start(f32[8,128,128]{2,1,0:T(8,128)} %bitcast.12), calls=%async_computation.2 | async-start | bytes 1048576 | tf_op jit(solution)/shard_map/all_to_all | solution.py:468
  45.2 0.0 copy-start.1
  45.2 15.9 %shard_map.96 = (f32[32,768]{1,0:T(8,128)S(1)}, f32[128,896]{1,0:T(8,128)}) custom-call(bf16[32,1536]{1,0:T(8,128)(2,1)S(1)} %collective-permute-done.first_ref, bf16[128,2688]{1,0:T(8,128)(2,1)S(1)} %bitcast.22), custom_call_target="tpu_custom_call" | custom-call | flops 2147483648 | bytes 1179648 | tf_op jit(solution)/shard_map/pallas_call | solution.py:160
  61.1 0.0 copy-start
  61.1 0.0 all-to-all-done.2
  61.2 0.6 constant_dynamic-update-slice_fusion
  61.8 3.6 %all-to-all-start.3 = ((f32[16,8,896]{2,1,0:T(8,128)}), f32[16,8,896]{2,1,0:T(8,128)S(1)}, u32[]{:S(2)}, u32[]{:S(2)}) async-start(f32[16,8,896]{2,1,0:T(8,128)} %bitcast.13), calls=%async_computation.3 | async-start | bytes 917504 | tf_op jit(solution)/shard_map/all_to_all | solution.py:473
  65.4 5.1 %collective-permute-start.1 = (f32[32,768]{1,0:T(8,128)S(1)}, f32[32,768]{1,0:T(8,128)S(1)}, u32[]{:S(2)}, u32[]{:S(2)}) collective-permute-start(f32[32,768]{1,0:T(8,128)S(1)} %get-tuple-element.28), channel_id=1, source_target_pairs={{8,0},{9,1},{26,2},{27,3},{40,4},{41,5},{58,6},{59,7},{72,8},{73,9... | collective-permute-start | bytes 294920 | tf_op jit(solution)/shard_map/ppermute | solution.py:471
  70.5 10.1 %collective-permute-done.1.near_first = f32[32,768]{1,0:T(8,128)S(1)} collective-permute-done((f32[32,768]{1,0:T(8,128)S(1)}, f32[32,768]{1,0:T(8,128)S(1)}, u32[]{:S(2)}, u32[]{:S(2)}) %collective-permute-start.1) | collective-permute-done | bytes 98336 | tf_op jit(solution)/shard_map/ppermute | solution.py:471
  80.6 0.0 all-to-all-done.3
  80.6 0.0 copy-done.1
  80.6 0.0 copy-done
  80.6 1.5 %shard_map.97 = f32[3,32,256]{2,1,0:T(8,128)} custom-call(f32[1,128]{1,0:T(1,128)S(1)} %get-tuple-element.21.back, f32[128,896]{1,0:T(8,128)S(1)} %bitcast.25, f32[32,768]{1,0:T(8,128)S(1)} %collective-permute-done.1.near_first, bf16[1024,768]{1,0:T(8,128)(2,1)S(1)} %bitcast.20, f32[1024,32]{1,0:T(8,128)S(1)} %bitcast.24), custom_call_target="tpu_custom_call" | custom-call | tf_op jit(solution)/shard_map/pallas_call | solution.py:399
  (3 shorter events, 0.1 us)
Async XLA Ops:
  0.0 4.2 %copy-start.2 = (bf16[32,3,256]{2,0,1:T(8,128)(2,1)S(1)}, bf16[32,3,256]{2,0,1:T(8,128)(2,1)}, u32[]{:S(2)}) copy-start(bf16[32,3,256]{2,0,1:T(8,128)(2,1)} %param.9) | copy-start | bytes 147460
  0.0 4.2 %copy-start.3 = (bf16[32,3,256]{2,0,1:T(8,128)(2,1)S(1)}, bf16[32,3,256]{2,0,1:T(8,128)(2,1)}, u32[]{:S(2)}) copy-start(bf16[32,3,256]{2,0,1:T(8,128)(2,1)} %param.10) | copy-start | bytes 147460
  0.7 25.1 %copy-start.5 = (s32[4096]{0:T(1024)S(1)}, s32[4096]{0:T(1024)}, u32[]{:S(2)}) copy-start(s32[4096]{0:T(1024)} %param.13) | copy-start | bytes 49156
  4.2 22.2 %copy-start.6 = (s32[2,64]{1,0:T(2,128)S(1)}, s32[2,64]{1,0:T(2,128)}, u32[]{:S(2)}) copy-start(s32[2,64]{1,0:T(2,128)} %param.16) | copy-start | bytes 1540
  4.2 22.3 %copy-start.4 = (f32[64,32,32]{0,2,1:T(8,128)S(1)}, f32[64,32,32]{0,2,1:T(8,128)}, u32[]{:S(2)}) copy-start(f32[64,32,32]{0,2,1:T(8,128)} %param.17) | copy-start | bytes 786436
  4.2 15.4 %collective-permute-start = (bf16[32,1536]{1,0:T(8,128)(2,1)S(1)}, bf16[32,1536]{1,0:T(8,128)(2,1)S(1)}, u32[]{:S(2)}, u32[]{:S(2)}) collective-permute-start(bf16[32,1536]{1,0:T(8,128)(2,1)S(1)} %shard_map.92.data), channel_id=1, source_target_pairs={{0,8},{1,9},{2,26},{3,27},{4,40},{5,41},{6,58},{7,59},{8,72},{9,73... | collective-permute-start | bytes 294920 | tf_op jit(solution)/shard_map/ppermute | solution.py:440
  11.8 7.9 %all-to-all-start = ((f32[8,10,128]{2,1,0:T(8,128)}), f32[8,10,128]{2,1,0:T(8,128)S(1)}, u32[]{:S(2)}, u32[]{:S(2)}) async-start(f32[8,10,128]{2,1,0:T(8,128)} %shard_map.91), calls=%async_computation | async-start | bytes 131072 | tf_op jit(solution)/shard_map/all_to_all | solution.py:438
  21.4 16.5 %all-to-all-start.1 = ((bf16[16,8,2688]{2,1,0:T(8,128)(2,1)}), bf16[16,8,2688]{2,1,0:T(8,128)(2,1)S(1)}, u32[]{:S(2)}, u32[]{:S(2)}) async-start(bf16[16,8,2688]{2,1,0:T(8,128)(2,1)} %bitcast.8), calls=%async_computation.1 | async-start | bytes 1376256 | tf_op jit(solution)/shard_map/all_to_all | solution.py:447
  39.6 21.5 %all-to-all-start.2 = ((f32[8,128,128]{2,1,0:T(8,128)}), f32[8,128,128]{2,1,0:T(8,128)S(1)}, u32[]{:S(2)}, u32[]{:S(2)}) async-start(f32[8,128,128]{2,1,0:T(8,128)} %bitcast.12), calls=%async_computation.2 | async-start | bytes 1048576 | tf_op jit(solution)/shard_map/all_to_all | solution.py:468
  45.2 35.3 %copy-start.1 = (f32[32,32,32]{2,1,0:T(8,128)S(1)}, f32[32,32,32]{2,1,0:T(8,128)}, u32[]{:S(2)}) copy-start(f32[32,32,32]{2,1,0:T(8,128)} %param.12) | copy-start | bytes 393220
  61.1 19.5 %copy-start = (bf16[32,32,768]{2,1,0:T(8,128)(2,1)S(1)}, bf16[32,32,768]{2,1,0:T(8,128)(2,1)}, u32[]{:S(2)}) copy-start(bf16[32,32,768]{2,1,0:T(8,128)(2,1)} %param.11) | copy-start | bytes 4718596
  61.8 18.8 %all-to-all-start.3 = ((f32[16,8,896]{2,1,0:T(8,128)}), f32[16,8,896]{2,1,0:T(8,128)S(1)}, u32[]{:S(2)}, u32[]{:S(2)}) async-start(f32[16,8,896]{2,1,0:T(8,128)} %bitcast.13), calls=%async_computation.3 | async-start | bytes 917504 | tf_op jit(solution)/shard_map/all_to_all | solution.py:473
  65.4 15.2 %collective-permute-start.1 = (f32[32,768]{1,0:T(8,128)S(1)}, f32[32,768]{1,0:T(8,128)S(1)}, u32[]{:S(2)}, u32[]{:S(2)}) collective-permute-start(f32[32,768]{1,0:T(8,128)S(1)} %get-tuple-element.28), channel_id=1, source_target_pairs={{8,0},{9,1},{26,2},{27,3},{40,4},{41,5},{58,6},{59,7},{72,8},{73,9... | collective-permute-start | bytes 294920 | tf_op jit(solution)/shard_map/ppermute | solution.py:471

commit v13 on v12

--- a/solution.py
+++ b/solution.py
@@ -14,6 +14,7 @@
 BOTH = ("row", "col")
 GROUP = 16
 BATCH = 8
+GROUPS = 4
 PANELS = 256
 FIELD_ROWS = 32
 POINT_ROWS = 16
@@ -88,7 +89,7 @@
 def near_kernel(ids_lane, first_ref, second_ref, near_first, out_hbm, to_second, sem, *scratch):
     own = first_ref.shape[0]
     near_first[...] = jnp.zeros_like(near_first)
-    sets = scratch[: len(scratch) // 2], scratch[len(scratch) // 2 :]
+    sets = [scratch[k : k + 6] for k in range(0, len(scratch), 6)]
 
     def load(ref, count, s):
         parts = [ref[half, pl.ds(s, count, stride=GROUP), :] for half in range(2)]
@@ -101,10 +102,10 @@
         for half in range(2):
             sums[half, pl.ds(s, FIELD_ROWS, stride=GROUP), :] = total[:, half * 128 : (half + 1) * 128]
 
-    def two_groups(g, carry):
+    def some_groups(g, carry):
         begun = []
         for k, (field_a, left, field_b, right, _, _) in enumerate(sets):
-            rows = pl.ds(pl.multiple_of((2 * g + k) * GROUP, GROUP), GROUP)
+            rows = pl.ds(pl.multiple_of((len(sets) * g + k) * GROUP, GROUP), GROUP)
             ids = second_ref[rows, ids_lane : ids_lane + 128].astype(f32)[:, :own]
             chosen = (ids == lax.broadcasted_iota(jnp.int32, (GROUP, own), 1).astype(f32)).astype(bf16)
             first = jnp.dot(chosen, first_ref[...], preferred_element_type=f32)
@@ -146,7 +147,7 @@
                     )
         return carry
 
-    lax.fori_loop(0, second_ref.shape[0] // (2 * GROUP), two_groups, 0)
+    lax.fori_loop(0, second_ref.shape[0] // (len(sets) * GROUP), some_groups, 0)
     pltpu.make_async_copy(to_second, out_hbm.at[:, pl.ds(0, 3 * PANELS)], sem).wait()
 
 
@@ -166,7 +167,7 @@
         in_specs=[vmem] * 2,
         out_specs=[vmem, pl.BlockSpec(memory_space=pltpu.HBM)],
         scratch_shapes=[pltpu.VMEM((slots, 3 * PANELS), f32), pltpu.SemaphoreType.DMA]
-        + ([rows(FIELD_ROWS), rows(POINT_ROWS)] * 2 + [rows(FIELD_ROWS)] * 2) * 2,
+        + ([rows(FIELD_ROWS), rows(POINT_ROWS)] * 2 + [rows(FIELD_ROWS)] * 2) * GROUPS,
         compiler_params=pltpu.CompilerParams(vmem_limit_bytes=32 << 20),
         cost_estimate=pl.CostEstimate(
             flops=slots * 2 * 2 * 64 * PANELS * PANELS, bytes_accessed=slots * 9216, transcendentals=0
@@ -363,6 +364,25 @@
     )(place, from_row, data)
 
 
+def part_kernel(joined, parts):
+    panels = parts.shape[2]
+    for i in range(parts.shape[0]):
+        parts[i] = joined[:, i * panels : (i + 1) * panels]
+
+
+def part(joined):
+    own, width = joined.shape
+    vmem = pl.BlockSpec(memory_space=pltpu.VMEM)
+    return pl.pallas_call(
+        part_kernel,
+        out_shape=jax.ShapeDtypeStruct((3, own, width // 3), joined.dtype),
+        in_specs=[vmem],
+        out_specs=vmem,
+        compiler_params=pltpu.CompilerParams(vmem_limit_bytes=8 << 20),
+        cost_estimate=pl.CostEstimate(flops=1 << 34, bytes_accessed=1 << 18, transcendentals=0),
+    )(joined)
+
+
 def end_kernel(back, returned, near_first, basis, transfer, out, velocity, sems):
     own, panels = velocity.shape[1:]
     rank = transfer.shape[1]
@@ -386,7 +406,7 @@
         total = far[:own] + far[own : 2 * own] + far[2 * own :]
         for piece in pieces(returned[:, lanes], 3):
             total += jnp.dot(chosen, piece.astype(bf16), preferred_element_type=f32)
-        velocity[i] = near_first[:, lanes] + total
+        velocity[i] = near_first[i] + total
         copies.append(pltpu.make_async_copy(velocity.at[i], out.at[i], sems.at[i]))
         copies[-1].start()
     for copy in copies:
@@ -471,7 +491,7 @@
     near_first = lax.ppermute(near_first, BOTH, home)
     message = lax.dynamic_update_slice(to_second, row_locals.sum(axis=0), (0, 3 * panels))
     returned = lax.all_to_all(message, "col", 0, 0, tiled=True)
-    return end(back_ids, returned, near_first, basis, transfer)
+    return end(back_ids, returned, part(near_first), basis, transfer)
 
 
 def solution(mesh):

time: 82.6 us -> 79.8 us (0.966)
  the two profiles are of different devices: /device:TPU:1 before, /device:TPU:0 now
where the time goes in v13:
time: 79.8 us; the launch traced here: 79.3 us
  waiting for transfers between devices  27.1 us (34%)
  starting transfers between devices  25.2 us (32%)
  Pallas kernels  24.2 us (30%)
  local copies, waits for them, and re-layouts  1.62 us (2%)
  between operations  0.84 us (1%)
    pallas_call x1, Pallas kernels, near_sums(): pl.pallas_call(functools.partial(near_kernel, ids_lane), out_shape=[jax.S...  15.1 us
    all_to_all x1, waiting for transfers between devices, shards(): second = lax.all_to_all(message, 'col', 0, 0, tiled=True)  11.4 us
    all_to_all x1, waiting for transfers between devices, shards(): returned = lax.all_to_all(message, 'col', 0, 0, tiled=True)  10.1 us
    all_to_all x1, waiting for transfers between devices, shards(): from_row = lax.all_to_all(message, 'row', 0, 0, tiled=True)  5.55 us
    all_to_all x1, starting transfers between devices, shards(): from_row = lax.all_to_all(message, 'row', 0, 0, tiled=True)  5.08 us
    all_to_all x1, starting transfers between devices, shards(): second = lax.all_to_all(message, 'col', 0, 0, tiled=True)  4.69 us
    all_to_all x1, starting transfers between devices, shards(): returned = lax.all_to_all(message, 'col', 0, 0, tiled=True)  4.42 us
    ppermute x1, starting transfers between devices, shards(): first_data = lax.ppermute(data, BOTH, swap)  4.03 us
  transfers between devices with their start and end apart: 6, of which 3 were waited for; matrix products, arithmetic and copies ran while one was open for 2% of the time, Pallas kernels for 20%

profile of v13, /device:TPU:0, one launch (start us, length us, event | category | flops | bytes accessed | tf_op | source)
XLA Modules:
  0.0 79.3 jit_solution(13769152211335090307)
XLA Ops:
  0.0 0.0 copy-start.2
  0.0 0.0 copy-start.3
  0.7 0.0 copy-start.5
  0.7 3.5 %shard_map.91 = f32[8,10,128]{2,1,0:T(8,128)} custom-call(s32[1,1]{1,0:T(1,128)} %bitcast.18.count_hbm, s32[2,128]{1,0:T(2,128)} %pairs_hbm.1, bf16[3,32,256]{2,1,0:T(8,128)(2,1)} %bitcast.26, bf16[1024,768]{1,0:T(8,128)(2,1)} %bitcast.19, f32[1024,32]{1,0:T(8,128)} %bitcast.23), custom_call_target="tpu_custom_call" | custom-call | tf_op jit(solution)/shard_map/pallas_call | solution.py:288
  4.2 0.0 copy-start.6
  4.2 0.0 copy-start.4
  4.2 0.0 copy-done.2
  4.2 0.0 copy-done.3
  4.2 4.0 %collective-permute-start = (bf16[32,1536]{1,0:T(8,128)(2,1)S(1)}, bf16[32,1536]{1,0:T(8,128)(2,1)S(1)}, u32[]{:S(2)}, u32[]{:S(2)}) collective-permute-start(bf16[32,1536]{1,0:T(8,128)(2,1)S(1)} %shard_map.92.data), channel_id=1, source_target_pairs={{0,8},{1,9},{2,26},{3,27},{4,40},{5,41},{6,58},{7,59},{8,72},{9,73... | collective-permute-start | bytes 294920 | tf_op jit(solution)/shard_map/ppermute | solution.py:460
  8.3 5.1 %all-to-all-start = ((f32[8,10,128]{2,1,0:T(8,128)}), f32[8,10,128]{2,1,0:T(8,128)S(1)}, u32[]{:S(2)}, u32[]{:S(2)}) async-start(f32[8,10,128]{2,1,0:T(8,128)} %shard_map.91), calls=%async_computation | async-start | bytes 131072 | tf_op jit(solution)/shard_map/all_to_all | solution.py:458
  13.4 0.1 pad_add_fusion.place
  13.4 5.5 %all-to-all-done.from_row = f32[8,10,128]{2,1,0:T(8,128)S(1)} async-done(((f32[8,10,128]{2,1,0:T(8,128)}), f32[8,10,128]{2,1,0:T(8,128)S(1)}, u32[]{:S(2)}, u32[]{:S(2)}) %all-to-all-start) | async-done | bytes 40992 | tf_op jit(solution)/shard_map/all_to_all | solution.py:458
  19.0 0.0 collective-permute-done.first_ref
  19.0 1.7 %shard_map.93 = (bf16[128,2688]{1,0:T(8,128)(2,1)}, f32[1,128]{1,0:T(1,128)S(1)}) custom-call(s32[2]{0:T(128)S(1)} %pad_add_fusion.place, f32[8,10,128]{2,1,0:T(8,128)S(1)} %all-to-all-done.from_row, bf16[32,1536]{1,0:T(8,128)(2,1)S(1)} %shard_map.92.data), custom_call_target="tpu_custom_call" | custom-call | tf_op jit(solution)/shard_map/pallas_call | solution.py:357
  20.7 4.7 %all-to-all-start.1 = ((bf16[16,8,2688]{2,1,0:T(8,128)(2,1)}), bf16[16,8,2688]{2,1,0:T(8,128)(2,1)S(1)}, u32[]{:S(2)}, u32[]{:S(2)}) async-start(bf16[16,8,2688]{2,1,0:T(8,128)(2,1)} %bitcast.8), calls=%async_computation.1 | async-start | bytes 1376256 | tf_op jit(solution)/shard_map/all_to_all | solution.py:467
  25.4 0.0 copy-done.5
  25.4 0.5 reshape.27.parents
  26.0 0.0 copy-done.6
  26.0 0.1 reshape.28.ends
  26.1 0.0 copy-done.4
  26.1 0.3 copy.13
  26.4 0.2 pad_maximum_fusion.factors
  26.6 0.6 shard_map.94.hits
  27.2 11.4 %all-to-all-done.1 = bf16[16,8,2688]{2,1,0:T(8,128)(2,1)S(1)} async-done(((bf16[16,8,2688]{2,1,0:T(8,128)(2,1)}), bf16[16,8,2688]{2,1,0:T(8,128)(2,1)S(1)}, u32[]{:S(2)}, u32[]{:S(2)}) %all-to-all-start.1) | async-done | bytes 688160 | tf_op jit(solution)/shard_map/all_to_all | solution.py:467
  38.6 1.8 %shard_map.95 = f32[1024,128]{1,0:T(8,128)} custom-call(bf16[128,2688]{1,0:T(8,128)(2,1)S(1)} %bitcast.21, bf16[1024,512]{1,0:T(8,128)(2,1)S(1)} %shard_map.94.hits, f32[32,32,128]{2,1,0:T(8,128)S(1)} %pad_maximum_fusion.factors), custom_call_target="tpu_custom_call" | custom-call | tf_op jit(solution)/shard_map/pallas_call | solution.py:479
  40.4 3.5 %all-to-all-start.2 = ((f32[8,128,128]{2,1,0:T(8,128)}), f32[8,128,128]{2,1,0:T(8,128)S(1)}, u32[]{:S(2)}, u32[]{:S(2)}) async-start(f32[8,128,128]{2,1,0:T(8,128)} %bitcast.12), calls=%async_computation.2 | async-start | bytes 1048576 | tf_op jit(solution)/shard_map/all_to_all | solution.py:488
  43.9 15.1 %shard_map.96 = (f32[32,768]{1,0:T(8,128)S(1)}, f32[128,896]{1,0:T(8,128)}) custom-call(bf16[32,1536]{1,0:T(8,128)(2,1)S(1)} %collective-permute-done.first_ref, bf16[128,2688]{1,0:T(8,128)(2,1)S(1)} %bitcast.22), custom_call_target="tpu_custom_call" | custom-call | flops 2147483648 | bytes 1179648 | tf_op jit(solution)/shard_map/pallas_call | solution.py:161
  59.0 3.5 %collective-permute-start.1 = (f32[32,768]{1,0:T(8,128)S(1)}, f32[32,768]{1,0:T(8,128)S(1)}, u32[]{:S(2)}, u32[]{:S(2)}) collective-permute-start(f32[32,768]{1,0:T(8,128)S(1)} %get-tuple-element.28), channel_id=1, source_target_pairs={{8,0},{9,1},{26,2},{27,3},{40,4},{41,5},{58,6},{59,7},{72,8},{73,9... | collective-permute-start | bytes 294920 | tf_op jit(solution)/shard_map/ppermute | solution.py:491
  62.5 0.0 all-to-all-done.2
  62.6 0.6 constant_dynamic-update-slice_fusion
  63.2 4.4 %all-to-all-start.3 = ((f32[16,8,896]{2,1,0:T(8,128)}), f32[16,8,896]{2,1,0:T(8,128)S(1)}, u32[]{:S(2)}, u32[]{:S(2)}) async-start(f32[16,8,896]{2,1,0:T(8,128)} %bitcast.13), calls=%async_computation.3 | async-start | bytes 917504 | tf_op jit(solution)/shard_map/all_to_all | solution.py:493
  67.6 0.0 copy-start
  67.6 0.0 copy-start.1
  67.6 0.0 collective-permute-done.1.joined
  67.7 10.1 %all-to-all-done.3 = f32[16,8,896]{2,1,0:T(8,128)S(1)} async-done(((f32[16,8,896]{2,1,0:T(8,128)}), f32[16,8,896]{2,1,0:T(8,128)S(1)}, u32[]{:S(2)}, u32[]{:S(2)}) %all-to-all-start.3) | async-done | bytes 458784 | tf_op jit(solution)/shard_map/all_to_all | solution.py:493
  77.8 0.0 copy-done
  77.8 0.0 copy-done.1
  77.8 1.5 %shard_map.98 = f32[3,32,256]{2,1,0:T(8,128)} custom-call(f32[1,128]{1,0:T(1,128)S(1)} %get-tuple-element.21.back, f32[128,896]{1,0:T(8,128)S(1)} %bitcast.25, f32[3,32,256]{2,1,0:T(8,128)S(1)} %shard_map.97.near_first, bf16[1024,768]{1,0:T(8,128)(2,1)S(1)} %bitcast.20, f32[1024,32]{1,0:T(8,128)S(1)} %bitcast.24), custom_call_target="tpu_custom_call" | custom-call | tf_op jit(solution)/shard_map/pallas_call | solution.py:419
  (4 shorter events, 0.1 us)
Async XLA Ops:
  0.0 4.2 %copy-start.2 = (bf16[32,3,256]{2,0,1:T(8,128)(2,1)S(1)}, bf16[32,3,256]{2,0,1:T(8,128)(2,1)}, u32[]{:S(2)}) copy-start(bf16[32,3,256]{2,0,1:T(8,128)(2,1)} %param.9) | copy-start | bytes 147460
  0.0 4.2 %copy-start.3 = (bf16[32,3,256]{2,0,1:T(8,128)(2,1)S(1)}, bf16[32,3,256]{2,0,1:T(8,128)(2,1)}, u32[]{:S(2)}) copy-start(bf16[32,3,256]{2,0,1:T(8,128)(2,1)} %param.10) | copy-start | bytes 147460
  0.7 24.8 %copy-start.5 = (s32[4096]{0:T(1024)S(1)}, s32[4096]{0:T(1024)}, u32[]{:S(2)}) copy-start(s32[4096]{0:T(1024)} %param.13) | copy-start | bytes 49156
  4.2 21.8 %copy-start.6 = (s32[2,64]{1,0:T(2,128)S(1)}, s32[2,64]{1,0:T(2,128)}, u32[]{:S(2)}) copy-start(s32[2,64]{1,0:T(2,128)} %param.16) | copy-start | bytes 1540
  4.2 21.9 %copy-start.4 = (f32[64,32,32]{0,2,1:T(8,128)S(1)}, f32[64,32,32]{0,2,1:T(8,128)}, u32[]{:S(2)}) copy-start(f32[64,32,32]{0,2,1:T(8,128)} %param.17) | copy-start | bytes 786436
  4.2 14.7 %collective-permute-start = (bf16[32,1536]{1,0:T(8,128)(2,1)S(1)}, bf16[32,1536]{1,0:T(8,128)(2,1)S(1)}, u32[]{:S(2)}, u32[]{:S(2)}) collective-permute-start(bf16[32,1536]{1,0:T(8,128)(2,1)S(1)} %shard_map.92.data), channel_id=1, source_target_pairs={{0,8},{1,9},{2,26},{3,27},{4,40},{5,41},{6,58},{7,59},{8,72},{9,73... | collective-permute-start | bytes 294920 | tf_op jit(solution)/shard_map/ppermute | solution.py:460
  8.3 10.7 %all-to-all-start = ((f32[8,10,128]{2,1,0:T(8,128)}), f32[8,10,128]{2,1,0:T(8,128)S(1)}, u32[]{:S(2)}, u32[]{:S(2)}) async-start(f32[8,10,128]{2,1,0:T(8,128)} %shard_map.91), calls=%async_computation | async-start | bytes 131072 | tf_op jit(solution)/shard_map/all_to_all | solution.py:458
  20.7 17.9 %all-to-all-start.1 = ((bf16[16,8,2688]{2,1,0:T(8,128)(2,1)}), bf16[16,8,2688]{2,1,0:T(8,128)(2,1)S(1)}, u32[]{:S(2)}, u32[]{:S(2)}) async-start(bf16[16,8,2688]{2,1,0:T(8,128)(2,1)} %bitcast.8), calls=%async_computation.1 | async-start | bytes 1376256 | tf_op jit(solution)/shard_map/all_to_all | solution.py:467
  40.4 22.1 %all-to-all-start.2 = ((f32[8,128,128]{2,1,0:T(8,128)}), f32[8,128,128]{2,1,0:T(8,128)S(1)}, u32[]{:S(2)}, u32[]{:S(2)}) async-start(f32[8,128,128]{2,1,0:T(8,128)} %bitcast.12), calls=%async_computation.2 | async-start | bytes 1048576 | tf_op jit(solution)/shard_map/all_to_all | solution.py:488
  59.0 8.7 %collective-permute-start.1 = (f32[32,768]{1,0:T(8,128)S(1)}, f32[32,768]{1,0:T(8,128)S(1)}, u32[]{:S(2)}, u32[]{:S(2)}) collective-permute-start(f32[32,768]{1,0:T(8,128)S(1)} %get-tuple-element.28), channel_id=1, source_target_pairs={{8,0},{9,1},{26,2},{27,3},{40,4},{41,5},{58,6},{59,7},{72,8},{73,9... | collective-permute-start | bytes 294920 | tf_op jit(solution)/shard_map/ppermute | solution.py:491
  63.2 14.6 %all-to-all-start.3 = ((f32[16,8,896]{2,1,0:T(8,128)}), f32[16,8,896]{2,1,0:T(8,128)S(1)}, u32[]{:S(2)}, u32[]{:S(2)}) async-start(f32[16,8,896]{2,1,0:T(8,128)} %bitcast.13), calls=%async_computation.3 | async-start | bytes 917504 | tf_op jit(solution)/shard_map/all_to_all | solution.py:493
  67.6 10.2 %copy-start = (bf16[32,32,768]{2,1,0:T(8,128)(2,1)S(1)}, bf16[32,32,768]{2,1,0:T(8,128)(2,1)}, u32[]{:S(2)}) copy-start(bf16[32,32,768]{2,1,0:T(8,128)(2,1)} %param.11) | copy-start | bytes 4718596
  67.6 10.2 %copy-start.1 = (f32[32,32,32]{2,1,0:T(8,128)S(1)}, f32[32,32,32]{2,1,0:T(8,128)}, u32[]{:S(2)}) copy-start(f32[32,32,32]{2,1,0:T(8,128)} %param.12) | copy-start | bytes 393220

commit v14 on v13

--- a/solution.py
+++ b/solution.py
@@ -364,6 +364,22 @@
     )(place, from_row, data)
 
 
+def keep_kernel(joined, kept):
+    kept[...] = joined[...]
+
+
+def keep(joined, cost):
+    vmem = pl.BlockSpec(memory_space=pltpu.VMEM)
+    return pl.pallas_call(
+        keep_kernel,
+        out_shape=jax.ShapeDtypeStruct(joined.shape, joined.dtype),
+        in_specs=[vmem],
+        out_specs=vmem,
+        compiler_params=pltpu.CompilerParams(vmem_limit_bytes=8 << 20),
+        cost_estimate=pl.CostEstimate(flops=cost, bytes_accessed=1 << 18, transcendentals=0),
+    )(joined)
+
+
 def part_kernel(joined, parts):
     panels = parts.shape[2]
     for i in range(parts.shape[0]):
@@ -458,7 +474,6 @@
     from_row = lax.all_to_all(message, "row", 0, 0, tiled=True)
     data = join(density, coords)
     first_data = lax.ppermute(data, BOTH, swap)
-    first_data, from_row = lax.optimization_barrier((first_data, from_row))
 
     place = jnp.stack([lax.axis_index("row"), lax.axis_index("col")])
     orders = [sorted((seat(p, r, h, rows), r, h) for r in range(rows) for h in range(half)) for p in range(2)]
@@ -484,6 +499,7 @@
         scratch_shapes=[pltpu.VMEM((rows * slots, 128), f32), pltpu.SemaphoreType.DMA((rows * slots // 256,))],
         compiler_params=pltpu.CompilerParams(vmem_limit_bytes=16 << 20),
     )(second, hits, factors)
+    first_data = keep(first_data, 1 << 34)
     first_data, partial = lax.optimization_barrier((first_data, partial))
     row_locals = lax.all_to_all(partial.reshape(rows, slots, 128), "row", 0, 0, tiled=True)
 

time: 79.8 us -> 78.7 us (0.986)
  waiting for transfers between devices: 27.1 us -> 23 us
  starting transfers between devices: 25.2 us -> 28.1 us
    all_to_all x1, waiting for transfers between devices: 5.55 us -> 0.37 us  [shards(): from_row = lax.all_to_all(message, 'row', 0, 0, tiled=True)]
    all_to_all x1, starting transfers between devices: 4.69 us -> 8.35 us  [shards(): second = lax.all_to_all(message, 'col', 0, 0, tiled=True)]
    all_to_all x1, waiting for transfers between devices: 11.4 us -> 12.5 us  [shards(): second = lax.all_to_all(message, 'col', 0, 0, tiled=True)]
  transfers between devices with their start and end apart: 6 -> 6, of which waited for: 3 -> 3; matrix products, arithmetic and copies ran while one was open for 2% -> 2% of each run, Pallas kernels for 20% -> 22%
where the time goes in v14:
time: 78.7 us; the launch traced here: 78.2 us
  starting transfers between devices  28.1 us (36%)
  Pallas kernels  24.2 us (31%)
  waiting for transfers between devices  23 us (29%)
  local copies, waits for them, and re-layouts  1.61 us (2%)
  between operations  0.88 us (1%)
    pallas_call x1, Pallas kernels, near_sums(): pl.pallas_call(functools.partial(near_kernel, ids_lane), out_shape=[jax.S...  15.1 us
    all_to_all x1, waiting for transfers between devices, shards(): second = lax.all_to_all(message, 'col', 0, 0, tiled=True)  12.5 us
    all_to_all x1, waiting for transfers between devices, shards(): returned = lax.all_to_all(message, 'col', 0, 0, tiled=True)  10.1 us
    all_to_all x1, starting transfers between devices, shards(): second = lax.all_to_all(message, 'col', 0, 0, tiled=True)  8.35 us
    all_to_all x1, starting transfers between devices, shards(): returned = lax.all_to_all(message, 'col', 0, 0, tiled=True)  4.42 us
    all_to_all x1, starting transfers between devices, shards(): from_row = lax.all_to_all(message, 'row', 0, 0, tiled=True)  4.39 us
    ppermute x1, starting transfers between devices, shards(): first_data = lax.ppermute(data, BOTH, swap)  3.96 us
    ppermute x1, starting transfers between devices, shards(): near_first = lax.ppermute(near_first, BOTH, home)  3.53 us
  transfers between devices with their start and end apart: 6, of which 3 were waited for; matrix products, arithmetic and copies ran while one was open for 2% of the time, Pallas kernels for 22%

profile of v14, /device:TPU:0, one launch (start us, length us, event | category | flops | bytes accessed | tf_op | source)
XLA Modules:
  0.0 78.2 jit_solution(3723862437570972255)
XLA Ops:
  0.0 0.0 copy-start.2
  0.0 0.0 copy-start.3
  0.0 0.0 copy-start.4
  0.7 3.5 %shard_map.91 = f32[8,10,128]{2,1,0:T(8,128)} custom-call(s32[1,1]{1,0:T(1,128)} %bitcast.18.count_hbm, s32[2,128]{1,0:T(2,128)} %pairs_hbm.1, bf16[3,32,256]{2,1,0:T(8,128)(2,1)} %bitcast.26, bf16[1024,768]{1,0:T(8,128)(2,1)} %bitcast.19, f32[1024,32]{1,0:T(8,128)} %bitcast.23), custom_call_target="tpu_custom_call" | custom-call | tf_op jit(solution)/shard_map/pallas_call | solution.py:288
  4.2 0.0 copy-start.5
  4.2 4.4 %all-to-all-start = ((f32[8,10,128]{2,1,0:T(8,128)}), f32[8,10,128]{2,1,0:T(8,128)S(1)}, u32[]{:S(2)}, u32[]{:S(2)}) async-start(f32[8,10,128]{2,1,0:T(8,128)} %shard_map.91), calls=%async_computation | async-start | bytes 131072 | tf_op jit(solution)/shard_map/all_to_all | solution.py:474
  8.6 0.0 copy-done.2
  8.6 0.0 copy-done.3
  8.7 4.0 %collective-permute-start = (bf16[32,1536]{1,0:T(8,128)(2,1)S(1)}, bf16[32,1536]{1,0:T(8,128)(2,1)S(1)}, u32[]{:S(2)}, u32[]{:S(2)}) collective-permute-start(bf16[32,1536]{1,0:T(8,128)(2,1)S(1)} %shard_map.92.data), channel_id=1, source_target_pairs={{0,8},{1,9},{2,26},{3,27},{4,40},{5,41},{6,58},{7,59},{8,72},{9,73... | collective-permute-start | bytes 294920 | tf_op jit(solution)/shard_map/ppermute | solution.py:476
  12.6 0.0 copy-done.4
  12.6 0.0 copy-start.6
  12.6 0.3 copy.13
  12.9 0.2 pad_maximum_fusion.factors
  13.1 0.1 pad_add_fusion.place
  13.2 0.0 copy-done.5
  13.2 0.5 reshape.27.parents
  13.8 0.0 copy-done.6
  13.8 0.1 reshape.28.ends
  13.9 0.4 all-to-all-done.from_row
  14.3 1.7 %shard_map.93 = (bf16[128,2688]{1,0:T(8,128)(2,1)}, f32[1,128]{1,0:T(1,128)S(1)}) custom-call(s32[2]{0:T(128)S(1)} %pad_add_fusion.place, f32[8,10,128]{2,1,0:T(8,128)S(1)} %all-to-all-done.from_row, bf16[32,1536]{1,0:T(8,128)(2,1)S(1)} %shard_map.92.data), custom_call_target="tpu_custom_call" | custom-call | tf_op jit(solution)/shard_map/pallas_call | solution.py:357
  16.0 8.3 %all-to-all-start.1 = ((bf16[16,8,2688]{2,1,0:T(8,128)(2,1)}), bf16[16,8,2688]{2,1,0:T(8,128)(2,1)S(1)}, u32[]{:S(2)}, u32[]{:S(2)}) async-start(bf16[16,8,2688]{2,1,0:T(8,128)(2,1)} %bitcast.8), calls=%async_computation.1 | async-start | bytes 1376256 | tf_op jit(solution)/shard_map/all_to_all | solution.py:482
  24.4 0.6 shard_map.95.hits
  25.0 0.0 collective-permute-done.joined
  25.0 12.5 %all-to-all-done.1 = bf16[16,8,2688]{2,1,0:T(8,128)(2,1)S(1)} async-done(((bf16[16,8,2688]{2,1,0:T(8,128)(2,1)}), bf16[16,8,2688]{2,1,0:T(8,128)(2,1)S(1)}, u32[]{:S(2)}, u32[]{:S(2)}) %all-to-all-start.1) | async-done | bytes 688160 | tf_op jit(solution)/shard_map/all_to_all | solution.py:482
  37.5 1.8 %shard_map.96 = f32[1024,128]{1,0:T(8,128)} custom-call(bf16[128,2688]{1,0:T(8,128)(2,1)S(1)} %bitcast.21, bf16[1024,512]{1,0:T(8,128)(2,1)S(1)} %shard_map.95.hits, f32[32,32,128]{2,1,0:T(8,128)S(1)} %pad_maximum_fusion.factors), custom_call_target="tpu_custom_call" | custom-call | tf_op jit(solution)/shard_map/pallas_call | solution.py:494
  39.2 3.5 %all-to-all-start.2 = ((f32[8,128,128]{2,1,0:T(8,128)}), f32[8,128,128]{2,1,0:T(8,128)S(1)}, u32[]{:S(2)}, u32[]{:S(2)}) async-start(f32[8,128,128]{2,1,0:T(8,128)} %bitcast.12), calls=%async_computation.2 | async-start | bytes 1048576 | tf_op jit(solution)/shard_map/all_to_all | solution.py:504
  42.7 15.1 %shard_map.97 = (f32[32,768]{1,0:T(8,128)S(1)}, f32[128,896]{1,0:T(8,128)}) custom-call(bf16[32,1536]{1,0:T(8,128)(2,1)S(1)} %shard_map.94.first_ref, bf16[128,2688]{1,0:T(8,128)(2,1)S(1)} %bitcast.22), custom_call_target="tpu_custom_call" | custom-call | flops 2147483648 | bytes 1179648 | tf_op jit(solution)/shard_map/pallas_call | solution.py:161
  57.8 3.5 %collective-permute-start.1 = (f32[32,768]{1,0:T(8,128)S(1)}, f32[32,768]{1,0:T(8,128)S(1)}, u32[]{:S(2)}, u32[]{:S(2)}) collective-permute-start(f32[32,768]{1,0:T(8,128)S(1)} %get-tuple-element.24), channel_id=1, source_target_pairs={{8,0},{9,1},{26,2},{27,3},{40,4},{41,5},{58,6},{59,7},{72,8},{73,9... | collective-permute-start | bytes 294920 | tf_op jit(solution)/shard_map/ppermute | solution.py:507
  61.4 0.0 all-to-all-done.2
  61.4 0.6 constant_dynamic-update-slice_fusion
  62.0 4.4 %all-to-all-start.3 = ((f32[16,8,896]{2,1,0:T(8,128)}), f32[16,8,896]{2,1,0:T(8,128)S(1)}, u32[]{:S(2)}, u32[]{:S(2)}) async-start(f32[16,8,896]{2,1,0:T(8,128)} %bitcast.13), calls=%async_computation.3 | async-start | bytes 917504 | tf_op jit(solution)/shard_map/all_to_all | solution.py:509
  66.5 0.0 copy-start
  66.5 0.0 copy-start.1
  66.5 0.0 collective-permute-done.1.joined
  66.5 10.1 %all-to-all-done.3 = f32[16,8,896]{2,1,0:T(8,128)S(1)} async-done(((f32[16,8,896]{2,1,0:T(8,128)}), f32[16,8,896]{2,1,0:T(8,128)S(1)}, u32[]{:S(2)}, u32[]{:S(2)}) %all-to-all-start.3) | async-done | bytes 458784 | tf_op jit(solution)/shard_map/all_to_all | solution.py:509
  76.6 0.0 copy-done
  76.7 0.0 copy-done.1
  76.7 1.5 %shard_map.99 = f32[3,32,256]{2,1,0:T(8,128)} custom-call(f32[1,128]{1,0:T(1,128)S(1)} %get-tuple-element.18.back, f32[128,896]{1,0:T(8,128)S(1)} %bitcast.25, f32[3,32,256]{2,1,0:T(8,128)S(1)} %shard_map.98.near_first, bf16[1024,768]{1,0:T(8,128)(2,1)S(1)} %bitcast.20, f32[1024,32]{1,0:T(8,128)S(1)} %bitcast.24), custom_call_target="tpu_custom_call" | custom-call | tf_op jit(solution)/shard_map/pallas_call | solution.py:435
  (5 shorter events, 0.1 us)
Async XLA Ops:
  0.0 8.6 %copy-start.2 = (bf16[32,3,256]{2,0,1:T(8,128)(2,1)S(1)}, bf16[32,3,256]{2,0,1:T(8,128)(2,1)}, u32[]{:S(2)}) copy-start(bf16[32,3,256]{2,0,1:T(8,128)(2,1)} %param.9) | copy-start | bytes 147460
  0.0 8.6 %copy-start.3 = (bf16[32,3,256]{2,0,1:T(8,128)(2,1)S(1)}, bf16[32,3,256]{2,0,1:T(8,128)(2,1)}, u32[]{:S(2)}) copy-start(bf16[32,3,256]{2,0,1:T(8,128)(2,1)} %param.10) | copy-start | bytes 147460
  0.0 12.6 %copy-start.4 = (f32[64,32,32]{0,2,1:T(8,128)S(1)}, f32[64,32,32]{0,2,1:T(8,128)}, u32[]{:S(2)}) copy-start(f32[64,32,32]{0,2,1:T(8,128)} %param.17) | copy-start | bytes 786436
  4.2 9.0 %copy-start.5 = (s32[4096]{0:T(1024)S(1)}, s32[4096]{0:T(1024)}, u32[]{:S(2)}) copy-start(s32[4096]{0:T(1024)} %param.13) | copy-start | bytes 49156
  4.2 10.0 %all-to-all-start = ((f32[8,10,128]{2,1,0:T(8,128)}), f32[8,10,128]{2,1,0:T(8,128)S(1)}, u32[]{:S(2)}, u32[]{:S(2)}) async-start(f32[8,10,128]{2,1,0:T(8,128)} %shard_map.91), calls=%async_computation | async-start | bytes 131072 | tf_op jit(solution)/shard_map/all_to_all | solution.py:474
  8.7 16.3 %collective-permute-start = (bf16[32,1536]{1,0:T(8,128)(2,1)S(1)}, bf16[32,1536]{1,0:T(8,128)(2,1)S(1)}, u32[]{:S(2)}, u32[]{:S(2)}) collective-permute-start(bf16[32,1536]{1,0:T(8,128)(2,1)S(1)} %shard_map.92.data), channel_id=1, source_target_pairs={{0,8},{1,9},{2,26},{3,27},{4,40},{5,41},{6,58},{7,59},{8,72},{9,73... | collective-permute-start | bytes 294920 | tf_op jit(solution)/shard_map/ppermute | solution.py:476
  12.6 1.1 %copy-start.6 = (s32[2,64]{1,0:T(2,128)S(1)}, s32[2,64]{1,0:T(2,128)}, u32[]{:S(2)}) copy-start(s32[2,64]{1,0:T(2,128)} %param.16) | copy-start | bytes 1540
  16.0 21.5 %all-to-all-start.1 = ((bf16[16,8,2688]{2,1,0:T(8,128)(2,1)}), bf16[16,8,2688]{2,1,0:T(8,128)(2,1)S(1)}, u32[]{:S(2)}, u32[]{:S(2)}) async-start(bf16[16,8,2688]{2,1,0:T(8,128)(2,1)} %bitcast.8), calls=%async_computation.1 | async-start | bytes 1376256 | tf_op jit(solution)/shard_map/all_to_all | solution.py:482
  39.2 22.1 %all-to-all-start.2 = ((f32[8,128,128]{2,1,0:T(8,128)}), f32[8,128,128]{2,1,0:T(8,128)S(1)}, u32[]{:S(2)}, u32[]{:S(2)}) async-start(f32[8,128,128]{2,1,0:T(8,128)} %bitcast.12), calls=%async_computation.2 | async-start | bytes 1048576 | tf_op jit(solution)/shard_map/all_to_all | solution.py:504
  57.8 8.7 %collective-permute-start.1 = (f32[32,768]{1,0:T(8,128)S(1)}, f32[32,768]{1,0:T(8,128)S(1)}, u32[]{:S(2)}, u32[]{:S(2)}) collective-permute-start(f32[32,768]{1,0:T(8,128)S(1)} %get-tuple-element.24), channel_id=1, source_target_pairs={{8,0},{9,1},{26,2},{27,3},{40,4},{41,5},{58,6},{59,7},{72,8},{73,9... | collective-permute-start | bytes 294920 | tf_op jit(solution)/shard_map/ppermute | solution.py:507
  62.0 14.6 %all-to-all-start.3 = ((f32[16,8,896]{2,1,0:T(8,128)}), f32[16,8,896]{2,1,0:T(8,128)S(1)}, u32[]{:S(2)}, u32[]{:S(2)}) async-start(f32[16,8,896]{2,1,0:T(8,128)} %bitcast.13), calls=%async_computation.3 | async-start | bytes 917504 | tf_op jit(solution)/shard_map/all_to_all | solution.py:509
  66.5 10.2 %copy-start = (bf16[32,32,768]{2,1,0:T(8,128)(2,1)S(1)}, bf16[32,32,768]{2,1,0:T(8,128)(2,1)}, u32[]{:S(2)}) copy-start(bf16[32,32,768]{2,1,0:T(8,128)(2,1)} %param.11) | copy-start | bytes 4718596
  66.5 10.2 %copy-start.1 = (f32[32,32,32]{2,1,0:T(8,128)S(1)}, f32[32,32,32]{2,1,0:T(8,128)}, u32[]{:S(2)}) copy-start(f32[32,32,32]{2,1,0:T(8,128)} %param.12) | copy-start | bytes 393220

commit v15 on v14

--- a/solution.py
+++ b/solution.py
@@ -14,7 +14,7 @@
 BOTH = ("row", "col")
 GROUP = 16
 BATCH = 8
-GROUPS = 4
+GROUPS = 8
 PANELS = 256
 FIELD_ROWS = 32
 POINT_ROWS = 16

time: 78.7 us -> 78.8 us (level)
  no operation moved by 1% of the time
where the time goes in v15:
time: 78.8 us; the launch traced here: 78.2 us
  starting transfers between devices  28.2 us (36%)
  Pallas kernels  24.1 us (31%)
  waiting for transfers between devices  23 us (29%)
  local copies, waits for them, and re-layouts  1.61 us (2%)
  between operations  1.06 us (1%)
    pallas_call x1, Pallas kernels, near_sums(): pl.pallas_call(functools.partial(near_kernel, ids_lane), out_shape=[jax.S...  14.9 us
    all_to_all x1, waiting for transfers between devices, shards(): second = lax.all_to_all(message, 'col', 0, 0, tiled=True)  12.5 us
    all_to_all x1, waiting for transfers between devices, shards(): returned = lax.all_to_all(message, 'col', 0, 0, tiled=True)  10.2 us
    all_to_all x1, starting transfers between devices, shards(): second = lax.all_to_all(message, 'col', 0, 0, tiled=True)  8.35 us
    all_to_all x1, starting transfers between devices, shards(): returned = lax.all_to_all(message, 'col', 0, 0, tiled=True)  4.44 us
    all_to_all x1, starting transfers between devices, shards(): from_row = lax.all_to_all(message, 'row', 0, 0, tiled=True)  4.4 us
    ppermute x1, starting transfers between devices, shards(): first_data = lax.ppermute(data, BOTH, swap)  3.95 us
    all_to_all x1, starting transfers between devices, shards(): lax.all_to_all(partial.reshape(rows, slots, 128), 'row', 0, 0, tiled=True)  3.68 us
  transfers between devices with their start and end apart: 6, of which 3 were waited for; matrix products, arithmetic and copies ran while one was open for 2% of the time, Pallas kernels for 22%

profile of v15, /device:TPU:0, one launch (start us, length us, event | category | flops | bytes accessed | tf_op | source)
XLA Modules:
  0.0 78.2 jit_solution(10021075379495249250)
XLA Ops:
  0.0 0.0 copy-start.2
  0.0 0.0 copy-start.3
  0.0 0.0 copy-start.4
  0.7 3.5 %shard_map.91 = f32[8,10,128]{2,1,0:T(8,128)} custom-call(s32[1,1]{1,0:T(1,128)} %bitcast.18.count_hbm, s32[2,128]{1,0:T(2,128)} %pairs_hbm.1, bf16[3,32,256]{2,1,0:T(8,128)(2,1)} %bitcast.26, bf16[1024,768]{1,0:T(8,128)(2,1)} %bitcast.19, f32[1024,32]{1,0:T(8,128)} %bitcast.23), custom_call_target="tpu_custom_call" | custom-call | tf_op jit(solution)/shard_map/pallas_call | solution.py:288
  4.2 0.0 copy-start.5
  4.2 4.4 %all-to-all-start = ((f32[8,10,128]{2,1,0:T(8,128)}), f32[8,10,128]{2,1,0:T(8,128)S(1)}, u32[]{:S(2)}, u32[]{:S(2)}) async-start(f32[8,10,128]{2,1,0:T(8,128)} %shard_map.91), calls=%async_computation | async-start | bytes 131072 | tf_op jit(solution)/shard_map/all_to_all | solution.py:474
  8.6 0.0 copy-done.2
  8.6 0.0 copy-done.3
  8.7 3.9 %collective-permute-start = (bf16[32,1536]{1,0:T(8,128)(2,1)S(1)}, bf16[32,1536]{1,0:T(8,128)(2,1)S(1)}, u32[]{:S(2)}, u32[]{:S(2)}) collective-permute-start(bf16[32,1536]{1,0:T(8,128)(2,1)S(1)} %shard_map.92.data), channel_id=1, source_target_pairs={{0,8},{1,9},{2,26},{3,27},{4,40},{5,41},{6,58},{7,59},{8,72},{9,73... | collective-permute-start | bytes 294920 | tf_op jit(solution)/shard_map/ppermute | solution.py:476
  12.6 0.0 copy-done.4
  12.6 0.0 copy-start.6
  12.6 0.3 copy.13
  12.9 0.2 pad_maximum_fusion.factors
  13.1 0.1 pad_add_fusion.place
  13.2 0.0 copy-done.5
  13.2 0.5 reshape.27.parents
  13.8 0.0 copy-done.6
  13.8 0.1 reshape.28.ends
  13.9 0.4 all-to-all-done.from_row
  14.3 1.7 %shard_map.93 = (bf16[128,2688]{1,0:T(8,128)(2,1)}, f32[1,128]{1,0:T(1,128)S(1)}) custom-call(s32[2]{0:T(128)S(1)} %pad_add_fusion.place, f32[8,10,128]{2,1,0:T(8,128)S(1)} %all-to-all-done.from_row, bf16[32,1536]{1,0:T(8,128)(2,1)S(1)} %shard_map.92.data), custom_call_target="tpu_custom_call" | custom-call | tf_op jit(solution)/shard_map/pallas_call | solution.py:357
  16.0 8.3 %all-to-all-start.1 = ((bf16[16,8,2688]{2,1,0:T(8,128)(2,1)}), bf16[16,8,2688]{2,1,0:T(8,128)(2,1)S(1)}, u32[]{:S(2)}, u32[]{:S(2)}) async-start(bf16[16,8,2688]{2,1,0:T(8,128)(2,1)} %bitcast.8), calls=%async_computation.1 | async-start | bytes 1376256 | tf_op jit(solution)/shard_map/all_to_all | solution.py:482
  24.4 0.6 shard_map.95.hits
  25.0 0.0 collective-permute-done.joined
  25.0 12.5 %all-to-all-done.1 = bf16[16,8,2688]{2,1,0:T(8,128)(2,1)S(1)} async-done(((bf16[16,8,2688]{2,1,0:T(8,128)(2,1)}), bf16[16,8,2688]{2,1,0:T(8,128)(2,1)S(1)}, u32[]{:S(2)}, u32[]{:S(2)}) %all-to-all-start.1) | async-done | bytes 688160 | tf_op jit(solution)/shard_map/all_to_all | solution.py:482
  37.5 1.8 %shard_map.96 = f32[1024,128]{1,0:T(8,128)} custom-call(bf16[128,2688]{1,0:T(8,128)(2,1)S(1)} %bitcast.21, bf16[1024,512]{1,0:T(8,128)(2,1)S(1)} %shard_map.95.hits, f32[32,32,128]{2,1,0:T(8,128)S(1)} %pad_maximum_fusion.factors), custom_call_target="tpu_custom_call" | custom-call | tf_op jit(solution)/shard_map/pallas_call | solution.py:494
  39.2 3.7 %all-to-all-start.2 = ((f32[8,128,128]{2,1,0:T(8,128)}), f32[8,128,128]{2,1,0:T(8,128)S(1)}, u32[]{:S(2)}, u32[]{:S(2)}) async-start(f32[8,128,128]{2,1,0:T(8,128)} %bitcast.12), calls=%async_computation.2 | async-start | bytes 1048576 | tf_op jit(solution)/shard_map/all_to_all | solution.py:504
  42.9 14.9 %shard_map.97 = (f32[32,768]{1,0:T(8,128)S(1)}, f32[128,896]{1,0:T(8,128)}) custom-call(bf16[32,1536]{1,0:T(8,128)(2,1)S(1)} %shard_map.94.first_ref, bf16[128,2688]{1,0:T(8,128)(2,1)S(1)} %bitcast.22), custom_call_target="tpu_custom_call" | custom-call | flops 2147483648 | bytes 1179648 | tf_op jit(solution)/shard_map/pallas_call | solution.py:161
  57.9 3.3 %collective-permute-start.1 = (f32[32,768]{1,0:T(8,128)S(1)}, f32[32,768]{1,0:T(8,128)S(1)}, u32[]{:S(2)}, u32[]{:S(2)}) collective-permute-start(f32[32,768]{1,0:T(8,128)S(1)} %get-tuple-element.24), channel_id=1, source_target_pairs={{8,0},{9,1},{26,2},{27,3},{40,4},{41,5},{58,6},{59,7},{72,8},{73,9... | collective-permute-start | bytes 294920 | tf_op jit(solution)/shard_map/ppermute | solution.py:507
  61.2 0.0 all-to-all-done.2
  61.3 0.6 constant_dynamic-update-slice_fusion
  61.9 4.4 %all-to-all-start.3 = ((f32[16,8,896]{2,1,0:T(8,128)}), f32[16,8,896]{2,1,0:T(8,128)S(1)}, u32[]{:S(2)}, u32[]{:S(2)}) async-start(f32[16,8,896]{2,1,0:T(8,128)} %bitcast.13), calls=%async_computation.3 | async-start | bytes 917504 | tf_op jit(solution)/shard_map/all_to_all | solution.py:509
  66.3 0.0 copy-start
  66.4 0.0 copy-start.1
  66.4 0.0 collective-permute-done.1.joined
  66.4 10.2 %all-to-all-done.3 = f32[16,8,896]{2,1,0:T(8,128)S(1)} async-done(((f32[16,8,896]{2,1,0:T(8,128)}), f32[16,8,896]{2,1,0:T(8,128)S(1)}, u32[]{:S(2)}, u32[]{:S(2)}) %all-to-all-start.3) | async-done | bytes 458784 | tf_op jit(solution)/shard_map/all_to_all | solution.py:509
  76.5 0.0 copy-done
  76.5 0.0 copy-done.1
  76.6 1.5 %shard_map.99 = f32[3,32,256]{2,1,0:T(8,128)} custom-call(f32[1,128]{1,0:T(1,128)S(1)} %get-tuple-element.18.back, f32[128,896]{1,0:T(8,128)S(1)} %bitcast.25, f32[3,32,256]{2,1,0:T(8,128)S(1)} %shard_map.98.near_first, bf16[1024,768]{1,0:T(8,128)(2,1)S(1)} %bitcast.20, f32[1024,32]{1,0:T(8,128)S(1)} %bitcast.24), custom_call_target="tpu_custom_call" | custom-call | tf_op jit(solution)/shard_map/pallas_call | solution.py:435
  (5 shorter events, 0.1 us)
Async XLA Ops:
  0.0 8.6 %copy-start.2 = (bf16[32,3,256]{2,0,1:T(8,128)(2,1)S(1)}, bf16[32,3,256]{2,0,1:T(8,128)(2,1)}, u32[]{:S(2)}) copy-start(bf16[32,3,256]{2,0,1:T(8,128)(2,1)} %param.9) | copy-start | bytes 147460
  0.0 8.6 %copy-start.3 = (bf16[32,3,256]{2,0,1:T(8,128)(2,1)S(1)}, bf16[32,3,256]{2,0,1:T(8,128)(2,1)}, u32[]{:S(2)}) copy-start(bf16[32,3,256]{2,0,1:T(8,128)(2,1)} %param.10) | copy-start | bytes 147460
  0.0 12.6 %copy-start.4 = (f32[64,32,32]{0,2,1:T(8,128)S(1)}, f32[64,32,32]{0,2,1:T(8,128)}, u32[]{:S(2)}) copy-start(f32[64,32,32]{0,2,1:T(8,128)} %param.17) | copy-start | bytes 786436
  4.2 9.0 %copy-start.5 = (s32[4096]{0:T(1024)S(1)}, s32[4096]{0:T(1024)}, u32[]{:S(2)}) copy-start(s32[4096]{0:T(1024)} %param.13) | copy-start | bytes 49156
  4.2 10.0 %all-to-all-start = ((f32[8,10,128]{2,1,0:T(8,128)}), f32[8,10,128]{2,1,0:T(8,128)S(1)}, u32[]{:S(2)}, u32[]{:S(2)}) async-start(f32[8,10,128]{2,1,0:T(8,128)} %shard_map.91), calls=%async_computation | async-start | bytes 131072 | tf_op jit(solution)/shard_map/all_to_all | solution.py:474
  8.7 16.3 %collective-permute-start = (bf16[32,1536]{1,0:T(8,128)(2,1)S(1)}, bf16[32,1536]{1,0:T(8,128)(2,1)S(1)}, u32[]{:S(2)}, u32[]{:S(2)}) collective-permute-start(bf16[32,1536]{1,0:T(8,128)(2,1)S(1)} %shard_map.92.data), channel_id=1, source_target_pairs={{0,8},{1,9},{2,26},{3,27},{4,40},{5,41},{6,58},{7,59},{8,72},{9,73... | collective-permute-start | bytes 294920 | tf_op jit(solution)/shard_map/ppermute | solution.py:476
  12.6 1.1 %copy-start.6 = (s32[2,64]{1,0:T(2,128)S(1)}, s32[2,64]{1,0:T(2,128)}, u32[]{:S(2)}) copy-start(s32[2,64]{1,0:T(2,128)} %param.16) | copy-start | bytes 1540
  16.0 21.5 %all-to-all-start.1 = ((bf16[16,8,2688]{2,1,0:T(8,128)(2,1)}), bf16[16,8,2688]{2,1,0:T(8,128)(2,1)S(1)}, u32[]{:S(2)}, u32[]{:S(2)}) async-start(bf16[16,8,2688]{2,1,0:T(8,128)(2,1)} %bitcast.8), calls=%async_computation.1 | async-start | bytes 1376256 | tf_op jit(solution)/shard_map/all_to_all | solution.py:482
  39.2 22.0 %all-to-all-start.2 = ((f32[8,128,128]{2,1,0:T(8,128)}), f32[8,128,128]{2,1,0:T(8,128)S(1)}, u32[]{:S(2)}, u32[]{:S(2)}) async-start(f32[8,128,128]{2,1,0:T(8,128)} %bitcast.12), calls=%async_computation.2 | async-start | bytes 1048576 | tf_op jit(solution)/shard_map/all_to_all | solution.py:504
  57.9 8.5 %collective-permute-start.1 = (f32[32,768]{1,0:T(8,128)S(1)}, f32[32,768]{1,0:T(8,128)S(1)}, u32[]{:S(2)}, u32[]{:S(2)}) collective-permute-start(f32[32,768]{1,0:T(8,128)S(1)} %get-tuple-element.24), channel_id=1, source_target_pairs={{8,0},{9,1},{26,2},{27,3},{40,4},{41,5},{58,6},{59,7},{72,8},{73,9... | collective-permute-start | bytes 294920 | tf_op jit(solution)/shard_map/ppermute | solution.py:507
  61.9 14.6 %all-to-all-start.3 = ((f32[16,8,896]{2,1,0:T(8,128)}), f32[16,8,896]{2,1,0:T(8,128)S(1)}, u32[]{:S(2)}, u32[]{:S(2)}) async-start(f32[16,8,896]{2,1,0:T(8,128)} %bitcast.13), calls=%async_computation.3 | async-start | bytes 917504 | tf_op jit(solution)/shard_map/all_to_all | solution.py:509
  66.3 10.2 %copy-start = (bf16[32,32,768]{2,1,0:T(8,128)(2,1)S(1)}, bf16[32,32,768]{2,1,0:T(8,128)(2,1)}, u32[]{:S(2)}) copy-start(bf16[32,32,768]{2,1,0:T(8,128)(2,1)} %param.11) | copy-start | bytes 4718596
  66.4 10.2 %copy-start.1 = (f32[32,32,32]{2,1,0:T(8,128)S(1)}, f32[32,32,32]{2,1,0:T(8,128)}, u32[]{:S(2)}) copy-start(f32[32,32,32]{2,1,0:T(8,128)} %param.12) | copy-start | bytes 393220
